TPU v7x, 32 devices: a whole 2x2x4 slice. The times are simulated.
32 devices in a mesh: tm: 16 (over z, x, core), space: 2 (over y).
Axes of the slice: x: 2, y: 2, z: 4, core: 2. Of those that a mesh axis runs over, the one named last changes fastest.
Arguments:
- start_disp: float32 [16, 3, 4, 64, 256], P('tm', None, None, 'space'), may hold values from -0.2 to 0.2
- start_vel: float32 [16, 3, 4, 64, 256], P('tm', None, None, 'space'), may hold values from -0.2 to 0.2
- start_visc: float32 [16, 3, 4, 64, 256], P('tm', None, None, 'space'), may hold values from -0.2 to 0.2
- init_state: float32 [3, 3, 4, 64, 256], P(None, None, None, 'space'), may hold values from -0.2 to 0.2
- inv_mass: float32 [4, 64, 256], P(None, 'space'), may hold values from 0.35 to 1
- damping_rate: float32 [4, 64, 256], P(None, 'space'), may hold values from 0.002 to 0.2
- visc_rate: float32 [4, 64, 256], P(None, 'space'), may hold values from 0.02 to 2
- fiber_stiff: float32 [4, 64, 256], P(None, 'space'), may hold values from 0.05 to 0.25
- fiber_family: int32 [16, 8], P('space'), may hold values from 0 to 3
- pressure: float32 [16, 4], P('tm'), may hold values from 0.2 to 1
Outputs:
- new_disp: float32 [16, 3, 4, 64, 256], P('tm', None, None, 'space')
- new_vel: float32 [16, 3, 4, 64, 256], P('tm', None, None, 'space')
- new_visc: float32 [16, 3, 4, 64, 256], P('tm', None, None, 'space')
All inputs are finite; a program needn't handle non-finite values.
Results may differ from a plain program's by a relative error of at most 0.000029.
Values sent between devices are 32-bit elements; how exact they have to be, the bound alone decides.
No kernel may reach another device: no remote copies, remote signals or barrier semaphores. Data moves between devices by JAX's collectives and lax.ppermute only.
A program may use at most 128 MiB of HBM per device.

v0:
```python
import math

import jax
import jax.numpy as jnp
from jax import lax
from jax.sharding import PartitionSpec as P

STEPS = 4
BLK_AX = 4
BLK_CIR = 32


COEF_AXIAL = 0.22
COEF_CIRC = 0.22
COEF_RADIAL = 0.12
VISC_SHARE = 0.6
TIME_STEP = 1.0
FIBER_ANGLES = (0.5, -0.5, 0.9, -0.9)


def with_halo(cells, sides, width):
    for axis, dim in sides:
        count = lax.axis_size(axis)
        ends = count - 1
        head = lax.slice_in_dim(cells, 0, width, axis=dim)
        tail = lax.slice_in_dim(cells, cells.shape[dim] - width, cells.shape[dim], axis=dim)
        cells = jnp.concatenate(
            [
                lax.ppermute(tail, axis, [(i, (i + 1) % count) for i in range(ends)]),
                cells,
                lax.ppermute(head, axis, [((i + 1) % count, i) for i in range(ends)]),
            ],
            axis=dim,
        )
    return cells


def from_behind(value, axis, steps):
    count = lax.axis_size(axis)
    leading, last = (max(0, -steps), min(count, count - steps))
    return lax.ppermute(value, axis, [(source, source + steps) for source in range(leading, last)])


def prefix_2(part, axis, combine, identity):
    place = lax.axis_index(axis)
    gathered = jax.tree.map(lambda a: lax.all_gather(a, axis), part)
    state = jax.tree.map(lambda a, e: jnp.zeros_like(a) + jnp.asarray(e, a.dtype), part, identity)

    def one(hop, state):
        return combine(
            state, jax.tree.map(lambda a: lax.dynamic_index_in_dim(a, hop, 0, False), gathered)
        )

    return lax.fori_loop(0, place, one, state)


def directions(fiber_family, block_rows, block_cols):
    count_a, count_c = fiber_family.shape
    spread = jnp.broadcast_to(
        fiber_family[:, None, :, None], (count_a, block_rows, count_c, block_cols)
    )
    spread = spread.reshape(count_a * block_rows, count_c * block_cols)
    cosine = jnp.zeros(spread.shape, jnp.float32)
    sine_part = jnp.zeros(spread.shape, jnp.float32)
    for family, radians in enumerate(FIBER_ANGLES):
        chosen = jnp.where(spread == family, 1.0, 0.0).astype(jnp.float32)
        cosine = cosine + chosen * math.cos(radians)
        sine_part = sine_part + chosen * math.sin(radians)
    return (cosine, sine_part)


def materials(fiber_stiff, fiber_family):
    cosine, sine_part = directions(fiber_family, BLK_AX, BLK_CIR)
    return jnp.stack(
        [
            fiber_stiff,
            jnp.broadcast_to(cosine, fiber_stiff.shape),
            jnp.broadcast_to(sine_part, fiber_stiff.shape),
        ]
    )


def stencil(u_pad, mat_pad):
    center = u_pad[:, :, 1:-1]
    axial = u_pad[:, :, 2:] + u_pad[:, :, :-2] - 2.0 * center
    circle = jnp.roll(center, 1, 3) + jnp.roll(center, -1, 3) - 2.0 * center
    radial_pad = jnp.pad(center, ((0, 0), (1, 1), (0, 0), (0, 0)))
    radial = radial_pad[:, 2:] + radial_pad[:, :-2] - 2.0 * center
    elastic = COEF_AXIAL * axial + COEF_CIRC * circle + COEF_RADIAL * radial
    grad_axial = u_pad[:, :, 1:] - u_pad[:, :, :-1]
    lower = u_pad[:, :, :-1]
    grad_circ = jnp.roll(lower, -1, 3) - lower
    stiffness = mat_pad[0, :, :-1]
    cosine = mat_pad[1, :, :-1]
    sine_part = mat_pad[2, :, :-1]
    strain = (
        cosine * cosine * grad_axial[1]
        + sine_part * sine_part * grad_circ[2]
        + cosine * sine_part * (grad_axial[2] + grad_circ[1])
    )
    weight = jnp.exp(strain * strain)
    sigma = stiffness * weight * strain
    axial_one = sigma * cosine * cosine
    mixed = sigma * cosine * sine_part
    circ_two = sigma * sine_part * sine_part
    own_mixed = mixed[:, 1:]
    own_circ = circ_two[:, 1:]
    force_one = axial_one[:, 1:] - axial_one[:, :-1] + (own_mixed - jnp.roll(own_mixed, 1, 2))
    force_two = mixed[:, 1:] - mixed[:, :-1] + (own_circ - jnp.roll(own_circ, 1, 2))
    fiber = jnp.stack([jnp.zeros_like(force_one), force_one, force_two])
    return (elastic + fiber, elastic, weight[:, 1:])


def fine_step(state, u_pad, mat_pad, inv_mass, damping_rate, decay_factor, pressure_now):
    displace, velocity, viscous = state
    force_total, elastic, weight = stencil(u_pad, mat_pad)
    inner_wall = jnp.zeros((3, displace.shape[1], 1, 1), jnp.float32).at[0, 0].set(1.0)
    load_total = force_total + viscous + pressure_now * inner_wall
    acceleration = inv_mass * load_total - damping_rate * velocity
    next_vel = velocity + TIME_STEP * acceleration
    next_disp = displace + TIME_STEP * next_vel
    next_visc = decay_factor * viscous + (1.0 - decay_factor) * VISC_SHARE * elastic
    return ((next_disp, next_vel, next_visc), weight)


def coarse_matrix(inv_mass, damping_rate, fiber_stiff, weight):
    half_step = 0.5 * STEPS * TIME_STEP
    stiffness = inv_mass * (
        2.0 * (COEF_AXIAL + COEF_CIRC + COEF_RADIAL) + 2.0 * fiber_stiff * weight
    )
    damping_part = half_step * damping_rate
    square_part = half_step * half_step * stiffness
    determinant = 1.0 + damping_part + square_part
    return jnp.stack(
        [
            (1.0 + damping_part - square_part) / determinant,
            2.0 * half_step / determinant,
            -2.0 * half_step * stiffness / determinant,
            (1.0 - damping_part - square_part) / determinant,
        ]
    )


def relax(
    start, mat_pad, inv_mass, damping_rate, decay_factor, fiber_stiff, pressure_row, pad_field
):
    state = start
    first_weight = None
    for section in range(STEPS):
        u_pad = pad_field(state[0])
        state, weight = fine_step(
            state, u_pad, mat_pad, inv_mass, damping_rate, decay_factor, pressure_row[section]
        )
        if section == 0:
            first_weight = weight
    return (state, coarse_matrix(inv_mass, damping_rate, fiber_stiff, first_weight))


def apply_map(gmat, pair):
    return jnp.stack([gmat[0] * pair[0] + gmat[1] * pair[1], gmat[2] * pair[0] + gmat[3] * pair[1]])


def compose(latter, earlier):
    return jnp.stack(
        [
            latter[0] * earlier[0] + latter[1] * earlier[2],
            latter[0] * earlier[1] + latter[1] * earlier[3],
            latter[2] * earlier[0] + latter[3] * earlier[2],
            latter[2] * earlier[1] + latter[3] * earlier[3],
        ]
    )


def combine(earlier, latter):
    return (compose(latter[0], earlier[0]), apply_map(latter[0], earlier[1]) + latter[1])


def face_pad(field):
    return with_halo(field, (("space", 2),), 1)


def shards(
    start_disp,
    start_vel,
    start_visc,
    init_state,
    inv_mass,
    damping_rate,
    visc_rate,
    fiber_stiff,
    fiber_family,
    pressure,
):
    own_mat = materials(fiber_stiff, fiber_family)
    before = from_behind(own_mat[:, :, -1:], "space", 1)
    mat_pad = jnp.concatenate([before, own_mat, jnp.zeros_like(before)], 2)
    decay_factor = jnp.exp(-TIME_STEP * visc_rate)
    starts = jnp.stack([start_disp[0], start_vel[0], start_visc[0]])
    state, gmat = relax(
        (starts[0], starts[1], starts[2]),
        mat_pad,
        inv_mass,
        damping_rate,
        decay_factor,
        fiber_stiff,
        pressure[0],
        face_pad,
    )
    ends = jnp.stack([state[0], state[1], state[2]])
    arrived = from_behind(ends, "tm", 1)
    first_slab = lax.axis_index("tm") == 0
    prior = jnp.where(first_slab, init_state, arrived)
    resid = prior[:2] - starts[:2]
    image = apply_map(gmat, resid)
    ones_field = jnp.ones_like(gmat[0])
    zero_field = jnp.zeros_like(gmat[0])
    identity = (jnp.stack([ones_field, zero_field, zero_field, ones_field]), jnp.zeros_like(image))
    prefix = prefix_2((gmat, image), "tm", combine, identity)
    error = prefix[1]
    new_disp = prior[0] + error[0]
    new_vel = prior[1] + error[1]
    return (new_disp[None], new_vel[None], prior[2][None])


def solution(mesh):
    return jax.shard_map(
        shards,
        mesh=mesh,
        in_specs=(
            P("tm", None, None, "space", None),
            P("tm", None, None, "space", None),
            P("tm", None, None, "space", None),
            P(None, None, None, "space", None),
            P(None, "space", None),
            P(None, "space", None),
            P(None, "space", None),
            P(None, "space", None),
            P("space", None),
            P("tm", None),
        ),
        out_specs=(
            P("tm", None, None, "space", None),
            P("tm", None, None, "space", None),
            P("tm", None, None, "space", None),
        ),
        check_vma=False,
    )
```

profile of v0, /device:TPU:27, one launch (start us, length us, event | category | flops | bytes accessed | tf_op | source)
XLA Modules:
  0.0 255.8 jit_solution(16421804280949117561)
XLA Ops:
  9.2 3.1 %collective-permute-start.2 = (f32[3,4,1,256]{3,2,1,0:T(1,128)S(1)}, f32[3,4,1,256]{3,2,1,0:T(1,128)S(1)}, u32[]{:S(2)}, u32[]{:S(2)}) collective-permute-start(f32[3,4,1,256]{3,2,1,0:T(1,128)S(1)} %pad_maximum_fusion.11), channel_id=1, source_target_pairs={{0,1},{2,3},{4,5},{6,7},{8,9},{10,11},{12,13},{14,15},{16,17},{18,... | collective-permute-start | bytes 36872 | tf_op jit(solution)/shard_map/ppermute | solution.py:41
  12.4 1.3 collective-permute-start
  13.7 4.0 %collective-permute-start.1 = (f32[3,4,1,256]{3,2,1,0:T(1,128)S(1)}, f32[3,4,1,256]{3,2,1,0:T(1,128)S(1)}, u32[]{:S(2)}, u32[]{:S(2)}) collective-permute-start(f32[3,4,1,256]{3,2,1,0:T(1,128)S(1)} %get-tuple-element.172), channel_id=1, source_target_pairs={{0,1},{2,3},{4,5},{6,7},{8,9},{10,11},{12,13},{14,15},{16,17},{18,... | collective-permute-start | bytes 36872 | tf_op jit(solution)/shard_map/ppermute | solution.py:29
  21.6 2.6 %broadcast_multiply_fusion = (f32[3,4]{1,0:T(4,128)S(1)}, f32[3,4]{1,0:T(4,128)S(1)}, f32[3,4]{1,0:T(4,128)S(1)}, f32[3,4]{1,0:T(4,128)S(1)}) fusion(f32[3,4]{1,0:T(4,128)S(1)} %copy-done.8, f32[]{:T(128)} %bitcast.35, f32[]{:T(128)} %bitcast.29, f32[]{:T(128)} %bitcast.23, f32[]{:T(128)} %bitcast.17), kind=kLoop, calls=%fused_computation.278 | loop fusion | flops 48 | bytes 256 | tf_op jit(solution)/shard_map/mul | solution.py:118
  26.2 3.6 %collective-permute-start.4 = (f32[3,4,1,256]{3,2,1,0:T(1,128)S(1)}, f32[3,4,1,256]{3,2,1,0:T(1,128)S(1)}, u32[]{:S(2)}, u32[]{:S(2)}) collective-permute-start(f32[3,4,1,256]{3,2,1,0:T(1,128)S(1)} %get-tuple-element.166), channel_id=1, source_target_pairs={{0,1},{2,3},{4,5},{6,7},{8,9},{10,11},{12,13},{14,15},{16,17},{18,... | collective-permute-start | bytes 36872 | tf_op jit(solution)/shard_map/ppermute | solution.py:29
  30.2 1.3 collective-permute-start.3
  31.7 3.3 %collective-permute-done.3 = f32[3,4,1,256]{3,2,1,0:T(1,128)S(1)} collective-permute-done((f32[3,4,1,256]{3,2,1,0:T(1,128)S(1)}, f32[3,4,1,256]{3,2,1,0:T(1,128)S(1)}, u32[]{:S(2)}, u32[]{:S(2)}) %collective-permute-start.3) | collective-permute-done | bytes 12320 | tf_op jit(solution)/shard_map/ppermute | solution.py:31
  36.3 1.3 collective-permute-start.6
  37.9 1.3 collective-permute-start.5
  39.5 3.3 %collective-permute-done.5 = f32[3,4,1,256]{3,2,1,0:T(1,128)S(1)} collective-permute-done((f32[3,4,1,256]{3,2,1,0:T(1,128)S(1)}, f32[3,4,1,256]{3,2,1,0:T(1,128)S(1)}, u32[]{:S(2)}, u32[]{:S(2)}) %collective-permute-start.5) | collective-permute-done | bytes 12320 | tf_op jit(solution)/shard_map/ppermute | solution.py:31
  44.1 1.3 collective-permute-start.8
  45.7 1.3 collective-permute-start.7
  47.3 3.3 %collective-permute-done.7 = f32[3,4,1,256]{3,2,1,0:T(1,128)S(1)} collective-permute-done((f32[3,4,1,256]{3,2,1,0:T(1,128)S(1)}, f32[3,4,1,256]{3,2,1,0:T(1,128)S(1)}, u32[]{:S(2)}, u32[]{:S(2)}) %collective-permute-start.7) | collective-permute-done | bytes 12320 | tf_op jit(solution)/shard_map/ppermute | solution.py:31
  52.0 1.3 collective-permute-start.9
  53.4 9.5 %collective-permute-done.9 = f32[3,3,4,32,256]{4,3,2,1,0:T(8,128)} collective-permute-done((f32[3,3,4,32,256]{4,3,2,1,0:T(8,128)S(1)}, f32[3,3,4,32,256]{4,3,2,1,0:T(8,128)}, u32[]{:S(2)}, u32[]{:S(2)}) %collective-permute-start.9) | collective-permute-done | bytes 1179680 | tf_op jit(solution)/shard_map/ppermute | solution.py:41
  62.8 1.5 broadcast_select_fusion
  65.6 42.2 %all-gather.5.cloned.1.call-done = f32[64,4,32,256]{3,2,1,0:T(8,128)} async-done(((f32[4,4,32,256]{3,2,1,0:T(8,128)}), f32[64,4,32,256]{3,2,1,0:T(8,128)}) %all-gather.5.cloned.1.call-update) | async-done | bytes 8388624 | tf_op jit(solution)/shard_map/all_gather | solution.py:46
  107.8 101.2 %all-gather.7.cloned.1.call-done = f32[32,3,4,32,256]{4,3,2,1,0:T(8,128)} async-done(((f32[2,3,4,32,256]{4,3,2,1,0:T(8,128)}), f32[32,3,4,32,256]{4,3,2,1,0:T(8,128)}) %all-gather.7.cloned.1.call-update) | async-done | bytes 12582928 | tf_op jit(solution)/shard_map/all_gather | solution.py:46
  209.0 38.8 %while.16 = (s32[]{:T(128)}, f32[2,3,4,32,256]{4,3,2,1,0:T(8,128)S(1)}, s32[]{:T(128)}, f32[16,4,4,32,256]{4,3,2,1,0:T(8,128)}, f32[16,2,3,4,32,256]{5,4,3,2,1,0...) while((s32[]{:T(128)}, f32[2,3,4,32,256]{4,3,2,1,0:T(8,128)S(1)}, ...), condition=%wide.region_1.2_spmd, body=%wide.region_0.1_spmd.sunk | while | flops 983048 | bytes 5505231 | solution.py:54
  236.2 1.3 maximum_add_fusion.10
  238.8 1.3 maximum_add_fusion.10
  241.4 1.3 maximum_add_fusion.10
  244.0 1.3 maximum_add_fusion.10
  246.6 1.3 maximum_add_fusion.10
  (147 shorter events, 47.7 us)
Async XLA Ops:
  7.2 10.5 %copy-start.5 = (f32[4,32,256]{2,1,0:T(8,128)S(1)}, f32[4,32,256]{2,1,0:T(8,128)}, u32[]{:S(2)}) copy-start(f32[4,32,256]{2,1,0:T(8,128)} %param.27) | copy-start | bytes 393220
  7.2 5.1 %copy-start = (f32[1,3,4,32,256]{4,3,2,1,0:T(8,128)S(1)}, f32[1,3,4,32,256]{4,3,2,1,0:T(8,128)}, u32[]{:S(2)}) copy-start(f32[1,3,4,32,256]{4,3,2,1,0:T(8,128)} %param.20) | copy-start | bytes 1179652
  7.2 100.6 %all-gather.5.cloned.1.call-start = ((), (), s32[]{:S(2)}) async-start(), calls=%async_computation | async-start | bytes 8912896 | tf_op jit(solution)/shard_map/all_gather | solution.py:46
  9.2 8.5 %collective-permute-start.2 = (f32[3,4,1,256]{3,2,1,0:T(1,128)S(1)}, f32[3,4,1,256]{3,2,1,0:T(1,128)S(1)}, u32[]{:S(2)}, u32[]{:S(2)}) collective-permute-start(f32[3,4,1,256]{3,2,1,0:T(1,128)S(1)} %pad_maximum_fusion.11), channel_id=1, source_target_pairs={{0,1},{2,3},{4,5},{6,7},{8,9},{10,11},{12,13},{14,15},{16,17},{18,... | collective-permute-start | bytes 36872 | tf_op jit(solution)/shard_map/ppermute | solution.py:41
  12.4 6.4 %collective-permute-start = (f32[3,4,1,256]{3,2,1,0:T(1,128)S(1)}, f32[3,4,1,256]{3,2,1,0:T(1,128)S(1)}, u32[]{:S(2)}, u32[]{:S(2)}) collective-permute-start(f32[3,4,1,256]{3,2,1,0:T(1,128)S(1)} %get-tuple-element.171), channel_id=1, source_target_pairs={{1,0},{3,2},{5,4},{7,6},{9,8},{11,10},{13,12},{15,14},{17,16},{19,... | collective-permute-start | bytes 36872 | tf_op jit(solution)/shard_map/ppermute | solution.py:31
  13.7 4.8 %collective-permute-start.1 = (f32[3,4,1,256]{3,2,1,0:T(1,128)S(1)}, f32[3,4,1,256]{3,2,1,0:T(1,128)S(1)}, u32[]{:S(2)}, u32[]{:S(2)}) collective-permute-start(f32[3,4,1,256]{3,2,1,0:T(1,128)S(1)} %get-tuple-element.172), channel_id=1, source_target_pairs={{0,1},{2,3},{4,5},{6,7},{8,9},{10,11},{12,13},{14,15},{16,17},{18,... | collective-permute-start | bytes 36872 | tf_op jit(solution)/shard_map/ppermute | solution.py:29
  18.9 0.9 copy-start.1
  18.9 1.0 copy-start.2
  19.9 1.1 copy-start.7
  19.9 1.6 copy-start.8
  20.0 4.2 %copy-start.6 = (f32[4,32,256]{2,1,0:T(8,128)S(1)}, f32[4,32,256]{2,1,0:T(8,128)}, u32[]{:S(2)}) copy-start(f32[4,32,256]{2,1,0:T(8,128)} %param.26) | copy-start | bytes 393220
  20.9 188.0 %all-gather.7.cloned.1.call-start = ((), (), s32[]{:S(2)}) async-start(), calls=%async_computation.1 | async-start | bytes 13369344 | tf_op jit(solution)/shard_map/all_gather | solution.py:46
  24.6 1.0 copy-start.3
  24.6 1.1 copy-start.4
  26.2 5.2 %collective-permute-start.4 = (f32[3,4,1,256]{3,2,1,0:T(1,128)S(1)}, f32[3,4,1,256]{3,2,1,0:T(1,128)S(1)}, u32[]{:S(2)}, u32[]{:S(2)}) collective-permute-start(f32[3,4,1,256]{3,2,1,0:T(1,128)S(1)} %get-tuple-element.166), channel_id=1, source_target_pairs={{0,1},{2,3},{4,5},{6,7},{8,9},{10,11},{12,13},{14,15},{16,17},{18,... | collective-permute-start | bytes 36872 | tf_op jit(solution)/shard_map/ppermute | solution.py:29
  30.2 4.8 %collective-permute-start.3 = (f32[3,4,1,256]{3,2,1,0:T(1,128)S(1)}, f32[3,4,1,256]{3,2,1,0:T(1,128)S(1)}, u32[]{:S(2)}, u32[]{:S(2)}) collective-permute-start(f32[3,4,1,256]{3,2,1,0:T(1,128)S(1)} %get-tuple-element.165), channel_id=1, source_target_pairs={{1,0},{3,2},{5,4},{7,6},{9,8},{11,10},{13,12},{15,14},{17,16},{19,... | collective-permute-start | bytes 36872 | tf_op jit(solution)/shard_map/ppermute | solution.py:31
  36.3 2.9 %collective-permute-start.6 = (f32[3,4,1,256]{3,2,1,0:T(1,128)S(1)}, f32[3,4,1,256]{3,2,1,0:T(1,128)S(1)}, u32[]{:S(2)}, u32[]{:S(2)}) collective-permute-start(f32[3,4,1,256]{3,2,1,0:T(1,128)S(1)} %get-tuple-element.160), channel_id=1, source_target_pairs={{0,1},{2,3},{4,5},{6,7},{8,9},{10,11},{12,13},{14,15},{16,17},{18,... | collective-permute-start | bytes 36872 | tf_op jit(solution)/shard_map/ppermute | solution.py:29
  37.9 4.8 %collective-permute-start.5 = (f32[3,4,1,256]{3,2,1,0:T(1,128)S(1)}, f32[3,4,1,256]{3,2,1,0:T(1,128)S(1)}, u32[]{:S(2)}, u32[]{:S(2)}) collective-permute-start(f32[3,4,1,256]{3,2,1,0:T(1,128)S(1)} %get-tuple-element.159), channel_id=1, source_target_pairs={{1,0},{3,2},{5,4},{7,6},{9,8},{11,10},{13,12},{15,14},{17,16},{19,... | collective-permute-start | bytes 36872 | tf_op jit(solution)/shard_map/ppermute | solution.py:31
  44.1 2.9 %collective-permute-start.8 = (f32[3,4,1,256]{3,2,1,0:T(1,128)S(1)}, f32[3,4,1,256]{3,2,1,0:T(1,128)S(1)}, u32[]{:S(2)}, u32[]{:S(2)}) collective-permute-start(f32[3,4,1,256]{3,2,1,0:T(1,128)S(1)} %get-tuple-element.154), channel_id=1, source_target_pairs={{0,1},{2,3},{4,5},{6,7},{8,9},{10,11},{12,13},{14,15},{16,17},{18,... | collective-permute-start | bytes 36872 | tf_op jit(solution)/shard_map/ppermute | solution.py:29
  45.7 4.8 %collective-permute-start.7 = (f32[3,4,1,256]{3,2,1,0:T(1,128)S(1)}, f32[3,4,1,256]{3,2,1,0:T(1,128)S(1)}, u32[]{:S(2)}, u32[]{:S(2)}) collective-permute-start(f32[3,4,1,256]{3,2,1,0:T(1,128)S(1)} %get-tuple-element.153), channel_id=1, source_target_pairs={{1,0},{3,2},{5,4},{7,6},{9,8},{11,10},{13,12},{15,14},{17,16},{19,... | collective-permute-start | bytes 36872 | tf_op jit(solution)/shard_map/ppermute | solution.py:31
  52.0 10.8 %collective-permute-start.9 = (f32[3,3,4,32,256]{4,3,2,1,0:T(8,128)S(1)}, f32[3,3,4,32,256]{4,3,2,1,0:T(8,128)}, u32[]{:S(2)}, u32[]{:S(2)}) collective-permute-start(f32[3,3,4,32,256]{4,3,2,1,0:T(8,128)S(1)} %pad_maximum_fusion), channel_id=1, source_target_pairs={{0,2},{2,4},{4,6},{6,8},{8,10},{10,12},{12,14},{14,16},{16,18},{18... | collective-permute-start | bytes 3538952 | tf_op jit(solution)/shard_map/ppermute | solution.py:41
Sparse Core Ops, SparseCore 0:
  21.0 86.6 all-gather.4
  110.1 98.8 all-gather.6
where the time goes:
time: 257 us; the launch traced here: 256 us
  waiting for transfers between devices  163 us (63%)
  other arithmetic  35.3 us (14%)
  local copies, waits for them, and re-layouts  21.9 us (9%)
  starting transfers between devices  19.9 us (8%)
  between operations  14.7 us (6%)
    all_gather x2, waiting for transfers between devices, prefix_2(): gathered = jax.tree.map(lambda a: lax.all_gather(a, axis), part)  143 us
    add x15, other arithmetic, combine(): apply_map(latter[0], earlier[1]) + latter[1]  19 us
    mul x15, local copies, waits for them, and re-layouts, apply_map(): gmat[0] * pair[0] + gmat[1] * pair[1]  17.2 us
    ppermute x4, starting transfers between devices, with_halo(): lax.ppermute(tail, axis, [(i, (i + 1) % count) for i in range(ends)])  10.2 us
    ppermute x4, waiting for transfers between devices, with_halo(): lax.ppermute(head, axis, [((i + 1) % count, i) for i in range(ends)])  9.8 us
    ppermute x2, waiting for transfers between devices, from_behind(): lax.ppermute(value, axis, [(source, source + steps) for source in range(l...  9.49 us
    ppermute x4, starting transfers between devices, with_halo(): lax.ppermute(head, axis, [((i + 1) % count, i) for i in range(ends)])  5.17 us
  transfers between devices with their start and end apart: 12, of which 7 were waited for; matrix products, arithmetic and copies ran while one was open for 5% of the time, Pallas kernels for 0%

commit v1 on v0

v1 whole, which is shorter than its diff:
```python
import functools
import math

import jax
import jax.numpy as jnp
from jax import lax
from jax.experimental import pallas as pl
from jax.experimental.pallas import tpu as pltpu
from jax.sharding import PartitionSpec as P

STEPS = 4
BLK_AX = 4
BLK_CIR = 32
COEF_AXIAL = 0.22
COEF_CIRC = 0.22
COEF_RADIAL = 0.12
VISC_SHARE = 0.6
TIME_STEP = 1.0
FIBER_ANGLES = (0.5, -0.5, 0.9, -0.9)
CORES = 2
HALO = STEPS
F32 = jnp.float32
VMEM_LIMIT = 24 * 1024 * 1024


def call(kernel, out_shape, operands, scratch=(), any_space=(), smem=()):
    specs = []
    for k in range(len(operands)):
        if k in any_space:
            specs.append(pl.BlockSpec(memory_space=pl.ANY))
        elif k in smem:
            specs.append(pl.BlockSpec(memory_space=pltpu.SMEM))
        else:
            specs.append(pl.BlockSpec(memory_space=pltpu.VMEM))
    return pl.pallas_call(
        kernel,
        out_shape=out_shape,
        in_specs=specs,
        out_specs=jax.tree.map(lambda _: pl.BlockSpec(memory_space=pltpu.VMEM), out_shape),
        scratch_shapes=list(scratch),
        compiler_params=pltpu.CompilerParams(vmem_limit_bytes=VMEM_LIMIT),
    )(*operands)


def shape(*dims):
    return jax.ShapeDtypeStruct(dims, F32)


def iota(dims, axis):
    return lax.broadcasted_iota(jnp.int32, dims, axis)


def direction_tile(family_ref, first, second, cols):
    row = iota((8, cols), 0)
    block = iota((8, cols), 1) // BLK_CIR
    family = jnp.zeros((8, cols), jnp.int32)
    for k in range(cols // BLK_CIR):
        index = jnp.where(row < BLK_AX, family_ref[first, k], family_ref[second, k])
        family = jnp.where(block == k, index, family)
    cosine = jnp.zeros((8, cols), F32)
    sine = jnp.zeros((8, cols), F32)
    for index, angle in enumerate(FIBER_ANGLES):
        cosine = jnp.where(family == index, math.cos(angle), cosine)
        sine = jnp.where(family == index, math.sin(angle), sine)
    return cosine, sine


def pack_kernel(sides, *refs):
    fields, family_ref = refs[:7], refs[7]
    outs = refs[8 : 8 + len(sides)]
    states = refs[8 + len(sides)]
    statics = refs[9 + len(sides)]
    sem = refs[10 + len(sides)]
    rows, cols = fields[0].shape[-2:]
    block_rows = family_ref.shape[0]
    place = lax.axis_index("space")
    for out_ref, side in zip(outs, sides):
        tail = (place == 0) if side == "inner" else (side == "tail")
        start = jnp.where(tail, rows - 8, 0) if side == "inner" else (rows - 8 if tail else 0)
        if side == "inner":
            start = pl.multiple_of(start, 8)
        copies = []
        for k in range(3):
            copies.append(
                pltpu.make_async_copy(
                    fields[k].at[0, :, :, pl.ds(start, 8), :], states.at[k], sem.at[k]
                )
            )
        for k in range(4):
            copies.append(
                pltpu.make_async_copy(
                    fields[3 + k].at[:, pl.ds(start, 8), :], statics.at[k], sem.at[3 + k]
                )
            )
        for copy in copies:
            copy.start()
        end_block = jnp.where(tail, block_rows - 1, 0) if side == "inner" else (block_rows - 1 if tail else 0)
        cosine, sine = direction_tile(family_ref, end_block, end_block, cols)
        low = iota((8, cols), 0) < HALO
        for copy in copies:
            copy.wait()

        def pair(first, second):
            up = pltpu.roll(first, 4, 0)
            down = pltpu.roll(second, 4, 0)
            return jnp.where(tail, jnp.where(low, up, second), jnp.where(low, first, down))

        at = 0
        for k in range(3):
            for comp in range(3):
                for layer in range(0, 4, 2):
                    out_ref[at] = pair(states[k, comp, layer], states[k, comp, layer + 1])
                    at += 1
        for k in range(4):
            for layer in range(0, 4, 2):
                out_ref[at] = pair(statics[k, layer], statics[k, layer + 1])
                at += 1
        out_ref[at] = jnp.where(low, cosine, sine)


def coarse(inv_mass, damping, stiff, weight):
    half_step = 0.5 * STEPS * TIME_STEP
    k = inv_mass * (2.0 * (COEF_AXIAL + COEF_CIRC + COEF_RADIAL) + 2.0 * stiff * weight)
    damp = half_step * damping
    square = half_step * half_step * k
    scale = 1.0 / (1.0 + damp + square)
    return (
        (1.0 + damp - square) * scale,
        (2.0 * half_step) * scale,
        (-2.0 * half_step) * k * scale,
        (1.0 - damp - square) * scale,
    )


def relax_kernel(
    disp_ref, vel_ref, visc_ref, mass_ref, damp_ref, rate_ref, stiff_ref, family_ref, pressure_ref,
    next_ref, prev_ref, keep_ref, send_ref, end_visc_ref,
    u_s, v_s, q_s, mass_s, damp_s, decay_s, share_s, stiff_s, cc_s, cs_s, ss_s, w_s,
):
    rows, cols = disp_ref.shape[-2:]
    total = rows + 8
    layers = disp_ref.shape[2]
    place = lax.axis_index("space")
    has_next = place < lax.axis_size("space") - 1
    has_prev = place > 0
    low = iota((8, cols), 0) < HALO
    live = jnp.where(low, has_next.astype(jnp.int32), has_prev.astype(jnp.int32)) > 0

    def halo(at):
        after, before = next_ref[at], prev_ref[at]
        first = jnp.where(live, jnp.where(low, after, pltpu.roll(before, 4, 0)), 0.0)
        second = jnp.where(live, jnp.where(low, pltpu.roll(after, 4, 0), before), 0.0)
        return first, second

    at = 0
    for source, target in ((disp_ref, u_s.at[0]), (vel_ref, v_s), (visc_ref, q_s)):
        for comp in range(3):
            for layer in range(0, layers, 2):
                pair = halo(at)
                at += 1
                for j in range(2):
                    target[comp * layers + layer + j, 0:rows, :] = source[0, comp, layer + j]
                    target[comp * layers + layer + j, rows:total, :] = pair[j]
    for source, target in ((mass_ref, mass_s), (damp_ref, damp_s), (rate_ref, decay_s), (stiff_ref, stiff_s)):
        for layer in range(0, layers, 2):
            pair = halo(at)
            at += 1
            for j in range(2):
                target[layer + j, 0:rows, :] = source[layer + j]
                target[layer + j, rows:total, :] = pair[j]
    for layer in range(layers):
        decay = jnp.exp(-TIME_STEP * decay_s[layer])
        decay_s[layer] = decay
        share_s[layer] = (1.0 - decay) * VISC_SHARE
    for tile in range(rows // 8):
        cosine, sine = direction_tile(family_ref, 2 * tile, 2 * tile + 1, cols)
        cc_s[8 * tile : 8 * tile + 8, :] = cosine * cosine
        cs_s[8 * tile : 8 * tile + 8, :] = cosine * sine
        ss_s[8 * tile : 8 * tile + 8, :] = sine * sine
    cosine, sine = halo(at)
    cc_s[rows:total, :] = cosine * cosine
    cs_s[rows:total, :] = cosine * sine
    ss_s[rows:total, :] = sine * sine

    def succ(a):
        return pltpu.roll(a, total - 1, 0)

    def pred(a):
        return pltpu.roll(a, 1, 0)

    def right(a):
        return pltpu.roll(a, cols - 1, 1)

    def left(a):
        return pltpu.roll(a, 1, 1)

    def step(s, carry):
        now = lax.rem(s, 2)
        later = 1 - now
        load = pressure_ref[0, s]
        for layer in range(layers):
            mass, damp = mass_s[layer], damp_s[layer]
            decay, share = decay_s[layer], share_s[layer]
            cc, cs, ss = cc_s[...], cs_s[...], ss_s[...]
            u = [u_s[now, comp * layers + layer] for comp in range(3)]
            ahead = [succ(a) for a in u]
            beside = [right(a) for a in u]
            strain = (
                cc * (ahead[1] - u[1])
                + ss * (beside[2] - u[2])
                + cs * ((ahead[2] - u[2]) + (beside[1] - u[1]))
            )
            weight = jnp.exp(strain * strain)
            w_s[s, layer] = weight
            sigma = stiff_s[layer] * weight * strain
            axial_one, mixed, circ_two = cc * sigma, cs * sigma, ss * sigma
            fiber = [
                None,
                (axial_one - pred(axial_one)) + (mixed - left(mixed)),
                (mixed - pred(mixed)) + (circ_two - left(circ_two)),
            ]
            for comp in range(3):
                k = comp * layers + layer
                elastic = COEF_AXIAL * ((ahead[comp] + pred(u[comp])) + (beside[comp] + left(u[comp])))
                if layer == 0:
                    radial = u_s[now, k + 1]
                elif layer == layers - 1:
                    radial = u_s[now, k - 1]
                else:
                    radial = u_s[now, k - 1] + u_s[now, k + 1]
                elastic = (elastic + COEF_RADIAL * radial) - (
                    2.0 * (COEF_AXIAL + COEF_CIRC + COEF_RADIAL)
                ) * u[comp]
                visc = q_s[k]
                force = elastic + visc
                if fiber[comp] is not None:
                    force = force + fiber[comp]
                elif layer == 0:
                    force = force + load
                vel = v_s[k]
                vel = vel + (mass * force - damp * vel)
                v_s[k] = vel
                u_s[later, k] = u[comp] + vel
                q_s[k] = decay * visc + share * elastic
        return carry

    lax.fori_loop(0, STEPS, step, 0)

    core = lax.rem(lax.axis_index("tm"), CORES)
    half = layers // CORES
    for layer in range(layers):
        weight = w_s[0, layer, 0:rows, :]
        g = coarse(mass_s[layer, 0:rows, :], damp_s[layer, 0:rows, :], stiff_s[layer, 0:rows, :], weight)
        mine = core == layer // half
        pieces = [weight]
        for comp in range(3):
            k = comp * layers + layer
            pieces.append(
                u_s[STEPS % 2, k, 0:rows, :] - (g[0] * disp_ref[0, comp, layer] + g[1] * vel_ref[0, comp, layer])
            )
        for comp in range(3):
            k = comp * layers + layer
            pieces.append(
                v_s[k, 0:rows, :] - (g[2] * disp_ref[0, comp, layer] + g[3] * vel_ref[0, comp, layer])
            )

        @pl.when(mine)
        def _():
            for k, piece in enumerate(pieces):
                keep_ref[k, layer % half] = piece

        @pl.when(jnp.logical_not(mine))
        def _():
            for k, piece in enumerate(pieces):
                send_ref[k, layer % half] = piece

        for comp in range(3):
            end_visc_ref[comp, layer] = q_s[comp * layers + layer, 0:rows, :]


def layout(group, half, rows):
    part_rows = half * rows // group
    return part_rows, rows // part_rows


def compose_kernel(group, keep_ref, got_ref, mass_ref, damp_ref, stiff_ref, *outs):
    half, rows, cols = keep_ref.shape[1:]
    part_rows, per_layer = layout(group, half, rows)
    index = lax.axis_index("tm")
    core = lax.rem(index, CORES)
    place = lax.rem(index // CORES, group)
    first_core = core == 0
    for m in range(group):
        part = jnp.bitwise_xor(place, m)
        layer = part // per_layer
        start = pl.multiple_of(lax.rem(part, per_layer) * part_rows, 8)
        own_layer = core * half + layer
        cut = pl.ds(start, part_rows)
        keep = [keep_ref[k, layer, cut, :] for k in range(7)]
        got = [got_ref[k, layer, cut, :] for k in range(7)]
        early = [jnp.where(first_core, a, b) for a, b in zip(keep, got)]
        late = [jnp.where(first_core, b, a) for a, b in zip(keep, got)]
        g = coarse(mass_ref[own_layer, cut, :], damp_ref[own_layer, cut, :], stiff_ref[own_layer, cut, :], late[0])
        outs[m][0] = early[0]
        outs[m][1] = late[0]
        for comp in range(3):
            a, b = early[1 + comp], early[4 + comp]
            outs[m][2 + comp] = (g[0] * a + g[1] * b) + late[1 + comp]
            outs[m][5 + comp] = (g[2] * a + g[3] * b) + late[4 + comp]


def chain(group, maps, mass, damp, stiff, state, visit):
    place = lax.rem(lax.axis_index("tm") // CORES, group)
    for s in range(group):
        visit(s, state)
        one = maps[s]
        first = coarse(mass, damp, stiff, one[0])
        second = coarse(mass, damp, stiff, one[1])
        new = [None] * 6
        for comp in range(3):
            a, b = state[comp], state[3 + comp]
            a, b = first[0] * a + first[1] * b, first[2] * a + first[3] * b
            new[comp] = (second[0] * a + second[1] * b) + one[2 + comp]
            new[3 + comp] = (second[2] * a + second[3] * b) + one[5 + comp]
        state = new
    return state


def own_cut(group, half, rows):
    part_rows, per_layer = layout(group, half, rows)
    index = lax.axis_index("tm")
    core = lax.rem(index, CORES)
    place = lax.rem(index // CORES, group)
    layer = core * half + place // per_layer
    start = pl.multiple_of(lax.rem(place, per_layer) * part_rows, 8)
    return place, layer, pl.ds(start, part_rows)


def lower_kernel(group, half, *refs):
    parts = refs[:group]
    mass_ref, damp_ref, stiff_ref, init_ref, out_ref, maps = refs[group:]
    rows = mass_ref.shape[-2]
    place, layer, cut = own_cut(group, half, rows)
    for m in range(group):
        maps[jnp.bitwise_xor(place, m)] = parts[m][...]
    state = [init_ref[k // 3, k % 3, layer, cut, :] for k in range(6)]
    state = chain(
        group, maps, mass_ref[layer, cut, :], damp_ref[layer, cut, :], stiff_ref[layer, cut, :], state,
        lambda s, state: None,
    )
    for k in range(6):
        out_ref[k] = state[k]


def upper_kernel(group, half, *refs):
    parts = refs[:group]
    mass_ref, damp_ref, stiff_ref, init_ref, hop_ref = refs[group : group + 5]
    outs = refs[group + 5 : 2 * group + 5]
    maps, found = refs[2 * group + 5 :]
    rows = mass_ref.shape[-2]
    place, layer, cut = own_cut(group, half, rows)
    lower = lax.axis_index("tm") < CORES * group
    for m in range(group):
        maps[jnp.bitwise_xor(place, m)] = parts[m][...]
    state = [jnp.where(lower, init_ref[k // 3, k % 3, layer, cut, :], hop_ref[k]) for k in range(6)]

    def visit(s, state):
        for k in range(6):
            found[s, k] = state[k]

    chain(
        group, maps, mass_ref[layer, cut, :], damp_ref[layer, cut, :], stiff_ref[layer, cut, :], state, visit
    )
    for m in range(group):
        outs[m][...] = found[jnp.bitwise_xor(place, m)]


def spread_kernel(group, *refs):
    parts = refs[:group]
    keep_ref, got_ref, mass_ref, damp_ref, stiff_ref, mine_ref, send_ref = refs[group:]
    half, rows, cols = keep_ref.shape[1:]
    part_rows, per_layer = layout(group, half, rows)
    index = lax.axis_index("tm")
    core = lax.rem(index, CORES)
    place = lax.rem(index // CORES, group)
    first_core = core == 0
    for m in range(group):
        part = jnp.bitwise_xor(place, m)
        layer = part // per_layer
        start = pl.multiple_of(lax.rem(part, per_layer) * part_rows, 8)
        own_layer = core * half + layer
        cut = pl.ds(start, part_rows)
        early = [jnp.where(first_core, keep_ref[k, layer, cut, :], got_ref[k, layer, cut, :]) for k in range(7)]
        g = coarse(mass_ref[own_layer, cut, :], damp_ref[own_layer, cut, :], stiff_ref[own_layer, cut, :], early[0])
        for comp in range(3):
            a, b = parts[m][comp], parts[m][3 + comp]
            next_a = (g[0] * a + g[1] * b) + early[1 + comp]
            next_b = (g[2] * a + g[3] * b) + early[4 + comp]
            mine_ref[comp, layer, cut, :] = jnp.where(first_core, a, next_a)
            mine_ref[3 + comp, layer, cut, :] = jnp.where(first_core, b, next_b)
            send_ref[comp, layer, cut, :] = jnp.where(first_core, next_a, a)
            send_ref[3 + comp, layer, cut, :] = jnp.where(first_core, next_b, b)


def join_kernel(mine_ref, got_ref, disp_ref, vel_ref):
    half = mine_ref.shape[1]
    core = lax.rem(lax.axis_index("tm"), CORES)
    for comp in range(3):
        for layer in range(half):
            disp_ref[0, comp, core * half + layer] = mine_ref[comp, layer]
            disp_ref[0, comp, (1 - core) * half + layer] = got_ref[comp, layer]
            vel_ref[0, comp, core * half + layer] = mine_ref[3 + comp, layer]
            vel_ref[0, comp, (1 - core) * half + layer] = got_ref[3 + comp, layer]


def swap_cores(value):
    count = lax.axis_size("tm")
    return lax.ppermute(value, "tm", [(i, i ^ 1) for i in range(count)])


def transpose_parts(parts):
    count = lax.axis_size("tm")
    done = [parts[0]]
    for m in range(1, len(parts)):
        done.append(lax.ppermute(parts[m], "tm", [(i, i ^ (CORES * m)) for i in range(count)]))
    return done


def shards(
    start_disp, start_vel, start_visc, init_state, inv_mass, damping_rate, visc_rate, fiber_stiff,
    fiber_family, pressure,
):
    slabs, spaces = lax.axis_size("tm"), lax.axis_size("space")
    group = slabs // CORES // 2
    layers, rows, cols = inv_mass.shape
    half = layers // CORES
    total = rows + 8
    part_rows, _ = layout(group, half, rows)

    tiles = (9 * layers + 4 * layers + 2) // 2
    packed = shape(tiles, 8, cols)
    sides = ("inner",) if spaces == 2 else ("tail", "head")
    packs = call(
        functools.partial(pack_kernel, sides),
        [packed] * len(sides),
        (start_disp, start_vel, start_visc, inv_mass, damping_rate, visc_rate, fiber_stiff, fiber_family),
        [
            pltpu.VMEM((3, 3, layers, 8, cols), F32),
            pltpu.VMEM((4, layers, 8, cols), F32),
            pltpu.SemaphoreType.DMA((7,)),
        ],
        any_space=range(7),
        smem=(7,),
    )
    if spaces == 2:
        after = before = lax.ppermute(packs[0], "space", [(0, 1), (1, 0)])
    else:
        before = lax.ppermute(packs[0], "space", [(i, i + 1) for i in range(spaces - 1)])
        after = lax.ppermute(packs[1], "space", [(i + 1, i) for i in range(spaces - 1)])

    keep, send, end_visc = call(
        relax_kernel,
        [shape(7, half, rows, cols), shape(7, half, rows, cols), shape(3, layers, rows, cols)],
        (
            start_disp, start_vel, start_visc, inv_mass, damping_rate, visc_rate, fiber_stiff, fiber_family,
            pressure, after, before,
        ),
        [
            pltpu.VMEM((2, 3 * layers, total, cols), F32),
            pltpu.VMEM((3 * layers, total, cols), F32),
            pltpu.VMEM((3 * layers, total, cols), F32),
        ]
        + [pltpu.VMEM((layers, total, cols), F32)] * 5
        + [pltpu.VMEM((total, cols), F32)] * 3
        + [pltpu.VMEM((STEPS, layers, total, cols), F32)],
        smem=(7, 8),
    )
    got = swap_cores(send)
    visc = lax.ppermute(end_visc, "tm", [(i, i + 1) for i in range(slabs - 1)])

    parts = call(
        functools.partial(compose_kernel, group),
        [shape(8, part_rows, cols)] * group,
        (keep, got, inv_mass, damping_rate, fiber_stiff),
    )
    parts = transpose_parts(parts)
    maps = pltpu.VMEM((group, 8, part_rows, cols), F32)
    edge = call(
        functools.partial(lower_kernel, group, half),
        shape(6, part_rows, cols),
        (*parts, inv_mass, damping_rate, fiber_stiff, init_state),
        [maps],
    )
    hop = lax.ppermute(edge, "tm", [(i, i + slabs // 2) for i in range(slabs // 2)])
    states = call(
        functools.partial(upper_kernel, group, half),
        [shape(6, part_rows, cols)] * group,
        (*parts, inv_mass, damping_rate, fiber_stiff, init_state, hop),
        [maps, pltpu.VMEM((group, 6, part_rows, cols), F32)],
    )
    states = transpose_parts(states)
    mine, other = call(
        functools.partial(spread_kernel, group),
        [shape(6, half, rows, cols)] * 2,
        (*states, keep, got, inv_mass, damping_rate, fiber_stiff),
    )
    other = swap_cores(other)
    field = shape(1, 3, layers, rows, cols)
    new_disp, new_vel = call(join_kernel, [field, field], (mine, other))
    first_slab = lax.axis_index("tm") == 0
    new_visc = jnp.where(first_slab, init_state[2], visc)[None]
    return new_disp, new_vel, new_visc


def solution(mesh):
    slab = P("tm", None, None, "space", None)
    cell = P(None, "space", None)
    return jax.shard_map(
        shards,
        mesh=mesh,
        in_specs=(
            slab, slab, slab, P(None, None, None, "space", None), cell, cell, cell, cell,
            P("space", None), P("tm", None),
        ),
        out_specs=(slab, slab, slab),
        check_vma=False,
    )
```

time: 257 us -> 53.9 us (0.21)
  the two profiles are of different devices: /device:TPU:27 before, /device:TPU:0 now
where the time goes in v1:
time: 53.9 us; the launch traced here: 53.5 us
  waiting for transfers between devices  20.5 us (38%)
  starting transfers between devices  16.9 us (31%)
  local copies, waits for them, and re-layouts  7.31 us (14%)
  Pallas kernels  7.25 us (13%)
  other arithmetic  0.8 us (1%)
  between operations  0.78 us (1%)
    ppermute x6, waiting for transfers between devices, transpose_parts(): lax.ppermute(parts[m], 'tm', [(i, i ^ CORES * m) for i in range(count)])  10.2 us
    ppermute x6, starting transfers between devices, transpose_parts(): lax.ppermute(parts[m], 'tm', [(i, i ^ CORES * m) for i in range(count)])  7.52 us
    unnamed x26, local copies, waits for them, and re-layouts  7.31 us
    pallas_call x7, Pallas kernels, call(): pl.pallas_call(kernel, out_shape=out_shape, in_specs=specs, out_specs=jax...  7.25 us
    ppermute x1, waiting for transfers between devices, shards(): after = before = lax.ppermute(packs[0], 'space', [(0, 1), (1, 0)])  5.43 us
    ppermute x1, starting transfers between devices, shards(): lax.ppermute(edge, 'tm', [(i, i + slabs // 2) for i in range(slabs // 2)])  4.91 us
    ppermute x1, starting transfers between devices, shards(): after = before = lax.ppermute(packs[0], 'space', [(0, 1), (1, 0)])  3.03 us
    ppermute x2, waiting for transfers between devices, swap_cores(): return lax.ppermute(value, 'tm', [(i, i ^ 1) for i in range(count)])  2.69 us
  transfers between devices with their start and end apart: 11, of which 10 were waited for; matrix products, arithmetic and copies ran while one was open for 2% of the time, Pallas kernels for 1%

profile of v1, /device:TPU:0, one launch (start us, length us, event | category | flops | bytes accessed | tf_op | source)
XLA Modules:
  0.0 53.5 jit_solution(1376026373946419066)
XLA Ops:
  0.6 0.9 %copy-done.1 = f32[4,32,256]{2,1,0:T(8,128)S(1)} copy-done((f32[4,32,256]{2,1,0:T(8,128)S(1)}, f32[4,32,256]{2,1,0:T(8,128)}, u32[]{:S(2)}) %copy-start.1) | copy-done | bytes 131096
  1.5 0.9 %copy-done.3 = f32[4,32,256]{2,1,0:T(8,128)S(1)} copy-done((f32[4,32,256]{2,1,0:T(8,128)S(1)}, f32[4,32,256]{2,1,0:T(8,128)}, u32[]{:S(2)}) %copy-start.3) | copy-done | bytes 131096
  2.4 0.9 %copy-done.5 = f32[4,32,256]{2,1,0:T(8,128)S(1)} copy-done((f32[4,32,256]{2,1,0:T(8,128)S(1)}, f32[4,32,256]{2,1,0:T(8,128)}, u32[]{:S(2)}) %copy-start.5) | copy-done | bytes 131096
  3.4 1.0 %copy-done.7 = f32[1,3,4,32,256]{4,3,2,1,0:T(8,128)S(1)} copy-done((f32[1,3,4,32,256]{4,3,2,1,0:T(8,128)S(1)}, f32[1,3,4,32,256]{4,3,2,1,0:T(8,128)}, u32[]{:S(2)}) %copy-start.7) | copy-done | bytes 393240
  4.3 1.0 %copy-done.8 = f32[1,3,4,32,256]{4,3,2,1,0:T(8,128)S(1)} copy-done((f32[1,3,4,32,256]{4,3,2,1,0:T(8,128)S(1)}, f32[1,3,4,32,256]{4,3,2,1,0:T(8,128)}, u32[]{:S(2)}) %copy-start.8) | copy-done | bytes 393240
  5.3 1.0 %copy-done.9 = f32[1,3,4,32,256]{4,3,2,1,0:T(8,128)S(1)} copy-done((f32[1,3,4,32,256]{4,3,2,1,0:T(8,128)S(1)}, f32[1,3,4,32,256]{4,3,2,1,0:T(8,128)}, u32[]{:S(2)}) %copy-start.9) | copy-done | bytes 393240
  6.3 0.9 %copy-done.10 = f32[4,32,256]{2,1,0:T(8,128)S(1)} copy-done((f32[4,32,256]{2,1,0:T(8,128)S(1)}, f32[4,32,256]{2,1,0:T(8,128)}, u32[]{:S(2)}) %copy-start.10) | copy-done | bytes 131096
  8.8 3.0 %collective-permute-start = (f32[27,8,256]{2,1,0:T(8,128)S(1)}, f32[27,8,256]{2,1,0:T(8,128)S(1)}, u32[]{:S(2)}, u32[]{:S(2)}) collective-permute-start(f32[27,8,256]{2,1,0:T(8,128)S(1)} %shard_map.121), channel_id=1, source_target_pairs={{0,1},{1,0},{2,3},{3,2},{4,5},{5,4},{6,7},{7,6},{8,9},{9,8},{10,11... | collective-permute-start | bytes 663560 | tf_op jit(solution)/shard_map/ppermute | solution.py:456
  11.8 5.4 %collective-permute-done.next_ref.prev_ref = f32[27,8,256]{2,1,0:T(8,128)S(1)} collective-permute-done((f32[27,8,256]{2,1,0:T(8,128)S(1)}, f32[27,8,256]{2,1,0:T(8,128)S(1)}, u32[]{:S(2)}, u32[]{:S(2)}) %collective-permute-start) | collective-permute-done | bytes 221216 | tf_op jit(solution)/shard_map/ppermute | solution.py:456
  17.3 4.7 %shard_map.122 = (f32[7,2,32,256]{3,2,1,0:T(8,128)S(1)}, f32[7,2,32,256]{3,2,1,0:T(8,128)S(1)}, f32[3,4,32,256]{3,2,1,0:T(8,128)S(1)}) custom-call(f32[1,3,4,32,256]{4,3,2,1,0:T(8,128)S(1)} %copy-done.7, f32[1,3,4,32,256]{4,3,2,1,0:T(8,128)S(1)} %copy-done.8, f32[1,3,4,32,256]{4,3,2,1,0:T(8,128)S(1)} %copy-done.9, f32[4,32,256]{2,1,0:T(8,128)S(1)} %copy-done.1, ...), custom_call_target="tpu_custom_call" | custom-call | tf_op jit(solution)/shard_map/pallas_call | solution.py:35
  22.1 1.8 %collective-permute-done.1.got_ref.refs_5_ = f32[7,2,32,256]{3,2,1,0:T(8,128)S(1)} collective-permute-done((f32[7,2,32,256]{3,2,1,0:T(8,128)S(1)}, f32[7,2,32,256]{3,2,1,0:T(8,128)S(1)}, u32[]{:S(2)}, u32[]{:S(2)}) %collective-permute-start.1) | collective-permute-done | bytes 458784 | tf_op jit(solution)/shard_map/ppermute | solution.py:418
  24.0 1.8 %collective-permute-start.2 = (f32[8,16,256]{2,1,0:T(8,128)S(1)}, f32[8,16,256]{2,1,0:T(8,128)S(1)}, u32[]{:S(2)}, u32[]{:S(2)}) collective-permute-start(f32[8,16,256]{2,1,0:T(8,128)S(1)} %get-tuple-element.21), channel_id=1, source_target_pairs={{0,4},{2,6},{4,0},{6,2},{8,12},{10,14},{12,8},{14,10},{16,20},{18,... | collective-permute-start | bytes 393224 | tf_op jit(solution)/shard_map/ppermute | solution.py:425
  25.8 1.6 %collective-permute-start.3 = (f32[8,16,256]{2,1,0:T(8,128)S(1)}, f32[8,16,256]{2,1,0:T(8,128)S(1)}, u32[]{:S(2)}, u32[]{:S(2)}) collective-permute-start(f32[8,16,256]{2,1,0:T(8,128)S(1)} %get-tuple-element.22), channel_id=1, source_target_pairs={{0,8},{2,10},{4,12},{6,14},{8,0},{10,2},{12,4},{14,6},{16,24},{18,... | collective-permute-start | bytes 393224 | tf_op jit(solution)/shard_map/ppermute | solution.py:425
  27.6 1.3 %collective-permute-start.10 = (f32[3,4,32,256]{3,2,1,0:T(8,128)S(1)}, f32[3,4,32,256]{3,2,1,0:T(8,128)S(1)}, u32[]{:S(2)}, u32[]{:S(2)}) collective-permute-start(f32[3,4,32,256]{3,2,1,0:T(8,128)S(1)} %get-tuple-element.32), channel_id=1, source_target_pairs={{0,2},{2,4},{4,6},{6,8},{8,10},{10,12},{12,14},{14,16},{16,18},{18... | collective-permute-start | bytes 1179656 | tf_op jit(solution)/shard_map/ppermute | solution.py:479
  29.6 2.6 %collective-permute-done.3.refs_2_ = f32[8,16,256]{2,1,0:T(8,128)S(1)} collective-permute-done((f32[8,16,256]{2,1,0:T(8,128)S(1)}, f32[8,16,256]{2,1,0:T(8,128)S(1)}, u32[]{:S(2)}, u32[]{:S(2)}) %collective-permute-start.3) | collective-permute-done | bytes 131104 | tf_op jit(solution)/shard_map/ppermute | solution.py:425
  32.2 1.5 %collective-permute-done.4.refs_3_ = f32[8,16,256]{2,1,0:T(8,128)S(1)} collective-permute-done((f32[8,16,256]{2,1,0:T(8,128)S(1)}, f32[8,16,256]{2,1,0:T(8,128)S(1)}, u32[]{:S(2)}, u32[]{:S(2)}) %collective-permute-start.4) | collective-permute-done | bytes 131104 | tf_op jit(solution)/shard_map/ppermute | solution.py:425
  33.9 4.9 %collective-permute-start.5 = (f32[6,16,256]{2,1,0:T(8,128)S(1)}, f32[6,16,256]{2,1,0:T(8,128)S(1)}, u32[]{:S(2)}, u32[]{:S(2)}) collective-permute-start(f32[6,16,256]{2,1,0:T(8,128)S(1)} %shard_map.124), channel_id=1, source_target_pairs={{0,16},{2,18},{4,20},{6,22},{8,24},{10,26},{12,28},{14,30},{1,17},... | collective-permute-start | bytes 294920 | tf_op jit(solution)/shard_map/ppermute | solution.py:494
  38.8 2.2 %collective-permute-done.5.refs_8_ = f32[6,16,256]{2,1,0:T(8,128)S(1)} collective-permute-done((f32[6,16,256]{2,1,0:T(8,128)S(1)}, f32[6,16,256]{2,1,0:T(8,128)S(1)}, u32[]{:S(2)}, u32[]{:S(2)}) %collective-permute-start.5) | collective-permute-done | bytes 98336 | tf_op jit(solution)/shard_map/ppermute | solution.py:494
  41.2 1.4 %collective-permute-start.6 = (f32[6,16,256]{2,1,0:T(8,128)S(1)}, f32[6,16,256]{2,1,0:T(8,128)S(1)}, u32[]{:S(2)}, u32[]{:S(2)}) collective-permute-start(f32[6,16,256]{2,1,0:T(8,128)S(1)} %get-tuple-element.25), channel_id=1, source_target_pairs={{0,4},{2,6},{4,0},{6,2},{8,12},{10,14},{12,8},{14,10},{16,20},{18,... | collective-permute-start | bytes 294920 | tf_op jit(solution)/shard_map/ppermute | solution.py:425
  42.6 2.4 %collective-permute-start.7 = (f32[6,16,256]{2,1,0:T(8,128)S(1)}, f32[6,16,256]{2,1,0:T(8,128)S(1)}, u32[]{:S(2)}, u32[]{:S(2)}) collective-permute-start(f32[6,16,256]{2,1,0:T(8,128)S(1)} %get-tuple-element.26), channel_id=1, source_target_pairs={{0,8},{2,10},{4,12},{6,14},{8,0},{10,2},{12,4},{14,6},{16,24},{18,... | collective-permute-start | bytes 294920 | tf_op jit(solution)/shard_map/ppermute | solution.py:425
  45.9 1.8 %collective-permute-done.7.refs_2_ = f32[6,16,256]{2,1,0:T(8,128)S(1)} collective-permute-done((f32[6,16,256]{2,1,0:T(8,128)S(1)}, f32[6,16,256]{2,1,0:T(8,128)S(1)}, u32[]{:S(2)}, u32[]{:S(2)}) %collective-permute-start.7) | collective-permute-done | bytes 98336 | tf_op jit(solution)/shard_map/ppermute | solution.py:425
  47.7 2.9 %collective-permute-done.8.refs_3_ = f32[6,16,256]{2,1,0:T(8,128)S(1)} collective-permute-done((f32[6,16,256]{2,1,0:T(8,128)S(1)}, f32[6,16,256]{2,1,0:T(8,128)S(1)}, u32[]{:S(2)}, u32[]{:S(2)}) %collective-permute-start.8) | collective-permute-done | bytes 98336 | tf_op jit(solution)/shard_map/ppermute | solution.py:425
  51.7 0.9 %collective-permute-done.9.got_ref = f32[6,2,32,256]{3,2,1,0:T(8,128)S(1)} collective-permute-done((f32[6,2,32,256]{3,2,1,0:T(8,128)S(1)}, f32[6,2,32,256]{3,2,1,0:T(8,128)S(1)}, u32[]{:S(2)}, u32[]{:S(2)}) %collective-permute-start.9) | collective-permute-done | bytes 393248 | tf_op jit(solution)/shard_map/ppermute | solution.py:418
  52.6 0.9 %shard_map.127 = (f32[1,3,4,32,256]{4,3,2,1,0:T(8,128)}, f32[1,3,4,32,256]{4,3,2,1,0:T(8,128)}) custom-call(f32[6,2,32,256]{3,2,1,0:T(8,128)S(1)} %get-tuple-element.28.mine_ref, f32[6,2,32,256]{3,2,1,0:T(8,128)S(1)} %collective-permute-done.9.got_ref), custom_call_target="tpu_custom_call" | custom-call | tf_op jit(solution)/shard_map/pallas_call | solution.py:35
  (32 shorter events, 5.0 us)
Async XLA Ops:
  0.6 0.9 %copy-start.1 = (f32[4,32,256]{2,1,0:T(8,128)S(1)}, f32[4,32,256]{2,1,0:T(8,128)}, u32[]{:S(2)}) copy-start(f32[4,32,256]{2,1,0:T(8,128)} %refs_6_.7) | copy-start | bytes 393220
  1.5 0.9 %copy-start.3 = (f32[4,32,256]{2,1,0:T(8,128)S(1)}, f32[4,32,256]{2,1,0:T(8,128)}, u32[]{:S(2)}) copy-start(f32[4,32,256]{2,1,0:T(8,128)} %refs_7_.7) | copy-start | bytes 393220
  2.4 0.9 %copy-start.5 = (f32[4,32,256]{2,1,0:T(8,128)S(1)}, f32[4,32,256]{2,1,0:T(8,128)}, u32[]{:S(2)}) copy-start(f32[4,32,256]{2,1,0:T(8,128)} %refs_8_.1) | copy-start | bytes 393220
  3.3 1.0 %copy-start.7 = (f32[1,3,4,32,256]{4,3,2,1,0:T(8,128)S(1)}, f32[1,3,4,32,256]{4,3,2,1,0:T(8,128)}, u32[]{:S(2)}) copy-start(f32[1,3,4,32,256]{4,3,2,1,0:T(8,128)} %disp_ref.1) | copy-start | bytes 1179652
  4.3 1.0 %copy-start.8 = (f32[1,3,4,32,256]{4,3,2,1,0:T(8,128)S(1)}, f32[1,3,4,32,256]{4,3,2,1,0:T(8,128)}, u32[]{:S(2)}) copy-start(f32[1,3,4,32,256]{4,3,2,1,0:T(8,128)} %vel_ref.1) | copy-start | bytes 1179652
  5.3 1.0 %copy-start.9 = (f32[1,3,4,32,256]{4,3,2,1,0:T(8,128)S(1)}, f32[1,3,4,32,256]{4,3,2,1,0:T(8,128)}, u32[]{:S(2)}) copy-start(f32[1,3,4,32,256]{4,3,2,1,0:T(8,128)} %visc_ref.1) | copy-start | bytes 1179652
  6.3 0.9 %copy-start.10 = (f32[4,32,256]{2,1,0:T(8,128)S(1)}, f32[4,32,256]{2,1,0:T(8,128)}, u32[]{:S(2)}) copy-start(f32[4,32,256]{2,1,0:T(8,128)} %rate_ref.1) | copy-start | bytes 393220
  7.2 0.7 %copy-start.11 = (s32[8,8]{1,0:T(8,128)S(1)}, s32[8,8]{1,0:T(8,128)}, u32[]{:S(2)}) copy-start(s32[8,8]{1,0:T(8,128)} %family_ref.1) | copy-start | bytes 772
  7.9 9.3 %copy-start.12 = (f32[1,4]{1,0:T(1,128)S(1)}, f32[1,4]{1,0:T(1,128)}, u32[]{:S(2)}) copy-start(f32[1,4]{1,0:T(1,128)} %pressure_ref.1) | copy-start | bytes 52
  8.8 15.1 %copy-start.2 = (f32[4,32,256]{2,1,0:T(8,128)S(1)}, f32[4,32,256]{2,1,0:T(8,128)}, u32[]{:S(2)}) copy-start(f32[4,32,256]{2,1,0:T(8,128)} %refs_6_.7) | copy-start | bytes 393220
  8.8 15.1 %copy-start.4 = (f32[4,32,256]{2,1,0:T(8,128)S(1)}, f32[4,32,256]{2,1,0:T(8,128)}, u32[]{:S(2)}) copy-start(f32[4,32,256]{2,1,0:T(8,128)} %refs_7_.7) | copy-start | bytes 393220
  8.8 15.1 %copy-start.6 = (f32[4,32,256]{2,1,0:T(8,128)S(1)}, f32[4,32,256]{2,1,0:T(8,128)}, u32[]{:S(2)}) copy-start(f32[4,32,256]{2,1,0:T(8,128)} %refs_8_.1) | copy-start | bytes 393220
  8.8 8.5 %collective-permute-start = (f32[27,8,256]{2,1,0:T(8,128)S(1)}, f32[27,8,256]{2,1,0:T(8,128)S(1)}, u32[]{:S(2)}, u32[]{:S(2)}) collective-permute-start(f32[27,8,256]{2,1,0:T(8,128)S(1)} %shard_map.121), channel_id=1, source_target_pairs={{0,1},{1,0},{2,3},{3,2},{4,5},{5,4},{6,7},{7,6},{8,9},{9,8},{10,11... | collective-permute-start | bytes 663560 | tf_op jit(solution)/shard_map/ppermute | solution.py:456
  22.0 11.7 %copy-start = (f32[3,3,4,32,256]{4,3,2,1,0:T(8,128)S(1)}, f32[3,3,4,32,256]{4,3,2,1,0:T(8,128)}, u32[]{:S(2)}) copy-start(f32[3,3,4,32,256]{4,3,2,1,0:T(8,128)} %refs_7_.6) | copy-start | bytes 3538948
  22.0 1.9 %collective-permute-start.1 = (f32[7,2,32,256]{3,2,1,0:T(8,128)S(1)}, f32[7,2,32,256]{3,2,1,0:T(8,128)S(1)}, u32[]{:S(2)}, u32[]{:S(2)}) collective-permute-start(f32[7,2,32,256]{3,2,1,0:T(8,128)S(1)} %get-tuple-element.19), channel_id=1, source_target_pairs={{0,2},{2,0},{4,6},{6,4},{8,10},{10,8},{12,14},{14,12},{16,18},{18,... | collective-permute-start | bytes 1376264 | tf_op jit(solution)/shard_map/ppermute | solution.py:418
  24.0 5.6 %collective-permute-start.2 = (f32[8,16,256]{2,1,0:T(8,128)S(1)}, f32[8,16,256]{2,1,0:T(8,128)S(1)}, u32[]{:S(2)}, u32[]{:S(2)}) collective-permute-start(f32[8,16,256]{2,1,0:T(8,128)S(1)} %get-tuple-element.21), channel_id=1, source_target_pairs={{0,4},{2,6},{4,0},{6,2},{8,12},{10,14},{12,8},{14,10},{16,20},{18,... | collective-permute-start | bytes 393224 | tf_op jit(solution)/shard_map/ppermute | solution.py:425
  25.8 6.4 %collective-permute-start.3 = (f32[8,16,256]{2,1,0:T(8,128)S(1)}, f32[8,16,256]{2,1,0:T(8,128)S(1)}, u32[]{:S(2)}, u32[]{:S(2)}) collective-permute-start(f32[8,16,256]{2,1,0:T(8,128)S(1)} %get-tuple-element.22), channel_id=1, source_target_pairs={{0,8},{2,10},{4,12},{6,14},{8,0},{10,2},{12,4},{14,6},{16,24},{18,... | collective-permute-start | bytes 393224 | tf_op jit(solution)/shard_map/ppermute | solution.py:425
  27.4 6.3 %collective-permute-start.4 = (f32[8,16,256]{2,1,0:T(8,128)S(1)}, f32[8,16,256]{2,1,0:T(8,128)S(1)}, u32[]{:S(2)}, u32[]{:S(2)}) collective-permute-start(f32[8,16,256]{2,1,0:T(8,128)S(1)} %get-tuple-element.23), channel_id=1, source_target_pairs={{0,12},{2,14},{4,8},{6,10},{8,4},{10,6},{12,0},{14,2},{16,28},{18,... | collective-permute-start | bytes 393224 | tf_op jit(solution)/shard_map/ppermute | solution.py:425
  27.6 23.3 %collective-permute-start.10 = (f32[3,4,32,256]{3,2,1,0:T(8,128)S(1)}, f32[3,4,32,256]{3,2,1,0:T(8,128)S(1)}, u32[]{:S(2)}, u32[]{:S(2)}) collective-permute-start(f32[3,4,32,256]{3,2,1,0:T(8,128)S(1)} %get-tuple-element.32), channel_id=1, source_target_pairs={{0,2},{2,4},{4,6},{6,8},{8,10},{10,12},{12,14},{14,16},{16,18},{18... | collective-permute-start | bytes 1179656 | tf_op jit(solution)/shard_map/ppermute | solution.py:479
  33.9 7.1 %collective-permute-start.5 = (f32[6,16,256]{2,1,0:T(8,128)S(1)}, f32[6,16,256]{2,1,0:T(8,128)S(1)}, u32[]{:S(2)}, u32[]{:S(2)}) collective-permute-start(f32[6,16,256]{2,1,0:T(8,128)S(1)} %shard_map.124), channel_id=1, source_target_pairs={{0,16},{2,18},{4,20},{6,22},{8,24},{10,26},{12,28},{14,30},{1,17},... | collective-permute-start | bytes 294920 | tf_op jit(solution)/shard_map/ppermute | solution.py:494
  41.2 4.7 %collective-permute-start.6 = (f32[6,16,256]{2,1,0:T(8,128)S(1)}, f32[6,16,256]{2,1,0:T(8,128)S(1)}, u32[]{:S(2)}, u32[]{:S(2)}) collective-permute-start(f32[6,16,256]{2,1,0:T(8,128)S(1)} %get-tuple-element.25), channel_id=1, source_target_pairs={{0,4},{2,6},{4,0},{6,2},{8,12},{10,14},{12,8},{14,10},{16,20},{18,... | collective-permute-start | bytes 294920 | tf_op jit(solution)/shard_map/ppermute | solution.py:425
  42.6 5.0 %collective-permute-start.7 = (f32[6,16,256]{2,1,0:T(8,128)S(1)}, f32[6,16,256]{2,1,0:T(8,128)S(1)}, u32[]{:S(2)}, u32[]{:S(2)}) collective-permute-start(f32[6,16,256]{2,1,0:T(8,128)S(1)} %get-tuple-element.26), channel_id=1, source_target_pairs={{0,8},{2,10},{4,12},{6,14},{8,0},{10,2},{12,4},{14,6},{16,24},{18,... | collective-permute-start | bytes 294920 | tf_op jit(solution)/shard_map/ppermute | solution.py:425
  45.1 5.5 %collective-permute-start.8 = (f32[6,16,256]{2,1,0:T(8,128)S(1)}, f32[6,16,256]{2,1,0:T(8,128)S(1)}, u32[]{:S(2)}, u32[]{:S(2)}) collective-permute-start(f32[6,16,256]{2,1,0:T(8,128)S(1)} %get-tuple-element.27), channel_id=1, source_target_pairs={{0,12},{2,14},{4,8},{6,10},{8,4},{10,6},{12,0},{14,2},{16,28},{18,... | collective-permute-start | bytes 294920 | tf_op jit(solution)/shard_map/ppermute | solution.py:425
  50.8 1.8 %collective-permute-start.9 = (f32[6,2,32,256]{3,2,1,0:T(8,128)S(1)}, f32[6,2,32,256]{3,2,1,0:T(8,128)S(1)}, u32[]{:S(2)}, u32[]{:S(2)}) collective-permute-start(f32[6,2,32,256]{3,2,1,0:T(8,128)S(1)} %get-tuple-element.29), channel_id=1, source_target_pairs={{0,2},{2,0},{4,6},{6,4},{8,10},{10,8},{12,14},{14,12},{16,18},{18,... | collective-permute-start | bytes 1179656 | tf_op jit(solution)/shard_map/ppermute | solution.py:418

commit v2 on v0

v2 whole, which is shorter than its diff:
```python
import functools
import math

import jax
import jax.numpy as jnp
from jax import lax
from jax.experimental import pallas as pl
from jax.experimental.pallas import tpu as pltpu
from jax.sharding import PartitionSpec as P

STEPS = 4
BLK_AX = 4
BLK_CIR = 32
COEF_AXIAL = 0.22
COEF_CIRC = 0.22
COEF_RADIAL = 0.12
VISC_SHARE = 0.6
TIME_STEP = 1.0
FIBER_ANGLES = (0.5, -0.5, 0.9, -0.9)
CORES = 2
HALO = STEPS
F32 = jnp.float32
VMEM_LIMIT = 24 * 1024 * 1024


def call(kernel, out_shape, operands, scratch=(), in_hbm=(), aliases={}):
    specs = []
    for k in range(len(operands)):
        specs.append(pl.BlockSpec(memory_space=pltpu.HBM if k in in_hbm else pltpu.VMEM))
    return pl.pallas_call(
        kernel,
        out_shape=out_shape,
        in_specs=specs,
        out_specs=jax.tree.map(lambda _: pl.BlockSpec(memory_space=pltpu.VMEM), out_shape),
        scratch_shapes=list(scratch),
        compiler_params=pltpu.CompilerParams(vmem_limit_bytes=VMEM_LIMIT),
        input_output_aliases=aliases,
    )(*operands)


def shape(*dims):
    return jax.ShapeDtypeStruct(dims, F32)


def iota(dims, axis):
    return lax.broadcasted_iota(jnp.int32, dims, axis)


def low_rows(cols):
    return iota((8, cols), 0) < HALO


def rolled_tile(load, tile, tiles, cols):
    last = (tile + tiles - 1) % tiles if isinstance(tile, int) else lax.rem(tile + tiles - 1, tiles)
    return jnp.where(low_rows(cols), pltpu.roll(load(last), 4, 0), pltpu.roll(load(tile), 4, 0))


def direction_tile(family_ref, first, second, cols):
    block = iota((8, cols), 1) // BLK_CIR
    family = jnp.zeros((8, cols), jnp.int32)
    for k in range(cols // BLK_CIR):
        index = jnp.where(low_rows(cols), family_ref[first, k], family_ref[second, k])
        family = jnp.where(block == k, index, family)
    cosine = jnp.zeros((8, cols), F32)
    sine = jnp.zeros((8, cols), F32)
    for index, angle in enumerate(FIBER_ANGLES):
        cosine = jnp.where(family == index, math.cos(angle), cosine)
        sine = jnp.where(family == index, math.sin(angle), sine)
    return cosine, sine


def pack_kernel(sides, *refs):
    fields, family_ref = refs[:7], refs[7]
    outs = refs[8 : 8 + len(sides)]
    states, statics, family_s, sem = refs[8 + len(sides) :]
    rows, cols = fields[0].shape[-2:]
    block_rows = family_ref.shape[0]
    place = lax.axis_index("space")
    directions = pltpu.make_async_copy(family_ref, family_s, sem.at[7])
    for n, (out_ref, side) in enumerate(zip(outs, sides)):
        tail = (place == 0) if side == "facing" else jnp.bool_(side == "tail")
        start = pl.multiple_of(jnp.where(tail, rows - 8, 0), 8)
        copies = [] if n else [directions]
        for k in range(3):
            source = fields[k].at[0, :, :, pl.ds(start, 8), :]
            copies.append(pltpu.make_async_copy(source, states.at[k], sem.at[k]))
        for k in range(4):
            source = fields[3 + k].at[:, pl.ds(start, 8), :]
            copies.append(pltpu.make_async_copy(source, statics.at[k], sem.at[3 + k]))
        for copy in copies:
            copy.start()
        for copy in copies:
            copy.wait()
        low = low_rows(cols)

        def pair(first, second):
            up = pltpu.roll(first, 4, 0)
            down = pltpu.roll(second, 4, 0)
            return jnp.where(tail, jnp.where(low, up, second), jnp.where(low, first, down))

        at = 0
        for k in range(3):
            for comp in range(3):
                for layer in range(0, 4, 2):
                    out_ref[at] = pair(states[k, comp, layer], states[k, comp, layer + 1])
                    at += 1
        for k in range(4):
            for layer in range(0, 4, 2):
                out_ref[at] = pair(statics[k, layer], statics[k, layer + 1])
                at += 1
        end_block = jnp.where(tail, block_rows - 1, 0)
        cosine, sine = direction_tile(family_s, end_block, end_block, cols)
        out_ref[at] = jnp.where(low, cosine, sine)


def coarse(inv_mass, damping, stiff, weight):
    half_step = 0.5 * STEPS * TIME_STEP
    k = inv_mass * (2.0 * (COEF_AXIAL + COEF_CIRC + COEF_RADIAL) + 2.0 * stiff * weight)
    damp = half_step * damping
    square = half_step * half_step * k
    scale = 1.0 / (1.0 + damp + square)
    return (
        (1.0 + damp - square) * scale,
        (2.0 * half_step) * scale,
        (-2.0 * half_step) * k * scale,
        (1.0 - damp - square) * scale,
    )


class Window:
    def __init__(self, refs):
        self.u, self.v, self.q, self.sigma, self.weight, self.static, self.dirs, self.load = refs
        self.steps, _, self.layers, self.tiles, _, self.cols = self.u.shape

    @staticmethod
    def shapes(layers, tiles, cols):
        return (
            [(STEPS + 1, 3, layers, tiles, 8, cols)] * 3
            + [(STEPS, layers, tiles, 8, cols)] * 2
            + [(MASS_TO_SHARE, layers, tiles, 8, cols)]
            + [(9, tiles, 8, cols), (STEPS, 8, cols)]
        )


MASS, DAMP, RATE, STIFF, DECAY, SHARE, MASS_TO_SHARE = range(7)


def pred(a, before):
    return jnp.where(iota(a.shape, 0) == 0, pltpu.roll(before, 1, 0), pltpu.roll(a, 1, 0))


def succ(a, after):
    return jnp.where(iota(a.shape, 0) == 7, pltpu.roll(after, 7, 0), pltpu.roll(a, 7, 0))


def right(a):
    return pltpu.roll(a, a.shape[1] - 1, 1)


def left(a):
    return pltpu.roll(a, 1, 1)


def prepare(win, before_dirs):
    pairs = []
    for tile in range(win.tiles):
        cosine, sine = win.dirs[0, tile], win.dirs[1, tile]
        pairs.append((cosine * cosine, cosine * sine, sine * sine))
    for tile in range(win.tiles):
        cc, cs, ss = pairs[tile]
        before = before_dirs(tile, pairs)
        values = (cc, cs, ss, cc + cs, cs + ss, pred(cc, before[0]), pred(cs, before[1]), left(cs), left(ss))
        for k, value in enumerate(values):
            win.dirs[k, tile] = value
        for layer in range(win.layers):
            decay = jnp.exp(-TIME_STEP * win.static[RATE, layer, tile])
            win.static[DECAY, layer, tile] = decay
            win.static[SHARE, layer, tile] = (1.0 - decay) * VISC_SHARE


def fine_steps(win, order, before, after, before_sigma):
    def step(s, carry):
        def neighbours(layer, tile):
            u = [win.u[s, comp, layer, tile] for comp in range(3)]
            ahead = [succ(u[comp], after(s, comp, layer, tile)) for comp in range(3)]
            return u, ahead, [right(a) for a in u]

        def stress(layer, tile, u, ahead, beside):
            strain = (
                win.dirs[0, tile] * (ahead[1] - u[1])
                + win.dirs[2, tile] * (beside[2] - u[2])
                + win.dirs[1, tile] * ((ahead[2] - u[2]) + (beside[1] - u[1]))
            )
            weight = jnp.exp(strain * strain)
            sigma = win.static[STIFF, layer, tile] * weight * strain
            win.sigma[s, layer, tile] = sigma
            win.weight[s, layer, tile] = weight
            return sigma

        for layer in range(win.layers):
            known = {}
            if before_sigma is None:
                known[order[-1]] = stress(layer, order[-1], *neighbours(layer, order[-1]))
            for n, tile in enumerate(order):
                u, ahead, beside = neighbours(layer, tile)
                if tile not in known:
                    known[tile] = stress(layer, tile, u, ahead, beside)
                sigma = known[tile]
                last = known[order[n - 1]] if before_sigma is None else before_sigma(s, layer, tile, sigma)
                sigma_pred, sigma_left = pred(sigma, last), left(sigma)
                behind = [pred(u[comp], before(s, comp, layer, tile)) for comp in range(3)]
                fiber = [None] + [
                    win.dirs[3 + k, tile] * sigma
                    - win.dirs[5 + k, tile] * sigma_pred
                    - win.dirs[7 + k, tile] * sigma_left
                    for k in range(2)
                ]
                for comp in range(3):
                    around = (ahead[comp] + behind[comp]) + (beside[comp] + left(u[comp]))
                    if layer == 0:
                        radial = win.u[s, comp, layer + 1, tile]
                    elif layer == win.layers - 1:
                        radial = win.u[s, comp, layer - 1, tile]
                    else:
                        radial = win.u[s, comp, layer - 1, tile] + win.u[s, comp, layer + 1, tile]
                    elastic = (COEF_AXIAL * around + COEF_RADIAL * radial) - (
                        2.0 * (COEF_AXIAL + COEF_CIRC + COEF_RADIAL)
                    ) * u[comp]
                    visc = win.q[s, comp, layer, tile]
                    force = elastic + visc
                    if fiber[comp] is not None:
                        force = force + fiber[comp]
                    elif layer == 0:
                        force = force + win.load[s]
                    vel = win.v[s, comp, layer, tile]
                    vel = vel + (win.static[MASS, layer, tile] * force - win.static[DAMP, layer, tile] * vel)
                    win.v[s + 1, comp, layer, tile] = vel
                    win.u[s + 1, comp, layer, tile] = u[comp] + vel
                    win.q[s + 1, comp, layer, tile] = (
                        win.static[DECAY, layer, tile] * visc + win.static[SHARE, layer, tile] * elastic
                    )
        return carry

    lax.fori_loop(0, STEPS, step, 0)


def put_maps(win, tiles, end, keep_ref, send_ref, end_visc_ref):
    core = lax.rem(lax.axis_index("tm"), CORES)
    half = win.layers // CORES
    for layer in range(win.layers):
        for tile in tiles:
            weight = end(lambda w: w.weight.at[0], layer, tile)
            g = coarse(win.static[MASS, layer, tile], win.static[DAMP, layer, tile], win.static[STIFF, layer, tile], weight)
            pieces = [weight]
            start = [(win.u[0, comp, layer, tile], win.v[0, comp, layer, tile]) for comp in range(3)]
            for comp, (disp, vel) in enumerate(start):
                pieces.append(end(lambda w: w.u.at[STEPS, comp], layer, tile) - (g[0] * disp + g[1] * vel))
            for comp, (disp, vel) in enumerate(start):
                pieces.append(end(lambda w: w.v.at[STEPS, comp], layer, tile) - (g[2] * disp + g[3] * vel))
            to = (layer % half) * win.tiles + tile

            @pl.when(core == layer // half)
            def _():
                for k, piece in enumerate(pieces):
                    keep_ref[k, to] = piece

            @pl.when(core != layer // half)
            def _():
                for k, piece in enumerate(pieces):
                    send_ref[k, to] = piece

            for comp in range(3):
                end_visc_ref[comp, layer, tile] = end(lambda w: w.q.at[STEPS, comp], layer, tile)


def inner_kernel(*refs):
    fields, family_ref, pressure_ref, outs = refs[:7], refs[7], refs[8], refs[9:12]
    win = Window(refs[12:20])
    facing_ref = refs[20]
    states, statics, family_s, pressure_s, sem = refs[21:]
    tiles, cols, layers = win.tiles, win.cols, win.layers
    blocks = family_ref.shape[0]
    copies = []
    for k in range(3):
        copies.append(pltpu.make_async_copy(fields[k].at[0], states.at[k], sem.at[k]))
    for k in range(4):
        copies.append(pltpu.make_async_copy(fields[3 + k], statics.at[k], sem.at[3 + k]))
    directions = pltpu.make_async_copy(family_ref, family_s, sem.at[7])
    loads = pltpu.make_async_copy(pressure_ref, pressure_s, sem.at[8])
    for copy in (directions, loads, *copies):
        copy.start()
    directions.wait()
    loads.wait()
    for tile in range(tiles):
        win.dirs[0, tile], win.dirs[1, tile] = direction_tile(
            family_s, (2 * tile + blocks - 1) % blocks, 2 * tile, cols
        )
    facing_ref[0], facing_ref[1] = win.dirs[0, 0], win.dirs[1, 0]
    for s in range(STEPS):
        win.load[s] = jnp.full((8, cols), pressure_s[0, s], F32)

    def rolled(source, target):
        rows = [pltpu.roll(source[8 * tile : 8 * tile + 8, :], 4, 0) for tile in range(tiles)]
        for tile in range(tiles):
            target[tile] = jnp.where(low_rows(cols), rows[tile - 1], rows[tile])

    for k, target in enumerate((win.u, win.v, win.q)):
        copies[k].wait()
        for comp in range(3):
            for layer in range(layers):
                rolled(states.at[k, comp, layer], target.at[0, comp, layer])
    for k in range(4):
        copies[3 + k].wait()
        for layer in range(layers):
            rolled(statics.at[k, layer], win.static.at[k, layer])
    prepare(win, lambda tile, pairs: pairs[tile - 1])
    fine_steps(
        win, [*range(1, tiles), 0],
        lambda s, comp, layer, tile: win.u[s, comp, layer, (tile + tiles - 1) % tiles],
        lambda s, comp, layer, tile: win.u[s, comp, layer, (tile + 1) % tiles],
        None,
    )
    put_maps(win, range(1, tiles), lambda of, layer, tile: of(win)[layer, tile], *outs)


def outer_kernel(*refs):
    next_ref, prev_ref = refs[:2]
    inner = Window(refs[2:10])
    facing_ref = refs[13]
    outs = refs[14:17]
    win = Window(refs[17:])
    layers, cols = win.layers, win.cols
    place = lax.axis_index("space")
    has_next = place < lax.axis_size("space") - 1
    has_prev = place > 0
    low = low_rows(cols)
    live = jnp.where(low, has_prev.astype(jnp.int32), has_next.astype(jnp.int32)) > 0

    def halo(at, own, target):
        after, before = next_ref[at], prev_ref[at]
        for j in range(2):
            ahead = pltpu.roll(after, 4, 0) if j == 0 else after
            behind = before if j == 0 else pltpu.roll(before, 4, 0)
            target(j)[0] = jnp.where(low, own(j), jnp.where(live, ahead, 0.0))
            target(j)[1] = jnp.where(low, jnp.where(live, behind, 0.0), own(j))

    at = 0
    for source, target in ((inner.u, win.u), (inner.v, win.v), (inner.q, win.q)):
        for comp in range(3):
            for layer in range(0, layers, 2):
                halo(at, lambda j: source[0, comp, layer + j, 0], lambda j: target.at[0, comp, layer + j])
                at += 1
    for k in (MASS, DAMP, RATE, STIFF):
        for layer in range(0, layers, 2):
            halo(at, lambda j: inner.static[k, layer + j, 0], lambda j: win.static.at[k, layer + j])
            at += 1
    halo(at, lambda j: facing_ref[j], lambda j: win.dirs.at[j])
    for s in range(STEPS):
        win.load[s] = inner.load[s]
    last = inner.tiles - 1
    prepare(win, lambda tile, pairs: (inner.dirs[0, last], inner.dirs[1, last]))
    fine_steps(
        win, [0, 1],
        lambda s, comp, layer, tile: inner.u[s, comp, layer, last],
        lambda s, comp, layer, tile: inner.u[s, comp, layer, 1],
        lambda s, layer, tile, own: inner.sigma[s, layer, last],
    )

    def end(of, layer, tile):
        return jnp.where(low, of(win)[layer, 0], of(win)[layer, 1])

    put_maps(inner, [0], end, *outs)


class Cut:
    def __init__(self, group, half, tiles, cols):
        self.group, self.half, self.tiles, self.cols = group, half, tiles, cols
        self.count = half * tiles
        self.size = self.count // group

    def of(self, part):
        first = part * self.size
        core = lax.rem(lax.axis_index("tm"), CORES)
        return first, core * self.half + first // self.tiles, lax.rem(first, self.tiles)

    def place(self):
        return lax.rem(lax.axis_index("tm") // CORES, self.group)


def part_coarse(static_ref, layer, tile, weight):
    return coarse(static_ref[MASS, layer, tile], static_ref[DAMP, layer, tile], static_ref[STIFF, layer, tile], weight)


def compose_kernel(cut, keep_ref, got_ref, static_ref, *outs):
    first_core = lax.rem(lax.axis_index("tm"), CORES) == 0
    for m in range(cut.group):
        first, layer, tile = cut.of(jnp.bitwise_xor(cut.place(), m))
        for i in range(cut.size):
            keep = [keep_ref[k, first + i] for k in range(7)]
            got = [got_ref[k, first + i] for k in range(7)]
            early = [jnp.where(first_core, a, b) for a, b in zip(keep, got)]
            late = [jnp.where(first_core, b, a) for a, b in zip(keep, got)]
            g = part_coarse(static_ref, layer, tile + i, late[0])
            outs[m][0, i] = early[0]
            outs[m][1, i] = late[0]
            for comp in range(3):
                a, b = early[1 + comp], early[4 + comp]
                outs[m][2 + comp, i] = (g[0] * a + g[1] * b) + late[1 + comp]
                outs[m][5 + comp, i] = (g[2] * a + g[3] * b) + late[4 + comp]


def chain(cut, parts, maps, static_ref, start, visit):
    place = cut.place()
    _, layer, tile = cut.of(place)
    for m in range(cut.group):
        maps[jnp.bitwise_xor(place, m)] = parts[m][...]
    for i in range(cut.size):
        state = [start(k, layer, tile + i, i) for k in range(6)]
        for s in range(cut.group):
            visit(s, i, state)
            first = part_coarse(static_ref, layer, tile + i, maps[s, 0, i])
            second = part_coarse(static_ref, layer, tile + i, maps[s, 1, i])
            new = [None] * 6
            for comp in range(3):
                a, b = state[comp], state[3 + comp]
                a, b = first[0] * a + first[1] * b, first[2] * a + first[3] * b
                new[comp] = (second[0] * a + second[1] * b) + maps[s, 2 + comp, i]
                new[3 + comp] = (second[2] * a + second[3] * b) + maps[s, 5 + comp, i]
            state = new
        visit(cut.group, i, state)


def first_state(cut, init_ref):
    def start(k, layer, tile, i):
        def load(t):
            return init_ref[k // 3, k % 3, layer, pl.ds(pl.multiple_of(8 * t, 8), 8), :]

        return rolled_tile(load, tile, cut.tiles, cut.cols)

    return start


def lower_kernel(cut, *refs):
    parts = refs[: cut.group]
    static_ref, init_ref, out_ref, maps = refs[cut.group :]

    def visit(s, i, state):
        if s == cut.group:
            for k in range(6):
                out_ref[k, i] = state[k]

    chain(cut, parts, maps, static_ref, first_state(cut, init_ref), visit)


def upper_kernel(cut, *refs):
    parts = refs[: cut.group]
    static_ref, init_ref, hop_ref = refs[cut.group : cut.group + 3]
    outs = refs[cut.group + 3 : 2 * cut.group + 3]
    maps, found = refs[2 * cut.group + 3 :]
    lower = lax.axis_index("tm") < CORES * cut.group
    first = first_state(cut, init_ref)

    def start(k, layer, tile, i):
        return jnp.where(lower, first(k, layer, tile, i), hop_ref[k, i])

    def visit(s, i, state):
        if s < cut.group:
            for k in range(6):
                found[s, k, i] = state[k]

    chain(cut, parts, maps, static_ref, start, visit)
    for m in range(cut.group):
        outs[m][...] = found[jnp.bitwise_xor(cut.place(), m)]


def spread_kernel(cut, *refs):
    parts = refs[: cut.group]
    keep_ref, got_ref, static_ref, mine_ref, send_ref = refs[cut.group :]
    first_core = lax.rem(lax.axis_index("tm"), CORES) == 0
    for m in range(cut.group):
        first, layer, tile = cut.of(jnp.bitwise_xor(cut.place(), m))
        for i in range(cut.size):
            early = [jnp.where(first_core, keep_ref[k, first + i], got_ref[k, first + i]) for k in range(7)]
            g = part_coarse(static_ref, layer, tile + i, early[0])
            for comp in range(3):
                a, b = parts[m][comp, i], parts[m][3 + comp, i]
                next_a = (g[0] * a + g[1] * b) + early[1 + comp]
                next_b = (g[2] * a + g[3] * b) + early[4 + comp]
                mine_ref[comp, first + i] = jnp.where(first_core, a, next_a)
                mine_ref[3 + comp, first + i] = jnp.where(first_core, b, next_b)
                send_ref[comp, first + i] = jnp.where(first_core, next_a, a)
                send_ref[3 + comp, first + i] = jnp.where(first_core, next_b, b)


def unroll(load, store, tiles, cols):
    rows = [pltpu.roll(load(tile), 4, 0) for tile in range(tiles)]
    for tile in range(tiles):
        store(slice(8 * tile, 8 * tile + 8), jnp.where(low_rows(cols), rows[tile], rows[(tile + 1) % tiles]))


def join_kernel(cut, mine_ref, got_ref, disp_ref, vel_ref):
    core = lax.rem(lax.axis_index("tm"), CORES)
    for k in range(6):
        for layer in range(cut.half):
            for source, own in ((mine_ref, core), (got_ref, 1 - core)):
                def store(rows, value):
                    (disp_ref, vel_ref)[k // 3][0, k % 3, own * cut.half + layer, rows, :] = value

                unroll(lambda tile: source[k, layer * cut.tiles + tile], store, cut.tiles, cut.cols)


def visc_kernel(cut, visc_ref, init_ref, out_ref):
    first_slab = lax.axis_index("tm") == 0
    for comp in range(3):
        for layer in range(visc_ref.shape[1]):
            def store(rows, value):
                out_ref[0, comp, layer, rows, :] = jnp.where(first_slab, init_ref[2, comp, layer, rows, :], value)

            unroll(lambda tile: visc_ref[comp, layer, tile], store, cut.tiles, cut.cols)


def swap_cores(value):
    count = lax.axis_size("tm")
    return lax.ppermute(value, "tm", [(i, i ^ 1) for i in range(count)])


def transpose_parts(parts):
    count = lax.axis_size("tm")
    done = [parts[0]]
    for m in range(1, len(parts)):
        done.append(lax.ppermute(parts[m], "tm", [(i, i ^ (CORES * m)) for i in range(count)]))
    return done


def shards(
    start_disp, start_vel, start_visc, init_state, inv_mass, damping_rate, visc_rate, fiber_stiff,
    fiber_family, pressure,
):
    slabs, spaces = lax.axis_size("tm"), lax.axis_size("space")
    group = slabs // CORES // 2
    layers, rows, cols = inv_mass.shape
    half, tiles = layers // CORES, rows // 8
    cut = Cut(group, half, tiles, cols)

    packed = shape((9 * layers + 4 * layers + 2) // 2, 8, cols)
    sides = ("facing",) if spaces == 2 else ("tail", "head")
    in_hbm = [
        pltpu.with_memory_space_constraint(x, pltpu.HBM)
        for x in (
            start_disp, start_vel, start_visc, inv_mass, damping_rate, visc_rate, fiber_stiff, fiber_family, pressure
        )
    ]
    packs = call(
        functools.partial(pack_kernel, sides),
        [packed] * len(sides),
        in_hbm[:8],
        [
            pltpu.VMEM((3, 3, layers, 8, cols), F32),
            pltpu.VMEM((4, layers, 8, cols), F32),
            pltpu.SMEM(fiber_family.shape, jnp.int32),
            pltpu.SemaphoreType.DMA((8,)),
        ],
        in_hbm=range(8),
    )
    if spaces == 2:
        after = before = lax.ppermute(packs[0], "space", [(0, 1), (1, 0)])
    else:
        before = lax.ppermute(packs[0], "space", [(i, i + 1) for i in range(spaces - 1)])
        after = lax.ppermute(packs[1], "space", [(i + 1, i) for i in range(spaces - 1)])

    map_shape = shape(7, cut.count, 8, cols)
    outs = [map_shape, map_shape, shape(3, layers, tiles, 8, cols)]
    held = [shape(*dims) for dims in Window.shapes(layers, tiles, cols)]
    partial = call(
        inner_kernel,
        outs + held + [shape(2, 8, cols)],
        in_hbm,
        [
            pltpu.VMEM((3, 3, layers, rows, cols), F32),
            pltpu.VMEM((4, layers, rows, cols), F32),
            pltpu.SMEM(fiber_family.shape, jnp.int32),
            pltpu.SMEM(pressure.shape, F32),
            pltpu.SemaphoreType.DMA((9,)),
        ],
        in_hbm=range(9),
    )
    ends, held, facing = partial[:3], partial[3:11], partial[11]
    keep, send, end_visc = call(
        outer_kernel,
        outs,
        (after, before, *held, *ends, facing),
        [pltpu.VMEM(dims, F32) for dims in Window.shapes(layers, 2, cols)],
        aliases={10: 0, 11: 1, 12: 2},
    )
    static = held[5]
    got = swap_cores(send)
    visc = lax.ppermute(end_visc, "tm", [(i, i + 1) for i in range(slabs - 1)])

    parts = call(
        functools.partial(compose_kernel, cut), [shape(8, cut.size, 8, cols)] * group, (keep, got, static)
    )
    parts = transpose_parts(parts)
    maps = pltpu.VMEM((group, 8, cut.size, 8, cols), F32)
    edge = call(
        functools.partial(lower_kernel, cut), shape(6, cut.size, 8, cols), (*parts, static, init_state), [maps]
    )
    hop = lax.ppermute(edge, "tm", [(i, i + slabs // 2) for i in range(slabs // 2)])
    states = call(
        functools.partial(upper_kernel, cut),
        [shape(6, cut.size, 8, cols)] * group,
        (*parts, static, init_state, hop),
        [maps, pltpu.VMEM((group, 6, cut.size, 8, cols), F32)],
    )
    states = transpose_parts(states)
    mine, other = call(
        functools.partial(spread_kernel, cut), [shape(6, cut.count, 8, cols)] * 2, (*states, keep, got, static)
    )
    other = swap_cores(other)
    field = shape(1, 3, layers, rows, cols)
    new_disp, new_vel = call(functools.partial(join_kernel, cut), [field, field], (mine, other))
    new_visc = call(functools.partial(visc_kernel, cut), field, (visc, init_state))
    return new_disp, new_vel, new_visc


def solution(mesh):
    slab = P("tm", None, None, "space", None)
    cell = P(None, "space", None)
    return jax.shard_map(
        shards,
        mesh=mesh,
        in_specs=(
            slab, slab, slab, P(None, None, None, "space", None), cell, cell, cell, cell,
            P("space", None), P("tm", None),
        ),
        out_specs=(slab, slab, slab),
        check_vma=False,
    )
```

time: 257 us -> 46.6 us (0.18)
  the two profiles are of different devices: /device:TPU:27 before, /device:TPU:24 now
where the time goes in v2:
time: 46.6 us; the launch traced here: 46.3 us
  waiting for transfers between devices  23.3 us (50%)
  starting transfers between devices  12 us (26%)
  Pallas kernels  10.2 us (22%)
  between operations  0.73 us (2%)
    pallas_call x9, Pallas kernels, call(): pl.pallas_call(kernel, out_shape=out_shape, in_specs=specs, out_specs=jax...  10.2 us
    ppermute x6, waiting for transfers between devices, transpose_parts(): lax.ppermute(parts[m], 'tm', [(i, i ^ CORES * m) for i in range(count)])  7.79 us
    ppermute x1, waiting for transfers between devices, shards(): lax.ppermute(edge, 'tm', [(i, i + slabs // 2) for i in range(slabs // 2)])  7.28 us
    ppermute x6, starting transfers between devices, transpose_parts(): lax.ppermute(parts[m], 'tm', [(i, i ^ CORES * m) for i in range(count)])  7.11 us
    ppermute x1, waiting for transfers between devices, shards(): visc = lax.ppermute(end_visc, 'tm', [(i, i + 1) for i in range(slabs - 1)])  6.03 us
    ppermute x1, starting transfers between devices, shards(): visc = lax.ppermute(end_visc, 'tm', [(i, i + 1) for i in range(slabs - 1)])  1.91 us
    ppermute x2, waiting for transfers between devices, swap_cores(): return lax.ppermute(value, 'tm', [(i, i ^ 1) for i in range(count)])  1.81 us
    ppermute x1, starting transfers between devices, shards(): after = before = lax.ppermute(packs[0], 'space', [(0, 1), (1, 0)])  1.58 us
  transfers between devices with their start and end apart: 11, of which 10 were waited for; matrix products, arithmetic and copies ran while one was open for 0% of the time, Pallas kernels for 13%

profile of v2, /device:TPU:24, one launch (start us, length us, event | category | flops | bytes accessed | tf_op | source)
XLA Modules:
  0.0 46.3 jit_solution(818302617933672837)
XLA Ops:
  0.6 1.1 %shard_map.121 = f32[27,8,256]{2,1,0:T(8,128)S(1)} custom-call(f32[1,3,4,32,256]{4,3,2,1,0:T(8,128)} %refs_0_.3, f32[1,3,4,32,256]{4,3,2,1,0:T(8,128)} %refs_1_.3, f32[1,3,4,32,256]{4,3,2,1,0:T(8,128)} %refs_2_.3, f32[4,32,256]{2,1,0:T(8,128)} %refs_3_.3, f32[4,32,256]{2,1,0:T(8,128)} %refs_4_.3, f32[4,32,256]{2,1,0:T(8,128)} %refs_5_.5, ...), custom_call_target="tpu_custom_call" | custom-call | tf_op jit(solution)/shard_map/pallas_call | solution.py:30
  1.8 1.6 %collective-permute-start = (f32[27,8,256]{2,1,0:T(8,128)S(1)}, f32[27,8,256]{2,1,0:T(8,128)S(1)}, u32[]{:S(2)}, u32[]{:S(2)}) collective-permute-start(f32[27,8,256]{2,1,0:T(8,128)S(1)} %shard_map.121), channel_id=1, source_target_pairs={{0,1},{1,0},{2,3},{3,2},{4,5},{5,4},{6,7},{7,6},{8,9},{9,8},{10,11... | collective-permute-start | bytes 663560 | tf_op jit(solution)/shard_map/ppermute | solution.py:566
  3.3 5.2 %shard_map.122 = (f32[7,8,8,256]{3,2,1,0:T(8,128)S(1)}, f32[7,8,8,256]{3,2,1,0:T(8,128)S(1)}, f32[3,4,4,8,256]{4,3,2,1,0:T(8,128)S(1)}, f32[5,3,4,4,8,256]{5,4,3...) custom-call(f32[1,3,4,32,256]{4,3,2,1,0:T(8,128)} %refs_0_.3, ...), custom_call_target="tpu_custom_call" | custom-call | tf_op jit(solution)/shard_map/pallas_call | solution.py:30
  8.6 0.4 collective-permute-done.refs_0_.refs_1_
  9.0 1.3 %shard_map.123 = (f32[7,8,8,256]{3,2,1,0:T(8,128)S(1)}, f32[7,8,8,256]{3,2,1,0:T(8,128)S(1)}, f32[3,4,4,8,256]{4,3,2,1,0:T(8,128)S(1)}) custom-call(f32[27,8,256]{2,1,0:T(8,128)S(1)} %collective-permute-done.refs_0_.refs_1_, f32[27,8,256]{2,1,0:T(8,128)S(1)} %collective-permute-done.refs_0_.refs_1_, ...), custom_call_target="tpu_custom_call", output_to_operand_aliasing={{0}: (10, {}), {1}: (11, {}), {2}: (12, {})} | custom-call | tf_op jit(solution)/shard_map/pallas_call | solution.py:30
  10.4 1.8 %collective-permute-done.1.got_ref.refs_5_ = f32[7,8,8,256]{3,2,1,0:T(8,128)S(1)} collective-permute-done((f32[7,8,8,256]{3,2,1,0:T(8,128)S(1)}, f32[7,8,8,256]{3,2,1,0:T(8,128)S(1)}, u32[]{:S(2)}, u32[]{:S(2)}) %collective-permute-start.1) | collective-permute-done | bytes 458784 | tf_op jit(solution)/shard_map/ppermute | solution.py:524
  12.4 1.6 %collective-permute-start.2 = (f32[8,2,8,256]{3,2,1,0:T(8,128)S(1)}, f32[8,2,8,256]{3,2,1,0:T(8,128)S(1)}, u32[]{:S(2)}, u32[]{:S(2)}) collective-permute-start(f32[8,2,8,256]{3,2,1,0:T(8,128)S(1)} %get-tuple-element.45), channel_id=1, source_target_pairs={{0,4},{2,6},{4,0},{6,2},{8,12},{10,14},{12,8},{14,10},{16,20},{18,... | collective-permute-start | bytes 393224 | tf_op jit(solution)/shard_map/ppermute | solution.py:531
  13.9 0.4 collective-permute-start.3
  14.4 1.5 %collective-permute-start.4 = (f32[8,2,8,256]{3,2,1,0:T(8,128)S(1)}, f32[8,2,8,256]{3,2,1,0:T(8,128)S(1)}, u32[]{:S(2)}, u32[]{:S(2)}) collective-permute-start(f32[8,2,8,256]{3,2,1,0:T(8,128)S(1)} %get-tuple-element.47), channel_id=1, source_target_pairs={{0,12},{2,14},{4,8},{6,10},{8,4},{10,6},{12,0},{14,2},{16,28},{18,... | collective-permute-start | bytes 393224 | tf_op jit(solution)/shard_map/ppermute | solution.py:531
  15.9 2.0 %collective-permute-done.2.refs_1_ = f32[8,2,8,256]{3,2,1,0:T(8,128)S(1)} collective-permute-done((f32[8,2,8,256]{3,2,1,0:T(8,128)S(1)}, f32[8,2,8,256]{3,2,1,0:T(8,128)S(1)}, u32[]{:S(2)}, u32[]{:S(2)}) %collective-permute-start.2) | collective-permute-done | bytes 131104 | tf_op jit(solution)/shard_map/ppermute | solution.py:531
  18.0 2.3 %collective-permute-done.3.refs_2_ = f32[8,2,8,256]{3,2,1,0:T(8,128)S(1)} collective-permute-done((f32[8,2,8,256]{3,2,1,0:T(8,128)S(1)}, f32[8,2,8,256]{3,2,1,0:T(8,128)S(1)}, u32[]{:S(2)}, u32[]{:S(2)}) %collective-permute-start.3) | collective-permute-done | bytes 131104 | tf_op jit(solution)/shard_map/ppermute | solution.py:531
  20.3 1.7 %collective-permute-done.4.refs_3_ = f32[8,2,8,256]{3,2,1,0:T(8,128)S(1)} collective-permute-done((f32[8,2,8,256]{3,2,1,0:T(8,128)S(1)}, f32[8,2,8,256]{3,2,1,0:T(8,128)S(1)}, u32[]{:S(2)}, u32[]{:S(2)}) %collective-permute-start.4) | collective-permute-done | bytes 131104 | tf_op jit(solution)/shard_map/ppermute | solution.py:531
  22.2 1.3 %collective-permute-start.5 = (f32[6,2,8,256]{3,2,1,0:T(8,128)S(1)}, f32[6,2,8,256]{3,2,1,0:T(8,128)S(1)}, u32[]{:S(2)}, u32[]{:S(2)}) collective-permute-start(f32[6,2,8,256]{3,2,1,0:T(8,128)S(1)} %shard_map.125), channel_id=1, source_target_pairs={{0,16},{2,18},{4,20},{6,22},{8,24},{10,26},{12,28},{14,30},{1,17},... | collective-permute-start | bytes 294920 | tf_op jit(solution)/shard_map/ppermute | solution.py:607
  23.5 7.3 %collective-permute-done.5.refs_6_ = f32[6,2,8,256]{3,2,1,0:T(8,128)S(1)} collective-permute-done((f32[6,2,8,256]{3,2,1,0:T(8,128)S(1)}, f32[6,2,8,256]{3,2,1,0:T(8,128)S(1)}, u32[]{:S(2)}, u32[]{:S(2)}) %collective-permute-start.5) | collective-permute-done | bytes 98336 | tf_op jit(solution)/shard_map/ppermute | solution.py:607
  30.8 0.2 shard_map.126
  31.0 1.4 %collective-permute-start.6 = (f32[6,2,8,256]{3,2,1,0:T(8,128)S(1)}, f32[6,2,8,256]{3,2,1,0:T(8,128)S(1)}, u32[]{:S(2)}, u32[]{:S(2)}) collective-permute-start(f32[6,2,8,256]{3,2,1,0:T(8,128)S(1)} %get-tuple-element.49), channel_id=1, source_target_pairs={{0,4},{2,6},{4,0},{6,2},{8,12},{10,14},{12,8},{14,10},{16,20},{18,... | collective-permute-start | bytes 294920 | tf_op jit(solution)/shard_map/ppermute | solution.py:531
  32.5 2.1 %collective-permute-start.8 = (f32[6,2,8,256]{3,2,1,0:T(8,128)S(1)}, f32[6,2,8,256]{3,2,1,0:T(8,128)S(1)}, u32[]{:S(2)}, u32[]{:S(2)}) collective-permute-start(f32[6,2,8,256]{3,2,1,0:T(8,128)S(1)} %get-tuple-element.51), channel_id=1, source_target_pairs={{0,12},{2,14},{4,8},{6,10},{8,4},{10,6},{12,0},{14,2},{16,28},{18,... | collective-permute-start | bytes 294920 | tf_op jit(solution)/shard_map/ppermute | solution.py:531
  34.6 1.9 %collective-permute-start.10 = (f32[3,4,4,8,256]{4,3,2,1,0:T(8,128)S(1)}, f32[3,4,4,8,256]{4,3,2,1,0:T(8,128)S(1)}, u32[]{:S(2)}, u32[]{:S(2)}) collective-permute-start(f32[3,4,4,8,256]{4,3,2,1,0:T(8,128)S(1)} %get-tuple-element.56), channel_id=1, source_target_pairs={{0,2},{2,4},{4,6},{6,8},{8,10},{10,12},{12,14},{14,16},{16,18},{18... | collective-permute-start | bytes 1179656 | tf_op jit(solution)/shard_map/ppermute | solution.py:597
  36.5 0.3 collective-permute-done.6.refs_1_
  36.7 0.3 collective-permute-done.7.refs_2_
  37.1 1.2 %collective-permute-done.8.refs_3_ = f32[6,2,8,256]{3,2,1,0:T(8,128)S(1)} collective-permute-done((f32[6,2,8,256]{3,2,1,0:T(8,128)S(1)}, f32[6,2,8,256]{3,2,1,0:T(8,128)S(1)}, u32[]{:S(2)}, u32[]{:S(2)}) %collective-permute-start.8) | collective-permute-done | bytes 98336 | tf_op jit(solution)/shard_map/ppermute | solution.py:531
  38.5 6.0 %collective-permute-done.10.visc_ref = f32[3,4,4,8,256]{4,3,2,1,0:T(8,128)S(1)} collective-permute-done((f32[3,4,4,8,256]{4,3,2,1,0:T(8,128)S(1)}, f32[3,4,4,8,256]{4,3,2,1,0:T(8,128)S(1)}, u32[]{:S(2)}, u32[]{:S(2)}) %collective-permute-start.10) | collective-permute-done | bytes 393248 | tf_op jit(solution)/shard_map/ppermute | solution.py:597
  44.5 0.8 %shard_map.129 = f32[1,3,4,32,256]{4,3,2,1,0:T(8,128)} custom-call(f32[3,4,4,8,256]{4,3,2,1,0:T(8,128)S(1)} %collective-permute-done.10.visc_ref, f32[3,3,4,32,256]{4,3,2,1,0:T(8,128)S(1)} %copy-done), custom_call_target="tpu_custom_call" | custom-call | tf_op jit(solution)/shard_map/pallas_call | solution.py:30
  45.3 0.9 %shard_map.128 = (f32[1,3,4,32,256]{4,3,2,1,0:T(8,128)}, f32[1,3,4,32,256]{4,3,2,1,0:T(8,128)}) custom-call(f32[6,8,8,256]{3,2,1,0:T(8,128)S(1)} %get-tuple-element.52.mine_ref, f32[6,8,8,256]{3,2,1,0:T(8,128)S(1)} %collective-permute-done.9.got_ref), custom_call_target="tpu_custom_call" | custom-call | tf_op jit(solution)/shard_map/pallas_call | solution.py:30
  (9 shorter events, 0.7 us)
Async XLA Ops:
  1.8 7.2 %collective-permute-start = (f32[27,8,256]{2,1,0:T(8,128)S(1)}, f32[27,8,256]{2,1,0:T(8,128)S(1)}, u32[]{:S(2)}, u32[]{:S(2)}) collective-permute-start(f32[27,8,256]{2,1,0:T(8,128)S(1)} %shard_map.121), channel_id=1, source_target_pairs={{0,1},{1,0},{2,3},{3,2},{4,5},{5,4},{6,7},{7,6},{8,9},{9,8},{10,11... | collective-permute-start | bytes 663560 | tf_op jit(solution)/shard_map/ppermute | solution.py:566
  10.3 11.6 %copy-start = (f32[3,3,4,32,256]{4,3,2,1,0:T(8,128)S(1)}, f32[3,3,4,32,256]{4,3,2,1,0:T(8,128)}, u32[]{:S(2)}) copy-start(f32[3,3,4,32,256]{4,3,2,1,0:T(8,128)} %init_ref.1) | copy-start | bytes 3538948
  10.3 1.9 %collective-permute-start.1 = (f32[7,8,8,256]{3,2,1,0:T(8,128)S(1)}, f32[7,8,8,256]{3,2,1,0:T(8,128)S(1)}, u32[]{:S(2)}, u32[]{:S(2)}) collective-permute-start(f32[7,8,8,256]{3,2,1,0:T(8,128)S(1)} %get-tuple-element.43), channel_id=1, source_target_pairs={{0,2},{2,0},{4,6},{6,4},{8,10},{10,8},{12,14},{14,12},{16,18},{18,... | collective-permute-start | bytes 1376264 | tf_op jit(solution)/shard_map/ppermute | solution.py:524
  12.4 5.6 %collective-permute-start.2 = (f32[8,2,8,256]{3,2,1,0:T(8,128)S(1)}, f32[8,2,8,256]{3,2,1,0:T(8,128)S(1)}, u32[]{:S(2)}, u32[]{:S(2)}) collective-permute-start(f32[8,2,8,256]{3,2,1,0:T(8,128)S(1)} %get-tuple-element.45), channel_id=1, source_target_pairs={{0,4},{2,6},{4,0},{6,2},{8,12},{10,14},{12,8},{14,10},{16,20},{18,... | collective-permute-start | bytes 393224 | tf_op jit(solution)/shard_map/ppermute | solution.py:531
  13.9 6.4 %collective-permute-start.3 = (f32[8,2,8,256]{3,2,1,0:T(8,128)S(1)}, f32[8,2,8,256]{3,2,1,0:T(8,128)S(1)}, u32[]{:S(2)}, u32[]{:S(2)}) collective-permute-start(f32[8,2,8,256]{3,2,1,0:T(8,128)S(1)} %get-tuple-element.46), channel_id=1, source_target_pairs={{0,8},{2,10},{4,12},{6,14},{8,0},{10,2},{12,4},{14,6},{16,24},{18,... | collective-permute-start | bytes 393224 | tf_op jit(solution)/shard_map/ppermute | solution.py:531
  14.4 7.6 %collective-permute-start.4 = (f32[8,2,8,256]{3,2,1,0:T(8,128)S(1)}, f32[8,2,8,256]{3,2,1,0:T(8,128)S(1)}, u32[]{:S(2)}, u32[]{:S(2)}) collective-permute-start(f32[8,2,8,256]{3,2,1,0:T(8,128)S(1)} %get-tuple-element.47), channel_id=1, source_target_pairs={{0,12},{2,14},{4,8},{6,10},{8,4},{10,6},{12,0},{14,2},{16,28},{18,... | collective-permute-start | bytes 393224 | tf_op jit(solution)/shard_map/ppermute | solution.py:531
  22.2 8.6 %collective-permute-start.5 = (f32[6,2,8,256]{3,2,1,0:T(8,128)S(1)}, f32[6,2,8,256]{3,2,1,0:T(8,128)S(1)}, u32[]{:S(2)}, u32[]{:S(2)}) collective-permute-start(f32[6,2,8,256]{3,2,1,0:T(8,128)S(1)} %shard_map.125), channel_id=1, source_target_pairs={{0,16},{2,18},{4,20},{6,22},{8,24},{10,26},{12,28},{14,30},{1,17},... | collective-permute-start | bytes 294920 | tf_op jit(solution)/shard_map/ppermute | solution.py:607
  31.0 5.7 %collective-permute-start.6 = (f32[6,2,8,256]{3,2,1,0:T(8,128)S(1)}, f32[6,2,8,256]{3,2,1,0:T(8,128)S(1)}, u32[]{:S(2)}, u32[]{:S(2)}) collective-permute-start(f32[6,2,8,256]{3,2,1,0:T(8,128)S(1)} %get-tuple-element.49), channel_id=1, source_target_pairs={{0,4},{2,6},{4,0},{6,2},{8,12},{10,14},{12,8},{14,10},{16,20},{18,... | collective-permute-start | bytes 294920 | tf_op jit(solution)/shard_map/ppermute | solution.py:531
  32.5 4.6 %collective-permute-start.7 = (f32[6,2,8,256]{3,2,1,0:T(8,128)S(1)}, f32[6,2,8,256]{3,2,1,0:T(8,128)S(1)}, u32[]{:S(2)}, u32[]{:S(2)}) collective-permute-start(f32[6,2,8,256]{3,2,1,0:T(8,128)S(1)} %get-tuple-element.50), channel_id=1, source_target_pairs={{0,8},{2,10},{4,12},{6,14},{8,0},{10,2},{12,4},{14,6},{16,24},{18,... | collective-permute-start | bytes 294920 | tf_op jit(solution)/shard_map/ppermute | solution.py:531
  32.5 5.8 %collective-permute-start.8 = (f32[6,2,8,256]{3,2,1,0:T(8,128)S(1)}, f32[6,2,8,256]{3,2,1,0:T(8,128)S(1)}, u32[]{:S(2)}, u32[]{:S(2)}) collective-permute-start(f32[6,2,8,256]{3,2,1,0:T(8,128)S(1)} %get-tuple-element.51), channel_id=1, source_target_pairs={{0,12},{2,14},{4,8},{6,10},{8,4},{10,6},{12,0},{14,2},{16,28},{18,... | collective-permute-start | bytes 294920 | tf_op jit(solution)/shard_map/ppermute | solution.py:531
  34.6 10.0 %collective-permute-start.10 = (f32[3,4,4,8,256]{4,3,2,1,0:T(8,128)S(1)}, f32[3,4,4,8,256]{4,3,2,1,0:T(8,128)S(1)}, u32[]{:S(2)}, u32[]{:S(2)}) collective-permute-start(f32[3,4,4,8,256]{4,3,2,1,0:T(8,128)S(1)} %get-tuple-element.56), channel_id=1, source_target_pairs={{0,2},{2,4},{4,6},{6,8},{8,10},{10,12},{12,14},{14,16},{16,18},{18... | collective-permute-start | bytes 1179656 | tf_op jit(solution)/shard_map/ppermute | solution.py:597
  38.4 6.9 %collective-permute-start.9 = (f32[6,8,8,256]{3,2,1,0:T(8,128)S(1)}, f32[6,8,8,256]{3,2,1,0:T(8,128)S(1)}, u32[]{:S(2)}, u32[]{:S(2)}) collective-permute-start(f32[6,8,8,256]{3,2,1,0:T(8,128)S(1)} %get-tuple-element.53), channel_id=1, source_target_pairs={{0,2},{2,0},{4,6},{6,4},{8,10},{10,8},{12,14},{14,12},{16,18},{18,... | collective-permute-start | bytes 1179656 | tf_op jit(solution)/shard_map/ppermute | solution.py:524

commit v3 on v2

--- a/solution.py
+++ b/solution.py
@@ -23,7 +23,7 @@
 VMEM_LIMIT = 24 * 1024 * 1024
 
 
-def call(kernel, out_shape, operands, scratch=(), in_hbm=(), aliases={}):
+def call(kernel, out_shape, operands, scratch=(), in_hbm=(), out_hbm=False, aliases={}):
     specs = []
     for k in range(len(operands)):
         specs.append(pl.BlockSpec(memory_space=pltpu.HBM if k in in_hbm else pltpu.VMEM))
@@ -31,7 +31,7 @@
         kernel,
         out_shape=out_shape,
         in_specs=specs,
-        out_specs=jax.tree.map(lambda _: pl.BlockSpec(memory_space=pltpu.VMEM), out_shape),
+        out_specs=jax.tree.map(lambda _: pl.BlockSpec(memory_space=pltpu.HBM if out_hbm else pltpu.VMEM), out_shape),
         scratch_shapes=list(scratch),
         compiler_params=pltpu.CompilerParams(vmem_limit_bytes=VMEM_LIMIT),
         input_output_aliases=aliases,
@@ -498,25 +498,39 @@
         store(slice(8 * tile, 8 * tile + 8), jnp.where(low_rows(cols), rows[tile], rows[(tile + 1) % tiles]))
 
 
-def join_kernel(cut, mine_ref, got_ref, disp_ref, vel_ref):
+def join_kernel(cut, other, *refs):
+    part_ref, (disp_ref, vel_ref, block, sem) = refs[0], refs[-4:]
     core = lax.rem(lax.axis_index("tm"), CORES)
+    place = 1 - core if other else core
+    copies = []
     for k in range(6):
         for layer in range(cut.half):
-            for source, own in ((mine_ref, core), (got_ref, 1 - core)):
-                def store(rows, value):
-                    (disp_ref, vel_ref)[k // 3][0, k % 3, own * cut.half + layer, rows, :] = value
-
-                unroll(lambda tile: source[k, layer * cut.tiles + tile], store, cut.tiles, cut.cols)
-
-
-def visc_kernel(cut, visc_ref, init_ref, out_ref):
+            def store(rows, value):
+                block[k, layer, rows, :] = value
+
+            unroll(lambda tile: part_ref[k, layer * cut.tiles + tile], store, cut.tiles, cut.cols)
+        target = (disp_ref, vel_ref)[k // 3].at[0, k % 3, pl.ds(place * cut.half, cut.half)]
+        copies.append(pltpu.make_async_copy(block.at[k], target, sem.at[k]))
+        copies[-1].start()
+    for copy in copies:
+        copy.wait()
+
+
+def last_kernel(cut, other, part_ref, visc_ref, init_ref, *refs):
+    disp_ref, vel_ref, out_ref, visc_s, block, sem, visc_sem = refs[-7:]
     first_slab = lax.axis_index("tm") == 0
+    copies = []
     for comp in range(3):
         for layer in range(visc_ref.shape[1]):
             def store(rows, value):
-                out_ref[0, comp, layer, rows, :] = jnp.where(first_slab, init_ref[2, comp, layer, rows, :], value)
+                visc_s[comp, layer, rows, :] = jnp.where(first_slab, init_ref[2, comp, layer, rows, :], value)
 
             unroll(lambda tile: visc_ref[comp, layer, tile], store, cut.tiles, cut.cols)
+        copies.append(pltpu.make_async_copy(visc_s.at[comp], out_ref.at[0, comp], visc_sem.at[comp]))
+        copies[-1].start()
+    join_kernel(cut, other, part_ref, disp_ref, vel_ref, block, sem)
+    for copy in copies:
+        copy.wait()
 
 
 def swap_cores(value):
@@ -604,7 +618,7 @@
     edge = call(
         functools.partial(lower_kernel, cut), shape(6, cut.size, 8, cols), (*parts, static, init_state), [maps]
     )
-    hop = lax.ppermute(edge, "tm", [(i, i + slabs // 2) for i in range(slabs // 2)])
+    hop = lax.ppermute(edge, "tm", [(i, i ^ (slabs // 2)) for i in range(slabs)])
     states = call(
         functools.partial(upper_kernel, cut),
         [shape(6, cut.size, 8, cols)] * group,
@@ -616,9 +630,14 @@
         functools.partial(spread_kernel, cut), [shape(6, cut.count, 8, cols)] * 2, (*states, keep, got, static)
     )
     other = swap_cores(other)
-    field = shape(1, 3, layers, rows, cols)
-    new_disp, new_vel = call(functools.partial(join_kernel, cut), [field, field], (mine, other))
-    new_visc = call(functools.partial(visc_kernel, cut), field, (visc, init_state))
+    field = pltpu.HBM((1, 3, layers, rows, cols), F32)
+    scratch = [pltpu.VMEM((6, half, rows, cols), F32), pltpu.SemaphoreType.DMA((6,))]
+    joined = call(functools.partial(join_kernel, cut, False), [field, field], (mine,), scratch, out_hbm=True)
+    new_disp, new_vel, new_visc = call(
+        functools.partial(last_kernel, cut, True), [field] * 3, (other, visc, init_state, *joined),
+        [pltpu.VMEM((3, layers, rows, cols), F32)] + scratch + [pltpu.SemaphoreType.DMA((3,))],
+        in_hbm=(3, 4), out_hbm=True, aliases={3: 0, 4: 1},
+    )
     return new_disp, new_vel, new_visc
 
 

time: 46.6 us -> 43.9 us (0.942)
  waiting for transfers between devices: 23.3 us -> 21.6 us
  starting transfers between devices: 12 us -> 11.1 us
    ppermute x1, waiting for transfers between devices: 7.28 us -> 6.35 us  [shards(): hop = lax.ppermute(edge, 'tm', [(i, i ^ slabs // 2) for i in range(slabs)])]
    ppermute x1, starting transfers between devices: 1.29 us -> 0.4 us  [shards(): hop = lax.ppermute(edge, 'tm', [(i, i ^ slabs // 2) for i in range(slabs)])]
    ppermute x1, waiting for transfers between devices: 6.03 us -> 5.22 us  [shards(): visc = lax.ppermute(end_visc, 'tm', [(i, i + 1) for i in range(slabs - 1)])]
  transfers between devices with their start and end apart: 11 -> 11, of which waited for: 10 -> 10; matrix products, arithmetic and copies ran while one was open for 0% -> 0% of each run, Pallas kernels for 13% -> 14%
where the time goes in v3:
time: 43.9 us; the launch traced here: 43.7 us
  waiting for transfers between devices  21.6 us (49%)
  starting transfers between devices  11.1 us (25%)
  Pallas kernels  10.2 us (23%)
  between operations  0.73 us (2%)
    pallas_call x9, Pallas kernels, call(): pl.pallas_call(kernel, out_shape=out_shape, in_specs=specs, out_specs=jax...  10.2 us
    ppermute x6, waiting for transfers between devices, transpose_parts(): lax.ppermute(parts[m], 'tm', [(i, i ^ CORES * m) for i in range(count)])  7.79 us
    ppermute x6, starting transfers between devices, transpose_parts(): lax.ppermute(parts[m], 'tm', [(i, i ^ CORES * m) for i in range(count)])  7.11 us
    ppermute x1, waiting for transfers between devices, shards(): hop = lax.ppermute(edge, 'tm', [(i, i ^ slabs // 2) for i in range(slabs)])  6.35 us
    ppermute x1, waiting for transfers between devices, shards(): visc = lax.ppermute(end_visc, 'tm', [(i, i + 1) for i in range(slabs - 1)])  5.22 us
    ppermute x1, starting transfers between devices, shards(): visc = lax.ppermute(end_visc, 'tm', [(i, i + 1) for i in range(slabs - 1)])  1.91 us
    ppermute x2, waiting for transfers between devices, swap_cores(): return lax.ppermute(value, 'tm', [(i, i ^ 1) for i in range(count)])  1.81 us
    ppermute x1, starting transfers between devices, shards(): after = before = lax.ppermute(packs[0], 'space', [(0, 1), (1, 0)])  1.58 us
  transfers between devices with their start and end apart: 11, of which 10 were waited for; matrix products, arithmetic and copies ran while one was open for 0% of the time, Pallas kernels for 14%

profile of v3, /device:TPU:24, one launch (start us, length us, event | category | flops | bytes accessed | tf_op | source)
XLA Modules:
  0.0 43.7 jit_solution(2714029963063284567)
XLA Ops:
  0.6 1.1 %shard_map.121 = f32[27,8,256]{2,1,0:T(8,128)S(1)} custom-call(f32[1,3,4,32,256]{4,3,2,1,0:T(8,128)} %refs_0_.3, f32[1,3,4,32,256]{4,3,2,1,0:T(8,128)} %refs_1_.3, f32[1,3,4,32,256]{4,3,2,1,0:T(8,128)} %refs_2_.3, f32[4,32,256]{2,1,0:T(8,128)} %refs_3_.3, f32[4,32,256]{2,1,0:T(8,128)} %refs_4_.3, f32[4,32,256]{2,1,0:T(8,128)} %refs_5_.5, ...), custom_call_target="tpu_custom_call" | custom-call | tf_op jit(solution)/shard_map/pallas_call | solution.py:30
  1.8 1.6 %collective-permute-start = (f32[27,8,256]{2,1,0:T(8,128)S(1)}, f32[27,8,256]{2,1,0:T(8,128)S(1)}, u32[]{:S(2)}, u32[]{:S(2)}) collective-permute-start(f32[27,8,256]{2,1,0:T(8,128)S(1)} %shard_map.121), channel_id=1, source_target_pairs={{0,1},{1,0},{2,3},{3,2},{4,5},{5,4},{6,7},{7,6},{8,9},{9,8},{10,11... | collective-permute-start | bytes 663560 | tf_op jit(solution)/shard_map/ppermute | solution.py:580
  3.3 5.2 %shard_map.122 = (f32[7,8,8,256]{3,2,1,0:T(8,128)S(1)}, f32[7,8,8,256]{3,2,1,0:T(8,128)S(1)}, f32[3,4,4,8,256]{4,3,2,1,0:T(8,128)S(1)}, f32[5,3,4,4,8,256]{5,4,3...) custom-call(f32[1,3,4,32,256]{4,3,2,1,0:T(8,128)} %refs_0_.3, ...), custom_call_target="tpu_custom_call" | custom-call | tf_op jit(solution)/shard_map/pallas_call | solution.py:30
  8.6 0.4 collective-permute-done.refs_0_.refs_1_
  9.0 1.3 %shard_map.123 = (f32[7,8,8,256]{3,2,1,0:T(8,128)S(1)}, f32[7,8,8,256]{3,2,1,0:T(8,128)S(1)}, f32[3,4,4,8,256]{4,3,2,1,0:T(8,128)S(1)}) custom-call(f32[27,8,256]{2,1,0:T(8,128)S(1)} %collective-permute-done.refs_0_.refs_1_, f32[27,8,256]{2,1,0:T(8,128)S(1)} %collective-permute-done.refs_0_.refs_1_, ...), custom_call_target="tpu_custom_call", output_to_operand_aliasing={{0}: (10, {}), {1}: (11, {}), {2}: (12, {})} | custom-call | tf_op jit(solution)/shard_map/pallas_call | solution.py:30
  10.4 1.8 %collective-permute-done.1.got_ref.refs_5_ = f32[7,8,8,256]{3,2,1,0:T(8,128)S(1)} collective-permute-done((f32[7,8,8,256]{3,2,1,0:T(8,128)S(1)}, f32[7,8,8,256]{3,2,1,0:T(8,128)S(1)}, u32[]{:S(2)}, u32[]{:S(2)}) %collective-permute-start.1) | collective-permute-done | bytes 458784 | tf_op jit(solution)/shard_map/ppermute | solution.py:538
  12.4 1.6 %collective-permute-start.2 = (f32[8,2,8,256]{3,2,1,0:T(8,128)S(1)}, f32[8,2,8,256]{3,2,1,0:T(8,128)S(1)}, u32[]{:S(2)}, u32[]{:S(2)}) collective-permute-start(f32[8,2,8,256]{3,2,1,0:T(8,128)S(1)} %get-tuple-element.45), channel_id=1, source_target_pairs={{0,4},{2,6},{4,0},{6,2},{8,12},{10,14},{12,8},{14,10},{16,20},{18,... | collective-permute-start | bytes 393224 | tf_op jit(solution)/shard_map/ppermute | solution.py:545
  13.9 0.4 %collective-permute-start.3 = (f32[8,2,8,256]{3,2,1,0:T(8,128)S(1)}, f32[8,2,8,256]{3,2,1,0:T(8,128)S(1)}, u32[]{:S(2)}, u32[]{:S(2)}) collective-permute-start(f32[8,2,8,256]{3,2,1,0:T(8,128)S(1)} %get-tuple-element.46), channel_id=1, source_target_pairs={{0,8},{2,10},{4,12},{6,14},{8,0},{10,2},{12,4},{14,6},{16,24},{18,... | collective-permute-start | bytes 393224 | tf_op jit(solution)/shard_map/ppermute | solution.py:545
  14.4 1.5 %collective-permute-start.4 = (f32[8,2,8,256]{3,2,1,0:T(8,128)S(1)}, f32[8,2,8,256]{3,2,1,0:T(8,128)S(1)}, u32[]{:S(2)}, u32[]{:S(2)}) collective-permute-start(f32[8,2,8,256]{3,2,1,0:T(8,128)S(1)} %get-tuple-element.47), channel_id=1, source_target_pairs={{0,12},{2,14},{4,8},{6,10},{8,4},{10,6},{12,0},{14,2},{16,28},{18,... | collective-permute-start | bytes 393224 | tf_op jit(solution)/shard_map/ppermute | solution.py:545
  15.9 2.0 %collective-permute-done.2.refs_1_ = f32[8,2,8,256]{3,2,1,0:T(8,128)S(1)} collective-permute-done((f32[8,2,8,256]{3,2,1,0:T(8,128)S(1)}, f32[8,2,8,256]{3,2,1,0:T(8,128)S(1)}, u32[]{:S(2)}, u32[]{:S(2)}) %collective-permute-start.2) | collective-permute-done | bytes 131104 | tf_op jit(solution)/shard_map/ppermute | solution.py:545
  18.0 2.3 %collective-permute-done.3.refs_2_ = f32[8,2,8,256]{3,2,1,0:T(8,128)S(1)} collective-permute-done((f32[8,2,8,256]{3,2,1,0:T(8,128)S(1)}, f32[8,2,8,256]{3,2,1,0:T(8,128)S(1)}, u32[]{:S(2)}, u32[]{:S(2)}) %collective-permute-start.3) | collective-permute-done | bytes 131104 | tf_op jit(solution)/shard_map/ppermute | solution.py:545
  20.3 1.7 %collective-permute-done.4.refs_3_ = f32[8,2,8,256]{3,2,1,0:T(8,128)S(1)} collective-permute-done((f32[8,2,8,256]{3,2,1,0:T(8,128)S(1)}, f32[8,2,8,256]{3,2,1,0:T(8,128)S(1)}, u32[]{:S(2)}, u32[]{:S(2)}) %collective-permute-start.4) | collective-permute-done | bytes 131104 | tf_op jit(solution)/shard_map/ppermute | solution.py:545
  22.2 0.4 collective-permute-start.5
  22.6 6.4 %collective-permute-done.5.refs_6_ = f32[6,2,8,256]{3,2,1,0:T(8,128)S(1)} collective-permute-done((f32[6,2,8,256]{3,2,1,0:T(8,128)S(1)}, f32[6,2,8,256]{3,2,1,0:T(8,128)S(1)}, u32[]{:S(2)}, u32[]{:S(2)}) %collective-permute-start.5) | collective-permute-done | bytes 98336 | tf_op jit(solution)/shard_map/ppermute | solution.py:621
  28.9 0.2 shard_map.126
  29.2 1.4 %collective-permute-start.6 = (f32[6,2,8,256]{3,2,1,0:T(8,128)S(1)}, f32[6,2,8,256]{3,2,1,0:T(8,128)S(1)}, u32[]{:S(2)}, u32[]{:S(2)}) collective-permute-start(f32[6,2,8,256]{3,2,1,0:T(8,128)S(1)} %get-tuple-element.49), channel_id=1, source_target_pairs={{0,4},{2,6},{4,0},{6,2},{8,12},{10,14},{12,8},{14,10},{16,20},{18,... | collective-permute-start | bytes 294920 | tf_op jit(solution)/shard_map/ppermute | solution.py:545
  30.6 2.1 %collective-permute-start.8 = (f32[6,2,8,256]{3,2,1,0:T(8,128)S(1)}, f32[6,2,8,256]{3,2,1,0:T(8,128)S(1)}, u32[]{:S(2)}, u32[]{:S(2)}) collective-permute-start(f32[6,2,8,256]{3,2,1,0:T(8,128)S(1)} %get-tuple-element.51), channel_id=1, source_target_pairs={{0,12},{2,14},{4,8},{6,10},{8,4},{10,6},{12,0},{14,2},{16,28},{18,... | collective-permute-start | bytes 294920 | tf_op jit(solution)/shard_map/ppermute | solution.py:545
  32.7 1.9 %collective-permute-start.10 = (f32[3,4,4,8,256]{4,3,2,1,0:T(8,128)S(1)}, f32[3,4,4,8,256]{4,3,2,1,0:T(8,128)S(1)}, u32[]{:S(2)}, u32[]{:S(2)}) collective-permute-start(f32[3,4,4,8,256]{4,3,2,1,0:T(8,128)S(1)} %get-tuple-element.53), channel_id=1, source_target_pairs={{0,2},{2,4},{4,6},{6,8},{8,10},{10,12},{12,14},{14,16},{16,18},{18... | collective-permute-start | bytes 1179656 | tf_op jit(solution)/shard_map/ppermute | solution.py:611
  34.7 0.3 collective-permute-done.6.refs_1_
  34.9 0.3 collective-permute-done.7.refs_2_
  35.2 1.2 %collective-permute-done.8.refs_3_ = f32[6,2,8,256]{3,2,1,0:T(8,128)S(1)} collective-permute-done((f32[6,2,8,256]{3,2,1,0:T(8,128)S(1)}, f32[6,2,8,256]{3,2,1,0:T(8,128)S(1)}, u32[]{:S(2)}, u32[]{:S(2)}) %collective-permute-start.8) | collective-permute-done | bytes 98336 | tf_op jit(solution)/shard_map/ppermute | solution.py:545
  36.7 0.8 %shard_map.128 = (f32[1,3,4,32,256]{4,3,2,1,0:T(8,128)}, f32[1,3,4,32,256]{4,3,2,1,0:T(8,128)}) custom-call(f32[6,8,8,256]{3,2,1,0:T(8,128)S(1)} %get-tuple-element.54.refs_0_), custom_call_target="tpu_custom_call" | custom-call | tf_op jit(solution)/shard_map/pallas_call | solution.py:30
  37.5 5.2 %collective-permute-done.10.visc_ref = f32[3,4,4,8,256]{4,3,2,1,0:T(8,128)S(1)} collective-permute-done((f32[3,4,4,8,256]{4,3,2,1,0:T(8,128)S(1)}, f32[3,4,4,8,256]{4,3,2,1,0:T(8,128)S(1)}, u32[]{:S(2)}, u32[]{:S(2)}) %collective-permute-start.10) | collective-permute-done | bytes 393248 | tf_op jit(solution)/shard_map/ppermute | solution.py:611
  42.7 1.0 %shard_map.129 = (f32[1,3,4,32,256]{4,3,2,1,0:T(8,128)}, f32[1,3,4,32,256]{4,3,2,1,0:T(8,128)}, f32[1,3,4,32,256]{4,3,2,1,0:T(8,128)}) custom-call(f32[6,8,8,256]{3,2,1,0:T(8,128)S(1)} %collective-permute-done.9.part_ref, f32[3,4,4,8,256]{4,3,2,1,0:T(8,128)S(1)} %collective-permute-done.10.visc_ref, ...), custom_call_target="tpu_custom_call", output_to_operand_aliasing={{0}: (3, {}), {1}: (4, {})} | custom-call | tf_op jit(solution)/shard_map/pallas_call | solution.py:30
  (9 shorter events, 0.7 us)
Async XLA Ops:
  1.8 7.2 %collective-permute-start = (f32[27,8,256]{2,1,0:T(8,128)S(1)}, f32[27,8,256]{2,1,0:T(8,128)S(1)}, u32[]{:S(2)}, u32[]{:S(2)}) collective-permute-start(f32[27,8,256]{2,1,0:T(8,128)S(1)} %shard_map.121), channel_id=1, source_target_pairs={{0,1},{1,0},{2,3},{3,2},{4,5},{5,4},{6,7},{7,6},{8,9},{9,8},{10,11... | collective-permute-start | bytes 663560 | tf_op jit(solution)/shard_map/ppermute | solution.py:580
  10.3 11.6 %copy-start = (f32[3,3,4,32,256]{4,3,2,1,0:T(8,128)S(1)}, f32[3,3,4,32,256]{4,3,2,1,0:T(8,128)}, u32[]{:S(2)}) copy-start(f32[3,3,4,32,256]{4,3,2,1,0:T(8,128)} %init_ref.1) | copy-start | bytes 3538948
  10.3 1.9 %collective-permute-start.1 = (f32[7,8,8,256]{3,2,1,0:T(8,128)S(1)}, f32[7,8,8,256]{3,2,1,0:T(8,128)S(1)}, u32[]{:S(2)}, u32[]{:S(2)}) collective-permute-start(f32[7,8,8,256]{3,2,1,0:T(8,128)S(1)} %get-tuple-element.43), channel_id=1, source_target_pairs={{0,2},{2,0},{4,6},{6,4},{8,10},{10,8},{12,14},{14,12},{16,18},{18,... | collective-permute-start | bytes 1376264 | tf_op jit(solution)/shard_map/ppermute | solution.py:538
  12.4 5.6 %collective-permute-start.2 = (f32[8,2,8,256]{3,2,1,0:T(8,128)S(1)}, f32[8,2,8,256]{3,2,1,0:T(8,128)S(1)}, u32[]{:S(2)}, u32[]{:S(2)}) collective-permute-start(f32[8,2,8,256]{3,2,1,0:T(8,128)S(1)} %get-tuple-element.45), channel_id=1, source_target_pairs={{0,4},{2,6},{4,0},{6,2},{8,12},{10,14},{12,8},{14,10},{16,20},{18,... | collective-permute-start | bytes 393224 | tf_op jit(solution)/shard_map/ppermute | solution.py:545
  13.9 6.4 %collective-permute-start.3 = (f32[8,2,8,256]{3,2,1,0:T(8,128)S(1)}, f32[8,2,8,256]{3,2,1,0:T(8,128)S(1)}, u32[]{:S(2)}, u32[]{:S(2)}) collective-permute-start(f32[8,2,8,256]{3,2,1,0:T(8,128)S(1)} %get-tuple-element.46), channel_id=1, source_target_pairs={{0,8},{2,10},{4,12},{6,14},{8,0},{10,2},{12,4},{14,6},{16,24},{18,... | collective-permute-start | bytes 393224 | tf_op jit(solution)/shard_map/ppermute | solution.py:545
  14.4 7.6 %collective-permute-start.4 = (f32[8,2,8,256]{3,2,1,0:T(8,128)S(1)}, f32[8,2,8,256]{3,2,1,0:T(8,128)S(1)}, u32[]{:S(2)}, u32[]{:S(2)}) collective-permute-start(f32[8,2,8,256]{3,2,1,0:T(8,128)S(1)} %get-tuple-element.47), channel_id=1, source_target_pairs={{0,12},{2,14},{4,8},{6,10},{8,4},{10,6},{12,0},{14,2},{16,28},{18,... | collective-permute-start | bytes 393224 | tf_op jit(solution)/shard_map/ppermute | solution.py:545
  22.2 6.8 %collective-permute-start.5 = (f32[6,2,8,256]{3,2,1,0:T(8,128)S(1)}, f32[6,2,8,256]{3,2,1,0:T(8,128)S(1)}, u32[]{:S(2)}, u32[]{:S(2)}) collective-permute-start(f32[6,2,8,256]{3,2,1,0:T(8,128)S(1)} %shard_map.125), channel_id=1, source_target_pairs={{0,16},{2,18},{4,20},{6,22},{8,24},{10,26},{12,28},{14,30},{16,0},... | collective-permute-start | bytes 294920 | tf_op jit(solution)/shard_map/ppermute | solution.py:621
  29.2 5.7 %collective-permute-start.6 = (f32[6,2,8,256]{3,2,1,0:T(8,128)S(1)}, f32[6,2,8,256]{3,2,1,0:T(8,128)S(1)}, u32[]{:S(2)}, u32[]{:S(2)}) collective-permute-start(f32[6,2,8,256]{3,2,1,0:T(8,128)S(1)} %get-tuple-element.49), channel_id=1, source_target_pairs={{0,4},{2,6},{4,0},{6,2},{8,12},{10,14},{12,8},{14,10},{16,20},{18,... | collective-permute-start | bytes 294920 | tf_op jit(solution)/shard_map/ppermute | solution.py:545
  30.6 4.6 %collective-permute-start.7 = (f32[6,2,8,256]{3,2,1,0:T(8,128)S(1)}, f32[6,2,8,256]{3,2,1,0:T(8,128)S(1)}, u32[]{:S(2)}, u32[]{:S(2)}) collective-permute-start(f32[6,2,8,256]{3,2,1,0:T(8,128)S(1)} %get-tuple-element.50), channel_id=1, source_target_pairs={{0,8},{2,10},{4,12},{6,14},{8,0},{10,2},{12,4},{14,6},{16,24},{18,... | collective-permute-start | bytes 294920 | tf_op jit(solution)/shard_map/ppermute | solution.py:545
  30.6 5.8 %collective-permute-start.8 = (f32[6,2,8,256]{3,2,1,0:T(8,128)S(1)}, f32[6,2,8,256]{3,2,1,0:T(8,128)S(1)}, u32[]{:S(2)}, u32[]{:S(2)}) collective-permute-start(f32[6,2,8,256]{3,2,1,0:T(8,128)S(1)} %get-tuple-element.51), channel_id=1, source_target_pairs={{0,12},{2,14},{4,8},{6,10},{8,4},{10,6},{12,0},{14,2},{16,28},{18,... | collective-permute-start | bytes 294920 | tf_op jit(solution)/shard_map/ppermute | solution.py:545
  32.7 10.0 %collective-permute-start.10 = (f32[3,4,4,8,256]{4,3,2,1,0:T(8,128)S(1)}, f32[3,4,4,8,256]{4,3,2,1,0:T(8,128)S(1)}, u32[]{:S(2)}, u32[]{:S(2)}) collective-permute-start(f32[3,4,4,8,256]{4,3,2,1,0:T(8,128)S(1)} %get-tuple-element.53), channel_id=1, source_target_pairs={{0,2},{2,4},{4,6},{6,8},{8,10},{10,12},{12,14},{14,16},{16,18},{18... | collective-permute-start | bytes 1179656 | tf_op jit(solution)/shard_map/ppermute | solution.py:611
  36.6 6.1 %collective-permute-start.9 = (f32[6,8,8,256]{3,2,1,0:T(8,128)S(1)}, f32[6,8,8,256]{3,2,1,0:T(8,128)S(1)}, u32[]{:S(2)}, u32[]{:S(2)}) collective-permute-start(f32[6,8,8,256]{3,2,1,0:T(8,128)S(1)} %get-tuple-element.52), channel_id=1, source_target_pairs={{0,2},{2,0},{4,6},{6,4},{8,10},{10,8},{12,14},{14,12},{16,18},{18,... | collective-permute-start | bytes 1179656 | tf_op jit(solution)/shard_map/ppermute | solution.py:538

commit v4 on v3

--- a/solution.py
+++ b/solution.py
@@ -53,6 +53,10 @@
 def rolled_tile(load, tile, tiles, cols):
     last = (tile + tiles - 1) % tiles if isinstance(tile, int) else lax.rem(tile + tiles - 1, tiles)
     return jnp.where(low_rows(cols), pltpu.roll(load(last), 4, 0), pltpu.roll(load(tile), 4, 0))
+
+
+def own_rows(first, second):
+    return jnp.where(low_rows(first.shape[1]), pltpu.roll(first, 4, 0), pltpu.roll(second, 4, 0))
 
 
 def direction_tile(family_ref, first, second, cols):
@@ -244,7 +248,7 @@
     lax.fori_loop(0, STEPS, step, 0)
 
 
-def put_maps(win, tiles, end, keep_ref, send_ref, end_visc_ref):
+def put_maps(win, tiles, end, keep_ref, send_ref):
     core = lax.rem(lax.axis_index("tm"), CORES)
     half = win.layers // CORES
     for layer in range(win.layers):
@@ -258,6 +262,7 @@
             for comp, (disp, vel) in enumerate(start):
                 pieces.append(end(lambda w: w.v.at[STEPS, comp], layer, tile) - (g[2] * disp + g[3] * vel))
             to = (layer % half) * win.tiles + tile
+            sent = (layer % half) * len(tiles) + tile - tiles[0]
 
             @pl.when(core == layer // half)
             def _():
@@ -267,10 +272,7 @@
             @pl.when(core != layer // half)
             def _():
                 for k, piece in enumerate(pieces):
-                    send_ref[k, to] = piece
-
-            for comp in range(3):
-                end_visc_ref[comp, layer, tile] = end(lambda w: w.q.at[STEPS, comp], layer, tile)
+                    send_ref[k, sent] = piece
 
 
 def inner_kernel(*refs):
@@ -320,15 +322,22 @@
         lambda s, comp, layer, tile: win.u[s, comp, layer, (tile + 1) % tiles],
         None,
     )
-    put_maps(win, range(1, tiles), lambda of, layer, tile: of(win)[layer, tile], *outs)
+    keep_ref, send_ref, visc_ref = outs
+    put_maps(win, range(1, tiles), lambda of, layer, tile: of(win)[layer, tile], keep_ref, send_ref)
+    for comp in range(3):
+        for layer in range(layers):
+            found = [win.q[STEPS, comp, layer, tile] for tile in range(1, tiles)]
+            for k in range(tiles - 2):
+                rows = slice(8 * k + 8, 8 * k + 16)
+                visc_ref[comp, layer, rows, :] = own_rows(found[k], found[k + 1])
 
 
 def outer_kernel(*refs):
     next_ref, prev_ref = refs[:2]
     inner = Window(refs[2:10])
-    facing_ref = refs[13]
-    outs = refs[14:17]
-    win = Window(refs[17:])
+    facing_ref = refs[12]
+    outs = refs[13:16]
+    win = Window(refs[16:])
     layers, cols = win.layers, win.cols
     place = lax.axis_index("space")
     has_next = place < lax.axis_size("space") - 1
@@ -369,7 +378,14 @@
     def end(of, layer, tile):
         return jnp.where(low, of(win)[layer, 0], of(win)[layer, 1])
 
-    put_maps(inner, [0], end, *outs)
+    keep_ref, send_ref, visc_ref = outs
+    put_maps(inner, [0], end, keep_ref, send_ref)
+    rows = visc_ref.shape[2]
+    for comp in range(3):
+        for layer in range(layers):
+            facing = end(lambda w: w.q.at[STEPS, comp], layer, 0)
+            visc_ref[comp, layer, 0:8, :] = own_rows(facing, inner.q[STEPS, comp, layer, 1])
+            visc_ref[comp, layer, rows - 8 : rows, :] = own_rows(inner.q[STEPS, comp, layer, last], facing)
 
 
 class Cut:
@@ -387,17 +403,23 @@
         return lax.rem(lax.axis_index("tm") // CORES, self.group)
 
 
+def sent_tile(facing_ref, rest_ref, cut, k, unit, tile):
+    layer = unit // cut.tiles
+    rest = rest_ref[k, layer * (cut.tiles - 1) + jnp.maximum(tile, 1) - 1]
+    return jnp.where(tile == 0, facing_ref[k, layer], rest)
+
+
 def part_coarse(static_ref, layer, tile, weight):
     return coarse(static_ref[MASS, layer, tile], static_ref[DAMP, layer, tile], static_ref[STIFF, layer, tile], weight)
 
 
-def compose_kernel(cut, keep_ref, got_ref, static_ref, *outs):
+def compose_kernel(cut, keep_ref, facing_ref, rest_ref, static_ref, *outs):
     first_core = lax.rem(lax.axis_index("tm"), CORES) == 0
     for m in range(cut.group):
         first, layer, tile = cut.of(jnp.bitwise_xor(cut.place(), m))
         for i in range(cut.size):
             keep = [keep_ref[k, first + i] for k in range(7)]
-            got = [got_ref[k, first + i] for k in range(7)]
+            got = [sent_tile(facing_ref, rest_ref, cut, k, first + i, tile + i) for k in range(7)]
             early = [jnp.where(first_core, a, b) for a, b in zip(keep, got)]
             late = [jnp.where(first_core, b, a) for a, b in zip(keep, got)]
             g = part_coarse(static_ref, layer, tile + i, late[0])
@@ -475,12 +497,13 @@
 
 def spread_kernel(cut, *refs):
     parts = refs[: cut.group]
-    keep_ref, got_ref, static_ref, mine_ref, send_ref = refs[cut.group :]
+    keep_ref, facing_ref, rest_ref, static_ref, mine_ref, send_ref = refs[cut.group :]
     first_core = lax.rem(lax.axis_index("tm"), CORES) == 0
     for m in range(cut.group):
         first, layer, tile = cut.of(jnp.bitwise_xor(cut.place(), m))
         for i in range(cut.size):
-            early = [jnp.where(first_core, keep_ref[k, first + i], got_ref[k, first + i]) for k in range(7)]
+            got = [sent_tile(facing_ref, rest_ref, cut, k, first + i, tile + i) for k in range(7)]
+            early = [jnp.where(first_core, keep_ref[k, first + i], got[k]) for k in range(7)]
             g = part_coarse(static_ref, layer, tile + i, early[0])
             for comp in range(3):
                 a, b = parts[m][comp, i], parts[m][3 + comp, i]
@@ -512,23 +535,6 @@
         target = (disp_ref, vel_ref)[k // 3].at[0, k % 3, pl.ds(place * cut.half, cut.half)]
         copies.append(pltpu.make_async_copy(block.at[k], target, sem.at[k]))
         copies[-1].start()
-    for copy in copies:
-        copy.wait()
-
-
-def last_kernel(cut, other, part_ref, visc_ref, init_ref, *refs):
-    disp_ref, vel_ref, out_ref, visc_s, block, sem, visc_sem = refs[-7:]
-    first_slab = lax.axis_index("tm") == 0
-    copies = []
-    for comp in range(3):
-        for layer in range(visc_ref.shape[1]):
-            def store(rows, value):
-                visc_s[comp, layer, rows, :] = jnp.where(first_slab, init_ref[2, comp, layer, rows, :], value)
-
-            unroll(lambda tile: visc_ref[comp, layer, tile], store, cut.tiles, cut.cols)
-        copies.append(pltpu.make_async_copy(visc_s.at[comp], out_ref.at[0, comp], visc_sem.at[comp]))
-        copies[-1].start()
-    join_kernel(cut, other, part_ref, disp_ref, vel_ref, block, sem)
     for copy in copies:
         copy.wait()
 
@@ -583,7 +589,8 @@
         after = lax.ppermute(packs[1], "space", [(i + 1, i) for i in range(spaces - 1)])
 
     map_shape = shape(7, cut.count, 8, cols)
-    outs = [map_shape, map_shape, shape(3, layers, tiles, 8, cols)]
+    visc_shape = shape(3, layers, rows, cols)
+    outs = [map_shape, shape(7, half * (tiles - 1), 8, cols), visc_shape]
     held = [shape(*dims) for dims in Window.shapes(layers, tiles, cols)]
     partial = call(
         inner_kernel,
@@ -598,20 +605,23 @@
         ],
         in_hbm=range(9),
     )
-    ends, held, facing = partial[:3], partial[3:11], partial[11]
+    (keep, rest, end_visc), held, facing = partial[:3], partial[3:11], partial[11]
+    before, rest = lax.optimization_barrier((before, rest))
+    after = before if spaces == 2 else after
+    rest = swap_cores(rest)
     keep, send, end_visc = call(
         outer_kernel,
-        outs,
-        (after, before, *held, *ends, facing),
+        [map_shape, shape(7, half, 8, cols), visc_shape],
+        (after, before, *held, keep, end_visc, facing),
         [pltpu.VMEM(dims, F32) for dims in Window.shapes(layers, 2, cols)],
-        aliases={10: 0, 11: 1, 12: 2},
+        aliases={10: 0, 11: 2},
     )
     static = held[5]
-    got = swap_cores(send)
+    got = (swap_cores(send), rest)
     visc = lax.ppermute(end_visc, "tm", [(i, i + 1) for i in range(slabs - 1)])
 
     parts = call(
-        functools.partial(compose_kernel, cut), [shape(8, cut.size, 8, cols)] * group, (keep, got, static)
+        functools.partial(compose_kernel, cut), [shape(8, cut.size, 8, cols)] * group, (keep, *got, static)
     )
     parts = transpose_parts(parts)
     maps = pltpu.VMEM((group, 8, cut.size, 8, cols), F32)
@@ -627,17 +637,17 @@
     )
     states = transpose_parts(states)
     mine, other = call(
-        functools.partial(spread_kernel, cut), [shape(6, cut.count, 8, cols)] * 2, (*states, keep, got, static)
+        functools.partial(spread_kernel, cut), [shape(6, cut.count, 8, cols)] * 2, (*states, keep, *got, static)
     )
     other = swap_cores(other)
     field = pltpu.HBM((1, 3, layers, rows, cols), F32)
     scratch = [pltpu.VMEM((6, half, rows, cols), F32), pltpu.SemaphoreType.DMA((6,))]
     joined = call(functools.partial(join_kernel, cut, False), [field, field], (mine,), scratch, out_hbm=True)
-    new_disp, new_vel, new_visc = call(
-        functools.partial(last_kernel, cut, True), [field] * 3, (other, visc, init_state, *joined),
-        [pltpu.VMEM((3, layers, rows, cols), F32)] + scratch + [pltpu.SemaphoreType.DMA((3,))],
-        in_hbm=(3, 4), out_hbm=True, aliases={3: 0, 4: 1},
-    )
+    new_disp, new_vel = call(
+        functools.partial(join_kernel, cut, True), [field, field], (other, *joined), scratch,
+        in_hbm=(1, 2), out_hbm=True, aliases={1: 0, 2: 1},
+    )
+    new_visc = jnp.where(lax.axis_index("tm") == 0, init_state[2], visc)[None]
     return new_disp, new_vel, new_visc
 
 

time: 43.9 us -> 41.8 us (0.952)
  the two profiles are of different devices: /device:TPU:24 before, /device:TPU:0 now
where the time goes in v4:
time: 41.8 us; the launch traced here: 41.6 us
  starting transfers between devices  15.6 us (37%)
  waiting for transfers between devices  14.3 us (34%)
  Pallas kernels  10.1 us (24%)
  other arithmetic  0.8 us (2%)
  between operations  0.74 us (2%)
    pallas_call x9, Pallas kernels, call(): pl.pallas_call(kernel, out_shape=out_shape, in_specs=specs, out_specs=jax...  10.1 us
    ppermute x6, waiting for transfers between devices, transpose_parts(): lax.ppermute(parts[m], 'tm', [(i, i ^ CORES * m) for i in range(count)])  8.98 us
    ppermute x6, starting transfers between devices, transpose_parts(): lax.ppermute(parts[m], 'tm', [(i, i ^ CORES * m) for i in range(count)])  7.12 us
    ppermute x1, waiting for transfers between devices, shards(): hop = lax.ppermute(edge, 'tm', [(i, i ^ slabs // 2) for i in range(slabs)])  4.08 us
    ppermute x1, starting transfers between devices, shards(): hop = lax.ppermute(edge, 'tm', [(i, i ^ slabs // 2) for i in range(slabs)])  3.3 us
    ppermute x1, starting transfers between devices, shards(): after = before = lax.ppermute(packs[0], 'space', [(0, 1), (1, 0)])  3.03 us
    ppermute x1, starting transfers between devices, shards(): visc = lax.ppermute(end_visc, 'tm', [(i, i + 1) for i in range(slabs - 1)])  1.5 us
    ppermute x3, waiting for transfers between devices, swap_cores(): return lax.ppermute(value, 'tm', [(i, i ^ 1) for i in range(count)])  1.05 us
  transfers between devices with their start and end apart: 12, of which 10 were waited for; matrix products, arithmetic and copies ran while one was open for 2% of the time, Pallas kernels for 19%

profile of v4, /device:TPU:0, one launch (start us, length us, event | category | flops | bytes accessed | tf_op | source)
XLA Modules:
  0.0 41.6 jit_solution(7221381495105535314)
XLA Ops:
  0.6 1.1 %shard_map.121 = f32[27,8,256]{2,1,0:T(8,128)S(1)} custom-call(f32[1,3,4,32,256]{4,3,2,1,0:T(8,128)} %refs_0_.3, f32[1,3,4,32,256]{4,3,2,1,0:T(8,128)} %refs_1_.3, f32[1,3,4,32,256]{4,3,2,1,0:T(8,128)} %refs_2_.3, f32[4,32,256]{2,1,0:T(8,128)} %refs_3_.3, f32[4,32,256]{2,1,0:T(8,128)} %refs_4_.3, f32[4,32,256]{2,1,0:T(8,128)} %refs_5_.5, ...), custom_call_target="tpu_custom_call" | custom-call | tf_op jit(solution)/shard_map/pallas_call | solution.py:30
  1.8 3.0 %collective-permute-start = (f32[27,8,256]{2,1,0:T(8,128)S(1)}, f32[27,8,256]{2,1,0:T(8,128)S(1)}, u32[]{:S(2)}, u32[]{:S(2)}) collective-permute-start(f32[27,8,256]{2,1,0:T(8,128)S(1)} %shard_map.121), channel_id=1, source_target_pairs={{0,1},{1,0},{2,3},{3,2},{4,5},{5,4},{6,7},{7,6},{8,9},{9,8},{10,11... | collective-permute-start | bytes 663560 | tf_op jit(solution)/shard_map/ppermute | solution.py:586
  4.8 5.2 %shard_map.122 = (f32[7,8,8,256]{3,2,1,0:T(8,128)S(1)}, f32[7,6,8,256]{3,2,1,0:T(8,128)S(1)}, f32[3,4,32,256]{3,2,1,0:T(8,128)S(1)}, f32[5,3,4,4,8,256]{5,4,3,2,...) custom-call(f32[1,3,4,32,256]{4,3,2,1,0:T(8,128)} %refs_0_.3, ...), custom_call_target="tpu_custom_call" | custom-call | tf_op jit(solution)/shard_map/pallas_call | solution.py:30
  10.2 1.3 %shard_map.123 = (f32[7,8,8,256]{3,2,1,0:T(8,128)S(1)}, f32[7,2,8,256]{3,2,1,0:T(8,128)S(1)}, f32[3,4,32,256]{3,2,1,0:T(8,128)S(1)}) custom-call(f32[27,8,256]{2,1,0:T(8,128)S(1)} %collective-permute-done.refs_0_.refs_1_, f32[27,8,256]{2,1,0:T(8,128)S(1)} %collective-permute-done.refs_0_.refs_1_, ...), custom_call_target="tpu_custom_call", output_to_operand_aliasing={{0}: (10, {}), {2}: (11, {})} | custom-call | tf_op jit(solution)/shard_map/pallas_call | solution.py:30
  11.6 0.6 %collective-permute-start.1 = (f32[7,2,8,256]{3,2,1,0:T(8,128)S(1)}, f32[7,2,8,256]{3,2,1,0:T(8,128)S(1)}, u32[]{:S(2)}, u32[]{:S(2)}) collective-permute-start(f32[7,2,8,256]{3,2,1,0:T(8,128)S(1)} %get-tuple-element.48), channel_id=1, source_target_pairs={{0,2},{2,0},{4,6},{6,4},{8,10},{10,8},{12,14},{14,12},{16,18},{18,... | collective-permute-start | bytes 344072 | tf_op jit(solution)/shard_map/ppermute | solution.py:544
  12.1 1.0 %collective-permute-done.1.facing_ref.refs_5_ = f32[7,2,8,256]{3,2,1,0:T(8,128)S(1)} collective-permute-done((f32[7,2,8,256]{3,2,1,0:T(8,128)S(1)}, f32[7,2,8,256]{3,2,1,0:T(8,128)S(1)}, u32[]{:S(2)}, u32[]{:S(2)}) %collective-permute-start.1) | collective-permute-done | bytes 114720 | tf_op jit(solution)/shard_map/ppermute | solution.py:544
  13.3 1.8 %collective-permute-start.3 = (f32[8,2,8,256]{3,2,1,0:T(8,128)S(1)}, f32[8,2,8,256]{3,2,1,0:T(8,128)S(1)}, u32[]{:S(2)}, u32[]{:S(2)}) collective-permute-start(f32[8,2,8,256]{3,2,1,0:T(8,128)S(1)} %get-tuple-element.51), channel_id=1, source_target_pairs={{0,4},{2,6},{4,0},{6,2},{8,12},{10,14},{12,8},{14,10},{16,20},{18,... | collective-permute-start | bytes 393224 | tf_op jit(solution)/shard_map/ppermute | solution.py:551
  15.1 1.6 %collective-permute-start.4 = (f32[8,2,8,256]{3,2,1,0:T(8,128)S(1)}, f32[8,2,8,256]{3,2,1,0:T(8,128)S(1)}, u32[]{:S(2)}, u32[]{:S(2)}) collective-permute-start(f32[8,2,8,256]{3,2,1,0:T(8,128)S(1)} %get-tuple-element.52), channel_id=1, source_target_pairs={{0,8},{2,10},{4,12},{6,14},{8,0},{10,2},{12,4},{14,6},{16,24},{18,... | collective-permute-start | bytes 393224 | tf_op jit(solution)/shard_map/ppermute | solution.py:551
  16.9 1.5 %collective-permute-start.11 = (f32[3,4,32,256]{3,2,1,0:T(8,128)S(1)}, f32[3,4,32,256]{3,2,1,0:T(8,128)S(1)}, u32[]{:S(2)}, u32[]{:S(2)}) collective-permute-start(f32[3,4,32,256]{3,2,1,0:T(8,128)S(1)} %get-tuple-element.64), channel_id=1, source_target_pairs={{0,2},{2,4},{4,6},{6,8},{8,10},{10,12},{12,14},{14,16},{16,18},{18... | collective-permute-start | bytes 1179656 | tf_op jit(solution)/shard_map/ppermute | solution.py:621
  18.4 0.7 %collective-permute-done.3.refs_1_ = f32[8,2,8,256]{3,2,1,0:T(8,128)S(1)} collective-permute-done((f32[8,2,8,256]{3,2,1,0:T(8,128)S(1)}, f32[8,2,8,256]{3,2,1,0:T(8,128)S(1)}, u32[]{:S(2)}, u32[]{:S(2)}) %collective-permute-start.3) | collective-permute-done | bytes 131104 | tf_op jit(solution)/shard_map/ppermute | solution.py:551
  19.1 2.3 %collective-permute-done.4.refs_2_ = f32[8,2,8,256]{3,2,1,0:T(8,128)S(1)} collective-permute-done((f32[8,2,8,256]{3,2,1,0:T(8,128)S(1)}, f32[8,2,8,256]{3,2,1,0:T(8,128)S(1)}, u32[]{:S(2)}, u32[]{:S(2)}) %collective-permute-start.4) | collective-permute-done | bytes 131104 | tf_op jit(solution)/shard_map/ppermute | solution.py:551
  21.4 1.7 %collective-permute-done.5.refs_3_ = f32[8,2,8,256]{3,2,1,0:T(8,128)S(1)} collective-permute-done((f32[8,2,8,256]{3,2,1,0:T(8,128)S(1)}, f32[8,2,8,256]{3,2,1,0:T(8,128)S(1)}, u32[]{:S(2)}, u32[]{:S(2)}) %collective-permute-start.5) | collective-permute-done | bytes 131104 | tf_op jit(solution)/shard_map/ppermute | solution.py:551
  23.4 3.3 %collective-permute-start.6 = (f32[6,2,8,256]{3,2,1,0:T(8,128)S(1)}, f32[6,2,8,256]{3,2,1,0:T(8,128)S(1)}, u32[]{:S(2)}, u32[]{:S(2)}) collective-permute-start(f32[6,2,8,256]{3,2,1,0:T(8,128)S(1)} %shard_map.125), channel_id=1, source_target_pairs={{0,16},{2,18},{4,20},{6,22},{8,24},{10,26},{12,28},{14,30},{16,0},... | collective-permute-start | bytes 294920 | tf_op jit(solution)/shard_map/ppermute | solution.py:631
  26.7 4.1 %collective-permute-done.6.refs_6_ = f32[6,2,8,256]{3,2,1,0:T(8,128)S(1)} collective-permute-done((f32[6,2,8,256]{3,2,1,0:T(8,128)S(1)}, f32[6,2,8,256]{3,2,1,0:T(8,128)S(1)}, u32[]{:S(2)}, u32[]{:S(2)}) %collective-permute-start.6) | collective-permute-done | bytes 98336 | tf_op jit(solution)/shard_map/ppermute | solution.py:631
  30.8 0.2 shard_map.126
  31.0 1.3 %collective-permute-start.7 = (f32[6,2,8,256]{3,2,1,0:T(8,128)S(1)}, f32[6,2,8,256]{3,2,1,0:T(8,128)S(1)}, u32[]{:S(2)}, u32[]{:S(2)}) collective-permute-start(f32[6,2,8,256]{3,2,1,0:T(8,128)S(1)} %get-tuple-element.55), channel_id=1, source_target_pairs={{0,4},{2,6},{4,0},{6,2},{8,12},{10,14},{12,8},{14,10},{16,20},{18,... | collective-permute-start | bytes 294920 | tf_op jit(solution)/shard_map/ppermute | solution.py:551
  32.4 0.9 %collective-permute-start.8 = (f32[6,2,8,256]{3,2,1,0:T(8,128)S(1)}, f32[6,2,8,256]{3,2,1,0:T(8,128)S(1)}, u32[]{:S(2)}, u32[]{:S(2)}) collective-permute-start(f32[6,2,8,256]{3,2,1,0:T(8,128)S(1)} %get-tuple-element.56), channel_id=1, source_target_pairs={{0,8},{2,10},{4,12},{6,14},{8,0},{10,2},{12,4},{14,6},{16,24},{18,... | collective-permute-start | bytes 294920 | tf_op jit(solution)/shard_map/ppermute | solution.py:551
  33.2 1.3 %collective-permute-start.9 = (f32[6,2,8,256]{3,2,1,0:T(8,128)S(1)}, f32[6,2,8,256]{3,2,1,0:T(8,128)S(1)}, u32[]{:S(2)}, u32[]{:S(2)}) collective-permute-start(f32[6,2,8,256]{3,2,1,0:T(8,128)S(1)} %get-tuple-element.57), channel_id=1, source_target_pairs={{0,12},{2,14},{4,8},{6,10},{8,4},{10,6},{12,0},{14,2},{16,28},{18,... | collective-permute-start | bytes 294920 | tf_op jit(solution)/shard_map/ppermute | solution.py:551
  34.6 2.1 %collective-permute-done.7.refs_1_ = f32[6,2,8,256]{3,2,1,0:T(8,128)S(1)} collective-permute-done((f32[6,2,8,256]{3,2,1,0:T(8,128)S(1)}, f32[6,2,8,256]{3,2,1,0:T(8,128)S(1)}, u32[]{:S(2)}, u32[]{:S(2)}) %collective-permute-start.7) | collective-permute-done | bytes 98336 | tf_op jit(solution)/shard_map/ppermute | solution.py:551
  36.6 0.3 collective-permute-done.8.refs_2_
  37.0 1.8 %collective-permute-done.9.refs_3_ = f32[6,2,8,256]{3,2,1,0:T(8,128)S(1)} collective-permute-done((f32[6,2,8,256]{3,2,1,0:T(8,128)S(1)}, f32[6,2,8,256]{3,2,1,0:T(8,128)S(1)}, u32[]{:S(2)}, u32[]{:S(2)}) %collective-permute-start.9) | collective-permute-done | bytes 98336 | tf_op jit(solution)/shard_map/ppermute | solution.py:551
  39.1 0.8 %fusion = f32[1,3,4,32,256]{4,3,2,1,0:T(8,128)} fusion(f32[3,4,32,256]{3,2,1,0:T(8,128)S(1)} %collective-permute-done.11, f32[3,3,4,32,256]{4,3,2,1,0:T(8,128)S(1)} %copy-done, pred[]{:T(512)S(6)} %eq.3), kind=kLoop, calls=%fused_computation.1 | loop fusion | flops 98304 | bytes 1179649 | tf_op jit(solution)/shard_map/broadcast_in_dim | solution.py:650
  39.9 0.8 %shard_map.128 = (f32[1,3,4,32,256]{4,3,2,1,0:T(8,128)}, f32[1,3,4,32,256]{4,3,2,1,0:T(8,128)}) custom-call(f32[6,8,8,256]{3,2,1,0:T(8,128)S(1)} %get-tuple-element.59.refs_0_), custom_call_target="tpu_custom_call" | custom-call | tf_op jit(solution)/shard_map/pallas_call | solution.py:30
  40.8 0.8 %shard_map.129 = (f32[1,3,4,32,256]{4,3,2,1,0:T(8,128)}, f32[1,3,4,32,256]{4,3,2,1,0:T(8,128)}) custom-call(f32[6,8,8,256]{3,2,1,0:T(8,128)S(1)} %collective-permute-done.10.refs_0_, f32[1,3,4,32,256]{4,3,2,1,0:T(8,128)} %get-tuple-element.60.refs_1_, f32[1,3,4,32,256]{4,3,2,1,0:T(8,128)} %get-tuple-element.61.refs_2_), custom_call_target="tpu_custom_call", output_to_operand_aliasing={{0}: (1, {}), {1}: (2, {})} | custom-call | tf_op jit(solution)/shard_map/pallas_call | solution.py:30
  (12 shorter events, 1.1 us)
Async XLA Ops:
  1.8 8.5 %collective-permute-start = (f32[27,8,256]{2,1,0:T(8,128)S(1)}, f32[27,8,256]{2,1,0:T(8,128)S(1)}, u32[]{:S(2)}, u32[]{:S(2)}) collective-permute-start(f32[27,8,256]{2,1,0:T(8,128)S(1)} %shard_map.121), channel_id=1, source_target_pairs={{0,1},{1,0},{2,3},{3,2},{4,5},{5,4},{6,7},{7,6},{8,9},{9,8},{10,11... | collective-permute-start | bytes 663560 | tf_op jit(solution)/shard_map/ppermute | solution.py:586
  10.2 2.9 %collective-permute-start.2 = (f32[7,6,8,256]{3,2,1,0:T(8,128)S(1)}, f32[7,6,8,256]{3,2,1,0:T(8,128)S(1)}, u32[]{:S(2)}, u32[]{:S(2)}) collective-permute-start(f32[7,6,8,256]{3,2,1,0:T(8,128)S(1)} %get-tuple-element.49), channel_id=1, source_target_pairs={{0,2},{2,0},{4,6},{6,4},{8,10},{10,8},{12,14},{14,12},{16,18},{18,... | collective-permute-start | bytes 1032200 | tf_op jit(solution)/shard_map/ppermute | solution.py:544
  11.6 11.6 %copy-start = (f32[3,3,4,32,256]{4,3,2,1,0:T(8,128)S(1)}, f32[3,3,4,32,256]{4,3,2,1,0:T(8,128)}, u32[]{:S(2)}) copy-start(f32[3,3,4,32,256]{4,3,2,1,0:T(8,128)} %refs_5_.7) | copy-start | bytes 3538948
  11.6 1.5 %collective-permute-start.1 = (f32[7,2,8,256]{3,2,1,0:T(8,128)S(1)}, f32[7,2,8,256]{3,2,1,0:T(8,128)S(1)}, u32[]{:S(2)}, u32[]{:S(2)}) collective-permute-start(f32[7,2,8,256]{3,2,1,0:T(8,128)S(1)} %get-tuple-element.48), channel_id=1, source_target_pairs={{0,2},{2,0},{4,6},{6,4},{8,10},{10,8},{12,14},{14,12},{16,18},{18,... | collective-permute-start | bytes 344072 | tf_op jit(solution)/shard_map/ppermute | solution.py:544
  13.3 5.8 %collective-permute-start.3 = (f32[8,2,8,256]{3,2,1,0:T(8,128)S(1)}, f32[8,2,8,256]{3,2,1,0:T(8,128)S(1)}, u32[]{:S(2)}, u32[]{:S(2)}) collective-permute-start(f32[8,2,8,256]{3,2,1,0:T(8,128)S(1)} %get-tuple-element.51), channel_id=1, source_target_pairs={{0,4},{2,6},{4,0},{6,2},{8,12},{10,14},{12,8},{14,10},{16,20},{18,... | collective-permute-start | bytes 393224 | tf_op jit(solution)/shard_map/ppermute | solution.py:551
  15.1 6.4 %collective-permute-start.4 = (f32[8,2,8,256]{3,2,1,0:T(8,128)S(1)}, f32[8,2,8,256]{3,2,1,0:T(8,128)S(1)}, u32[]{:S(2)}, u32[]{:S(2)}) collective-permute-start(f32[8,2,8,256]{3,2,1,0:T(8,128)S(1)} %get-tuple-element.52), channel_id=1, source_target_pairs={{0,8},{2,10},{4,12},{6,14},{8,0},{10,2},{12,4},{14,6},{16,24},{18,... | collective-permute-start | bytes 393224 | tf_op jit(solution)/shard_map/ppermute | solution.py:551
  16.7 6.5 %collective-permute-start.5 = (f32[8,2,8,256]{3,2,1,0:T(8,128)S(1)}, f32[8,2,8,256]{3,2,1,0:T(8,128)S(1)}, u32[]{:S(2)}, u32[]{:S(2)}) collective-permute-start(f32[8,2,8,256]{3,2,1,0:T(8,128)S(1)} %get-tuple-element.53), channel_id=1, source_target_pairs={{0,12},{2,14},{4,8},{6,10},{8,4},{10,6},{12,0},{14,2},{16,28},{18,... | collective-permute-start | bytes 393224 | tf_op jit(solution)/shard_map/ppermute | solution.py:551
  16.9 22.2 %collective-permute-start.11 = (f32[3,4,32,256]{3,2,1,0:T(8,128)S(1)}, f32[3,4,32,256]{3,2,1,0:T(8,128)S(1)}, u32[]{:S(2)}, u32[]{:S(2)}) collective-permute-start(f32[3,4,32,256]{3,2,1,0:T(8,128)S(1)} %get-tuple-element.64), channel_id=1, source_target_pairs={{0,2},{2,4},{4,6},{6,8},{8,10},{10,12},{12,14},{14,16},{16,18},{18... | collective-permute-start | bytes 1179656 | tf_op jit(solution)/shard_map/ppermute | solution.py:621
  23.4 7.4 %collective-permute-start.6 = (f32[6,2,8,256]{3,2,1,0:T(8,128)S(1)}, f32[6,2,8,256]{3,2,1,0:T(8,128)S(1)}, u32[]{:S(2)}, u32[]{:S(2)}) collective-permute-start(f32[6,2,8,256]{3,2,1,0:T(8,128)S(1)} %shard_map.125), channel_id=1, source_target_pairs={{0,16},{2,18},{4,20},{6,22},{8,24},{10,26},{12,28},{14,30},{16,0},... | collective-permute-start | bytes 294920 | tf_op jit(solution)/shard_map/ppermute | solution.py:631
  31.0 5.6 %collective-permute-start.7 = (f32[6,2,8,256]{3,2,1,0:T(8,128)S(1)}, f32[6,2,8,256]{3,2,1,0:T(8,128)S(1)}, u32[]{:S(2)}, u32[]{:S(2)}) collective-permute-start(f32[6,2,8,256]{3,2,1,0:T(8,128)S(1)} %get-tuple-element.55), channel_id=1, source_target_pairs={{0,4},{2,6},{4,0},{6,2},{8,12},{10,14},{12,8},{14,10},{16,20},{18,... | collective-permute-start | bytes 294920 | tf_op jit(solution)/shard_map/ppermute | solution.py:551
  32.4 4.6 %collective-permute-start.8 = (f32[6,2,8,256]{3,2,1,0:T(8,128)S(1)}, f32[6,2,8,256]{3,2,1,0:T(8,128)S(1)}, u32[]{:S(2)}, u32[]{:S(2)}) collective-permute-start(f32[6,2,8,256]{3,2,1,0:T(8,128)S(1)} %get-tuple-element.56), channel_id=1, source_target_pairs={{0,8},{2,10},{4,12},{6,14},{8,0},{10,2},{12,4},{14,6},{16,24},{18,... | collective-permute-start | bytes 294920 | tf_op jit(solution)/shard_map/ppermute | solution.py:551
  33.2 5.5 %collective-permute-start.9 = (f32[6,2,8,256]{3,2,1,0:T(8,128)S(1)}, f32[6,2,8,256]{3,2,1,0:T(8,128)S(1)}, u32[]{:S(2)}, u32[]{:S(2)}) collective-permute-start(f32[6,2,8,256]{3,2,1,0:T(8,128)S(1)} %get-tuple-element.57), channel_id=1, source_target_pairs={{0,12},{2,14},{4,8},{6,10},{8,4},{10,6},{12,0},{14,2},{16,28},{18,... | collective-permute-start | bytes 294920 | tf_op jit(solution)/shard_map/ppermute | solution.py:551
  39.0 1.8 %collective-permute-start.10 = (f32[6,8,8,256]{3,2,1,0:T(8,128)S(1)}, f32[6,8,8,256]{3,2,1,0:T(8,128)S(1)}, u32[]{:S(2)}, u32[]{:S(2)}) collective-permute-start(f32[6,8,8,256]{3,2,1,0:T(8,128)S(1)} %get-tuple-element.58), channel_id=1, source_target_pairs={{0,2},{2,0},{4,6},{6,4},{8,10},{10,8},{12,14},{14,12},{16,18},{18,... | collective-permute-start | bytes 1179656 | tf_op jit(solution)/shard_map/ppermute | solution.py:544

commit v5 on v4

--- a/solution.py
+++ b/solution.py
@@ -431,23 +431,36 @@
                 outs[m][5 + comp, i] = (g[2] * a + g[3] * b) + late[4 + comp]
 
 
-def chain(cut, parts, maps, static_ref, start, visit):
+def order_kernel(cut, *refs):
+    parts = refs[: cut.group]
+    static_ref, out_ref = refs[cut.group :]
     place = cut.place()
     _, layer, tile = cut.of(place)
     for m in range(cut.group):
-        maps[jnp.bitwise_xor(place, m)] = parts[m][...]
+        to = jnp.bitwise_xor(place, m)
+        for i in range(cut.size):
+            for j in range(2):
+                g = part_coarse(static_ref, layer, tile + i, parts[m][j, i])
+                for k in range(4):
+                    out_ref[to, 4 * j + k, i] = g[k]
+            for k in range(6):
+                out_ref[to, 8 + k, i] = parts[m][2 + k, i]
+
+
+def chain(cut, maps, start, visit):
+    _, layer, tile = cut.of(cut.place())
     for i in range(cut.size):
         state = [start(k, layer, tile + i, i) for k in range(6)]
         for s in range(cut.group):
             visit(s, i, state)
-            first = part_coarse(static_ref, layer, tile + i, maps[s, 0, i])
-            second = part_coarse(static_ref, layer, tile + i, maps[s, 1, i])
+            first = [maps[s, k, i] for k in range(4)]
+            second = [maps[s, 4 + k, i] for k in range(4)]
             new = [None] * 6
             for comp in range(3):
                 a, b = state[comp], state[3 + comp]
                 a, b = first[0] * a + first[1] * b, first[2] * a + first[3] * b
-                new[comp] = (second[0] * a + second[1] * b) + maps[s, 2 + comp, i]
-                new[3 + comp] = (second[2] * a + second[3] * b) + maps[s, 5 + comp, i]
+                new[comp] = (second[0] * a + second[1] * b) + maps[s, 8 + comp, i]
+                new[3 + comp] = (second[2] * a + second[3] * b) + maps[s, 11 + comp, i]
             state = new
         visit(cut.group, i, state)
 
@@ -463,22 +476,20 @@
 
 
 def lower_kernel(cut, *refs):
-    parts = refs[: cut.group]
-    static_ref, init_ref, out_ref, maps = refs[cut.group :]
+    parts, (static_ref, init_ref, out_ref, maps) = refs[: cut.group], refs[cut.group :]
+    order_kernel(cut, *parts, static_ref, maps)
 
     def visit(s, i, state):
         if s == cut.group:
             for k in range(6):
                 out_ref[k, i] = state[k]
 
-    chain(cut, parts, maps, static_ref, first_state(cut, init_ref), visit)
+    chain(cut, maps, first_state(cut, init_ref), visit)
 
 
 def upper_kernel(cut, *refs):
-    parts = refs[: cut.group]
-    static_ref, init_ref, hop_ref = refs[cut.group : cut.group + 3]
-    outs = refs[cut.group + 3 : 2 * cut.group + 3]
-    maps, found = refs[2 * cut.group + 3 :]
+    maps, init_ref, hop_ref = refs[:3]
+    outs, found = refs[3 : cut.group + 3], refs[cut.group + 3]
     lower = lax.axis_index("tm") < CORES * cut.group
     first = first_state(cut, init_ref)
 
@@ -490,7 +501,7 @@
             for k in range(6):
                 found[s, k, i] = state[k]
 
-    chain(cut, parts, maps, static_ref, start, visit)
+    chain(cut, maps, start, visit)
     for m in range(cut.group):
         outs[m][...] = found[jnp.bitwise_xor(cut.place(), m)]
 
@@ -624,16 +635,17 @@
         functools.partial(compose_kernel, cut), [shape(8, cut.size, 8, cols)] * group, (keep, *got, static)
     )
     parts = transpose_parts(parts)
-    maps = pltpu.VMEM((group, 8, cut.size, 8, cols), F32)
-    edge = call(
-        functools.partial(lower_kernel, cut), shape(6, cut.size, 8, cols), (*parts, static, init_state), [maps]
+    edge, maps = call(
+        functools.partial(lower_kernel, cut),
+        [shape(6, cut.size, 8, cols), shape(group, 14, cut.size, 8, cols)],
+        (*parts, static, init_state),
     )
     hop = lax.ppermute(edge, "tm", [(i, i ^ (slabs // 2)) for i in range(slabs)])
     states = call(
         functools.partial(upper_kernel, cut),
         [shape(6, cut.size, 8, cols)] * group,
-        (*parts, static, init_state, hop),
-        [maps, pltpu.VMEM((group, 6, cut.size, 8, cols), F32)],
+        (maps, init_state, hop),
+        [pltpu.VMEM((group, 6, cut.size, 8, cols), F32)],
     )
     states = transpose_parts(states)
     mine, other = call(

time: 41.8 us -> 41.7 us (level)
  no operation moved by 1% of the time
where the time goes in v5:
time: 41.7 us; the launch traced here: 41.5 us
  starting transfers between devices  15.6 us (37%)
  waiting for transfers between devices  14.3 us (34%)
  Pallas kernels  10 us (24%)
  other arithmetic  0.8 us (2%)
  between operations  0.73 us (2%)
    pallas_call x9, Pallas kernels, call(): pl.pallas_call(kernel, out_shape=out_shape, in_specs=specs, out_specs=jax...  10 us
    ppermute x6, waiting for transfers between devices, transpose_parts(): lax.ppermute(parts[m], 'tm', [(i, i ^ CORES * m) for i in range(count)])  9 us
    ppermute x6, starting transfers between devices, transpose_parts(): lax.ppermute(parts[m], 'tm', [(i, i ^ CORES * m) for i in range(count)])  7.12 us
    ppermute x1, waiting for transfers between devices, shards(): hop = lax.ppermute(edge, 'tm', [(i, i ^ slabs // 2) for i in range(slabs)])  4.08 us
    ppermute x1, starting transfers between devices, shards(): hop = lax.ppermute(edge, 'tm', [(i, i ^ slabs // 2) for i in range(slabs)])  3.3 us
    ppermute x1, starting transfers between devices, shards(): after = before = lax.ppermute(packs[0], 'space', [(0, 1), (1, 0)])  3.03 us
    ppermute x1, starting transfers between devices, shards(): visc = lax.ppermute(end_visc, 'tm', [(i, i + 1) for i in range(slabs - 1)])  1.5 us
    ppermute x3, waiting for transfers between devices, swap_cores(): return lax.ppermute(value, 'tm', [(i, i ^ 1) for i in range(count)])  1.05 us
  transfers between devices with their start and end apart: 12, of which 10 were waited for; matrix products, arithmetic and copies ran while one was open for 2% of the time, Pallas kernels for 19%

profile of v5, /device:TPU:0, one launch (start us, length us, event | category | flops | bytes accessed | tf_op | source)
XLA Modules:
  0.0 41.5 jit_solution(6669838832277089797)
XLA Ops:
  0.6 1.1 %shard_map.121 = f32[27,8,256]{2,1,0:T(8,128)S(1)} custom-call(f32[1,3,4,32,256]{4,3,2,1,0:T(8,128)} %refs_0_.3, f32[1,3,4,32,256]{4,3,2,1,0:T(8,128)} %refs_1_.4, f32[1,3,4,32,256]{4,3,2,1,0:T(8,128)} %refs_2_.3, f32[4,32,256]{2,1,0:T(8,128)} %refs_3_.3, f32[4,32,256]{2,1,0:T(8,128)} %refs_4_.3, f32[4,32,256]{2,1,0:T(8,128)} %refs_5_.4, ...), custom_call_target="tpu_custom_call" | custom-call | tf_op jit(solution)/shard_map/pallas_call | solution.py:30
  1.8 3.0 %collective-permute-start = (f32[27,8,256]{2,1,0:T(8,128)S(1)}, f32[27,8,256]{2,1,0:T(8,128)S(1)}, u32[]{:S(2)}, u32[]{:S(2)}) collective-permute-start(f32[27,8,256]{2,1,0:T(8,128)S(1)} %shard_map.121), channel_id=1, source_target_pairs={{0,1},{1,0},{2,3},{3,2},{4,5},{5,4},{6,7},{7,6},{8,9},{9,8},{10,11... | collective-permute-start | bytes 663560 | tf_op jit(solution)/shard_map/ppermute | solution.py:597
  4.8 5.2 %shard_map.122 = (f32[7,8,8,256]{3,2,1,0:T(8,128)S(1)}, f32[7,6,8,256]{3,2,1,0:T(8,128)S(1)}, f32[3,4,32,256]{3,2,1,0:T(8,128)S(1)}, f32[5,3,4,4,8,256]{5,4,3,2,...) custom-call(f32[1,3,4,32,256]{4,3,2,1,0:T(8,128)} %refs_0_.3, ...), custom_call_target="tpu_custom_call" | custom-call | tf_op jit(solution)/shard_map/pallas_call | solution.py:30
  10.2 1.3 %shard_map.123 = (f32[7,8,8,256]{3,2,1,0:T(8,128)S(1)}, f32[7,2,8,256]{3,2,1,0:T(8,128)S(1)}, f32[3,4,32,256]{3,2,1,0:T(8,128)S(1)}) custom-call(f32[27,8,256]{2,1,0:T(8,128)S(1)} %collective-permute-done.refs_0_.refs_1_, f32[27,8,256]{2,1,0:T(8,128)S(1)} %collective-permute-done.refs_0_.refs_1_, ...), custom_call_target="tpu_custom_call", output_to_operand_aliasing={{0}: (10, {}), {2}: (11, {})} | custom-call | tf_op jit(solution)/shard_map/pallas_call | solution.py:30
  11.6 0.6 %collective-permute-start.1 = (f32[7,2,8,256]{3,2,1,0:T(8,128)S(1)}, f32[7,2,8,256]{3,2,1,0:T(8,128)S(1)}, u32[]{:S(2)}, u32[]{:S(2)}) collective-permute-start(f32[7,2,8,256]{3,2,1,0:T(8,128)S(1)} %get-tuple-element.50), channel_id=1, source_target_pairs={{0,2},{2,0},{4,6},{6,4},{8,10},{10,8},{12,14},{14,12},{16,18},{18,... | collective-permute-start | bytes 344072 | tf_op jit(solution)/shard_map/ppermute | solution.py:555
  12.1 1.0 %collective-permute-done.1.facing_ref.refs_5_ = f32[7,2,8,256]{3,2,1,0:T(8,128)S(1)} collective-permute-done((f32[7,2,8,256]{3,2,1,0:T(8,128)S(1)}, f32[7,2,8,256]{3,2,1,0:T(8,128)S(1)}, u32[]{:S(2)}, u32[]{:S(2)}) %collective-permute-start.1) | collective-permute-done | bytes 114720 | tf_op jit(solution)/shard_map/ppermute | solution.py:555
  13.3 1.8 %collective-permute-start.3 = (f32[8,2,8,256]{3,2,1,0:T(8,128)S(1)}, f32[8,2,8,256]{3,2,1,0:T(8,128)S(1)}, u32[]{:S(2)}, u32[]{:S(2)}) collective-permute-start(f32[8,2,8,256]{3,2,1,0:T(8,128)S(1)} %get-tuple-element.53), channel_id=1, source_target_pairs={{0,4},{2,6},{4,0},{6,2},{8,12},{10,14},{12,8},{14,10},{16,20},{18,... | collective-permute-start | bytes 393224 | tf_op jit(solution)/shard_map/ppermute | solution.py:562
  15.1 1.6 %collective-permute-start.4 = (f32[8,2,8,256]{3,2,1,0:T(8,128)S(1)}, f32[8,2,8,256]{3,2,1,0:T(8,128)S(1)}, u32[]{:S(2)}, u32[]{:S(2)}) collective-permute-start(f32[8,2,8,256]{3,2,1,0:T(8,128)S(1)} %get-tuple-element.54), channel_id=1, source_target_pairs={{0,8},{2,10},{4,12},{6,14},{8,0},{10,2},{12,4},{14,6},{16,24},{18,... | collective-permute-start | bytes 393224 | tf_op jit(solution)/shard_map/ppermute | solution.py:562
  16.9 1.5 %collective-permute-start.11 = (f32[3,4,32,256]{3,2,1,0:T(8,128)S(1)}, f32[3,4,32,256]{3,2,1,0:T(8,128)S(1)}, u32[]{:S(2)}, u32[]{:S(2)}) collective-permute-start(f32[3,4,32,256]{3,2,1,0:T(8,128)S(1)} %get-tuple-element.68), channel_id=1, source_target_pairs={{0,2},{2,4},{4,6},{6,8},{8,10},{10,12},{12,14},{14,16},{16,18},{18... | collective-permute-start | bytes 1179656 | tf_op jit(solution)/shard_map/ppermute | solution.py:632
  18.4 0.7 %collective-permute-done.3.refs_1_ = f32[8,2,8,256]{3,2,1,0:T(8,128)S(1)} collective-permute-done((f32[8,2,8,256]{3,2,1,0:T(8,128)S(1)}, f32[8,2,8,256]{3,2,1,0:T(8,128)S(1)}, u32[]{:S(2)}, u32[]{:S(2)}) %collective-permute-start.3) | collective-permute-done | bytes 131104 | tf_op jit(solution)/shard_map/ppermute | solution.py:562
  19.1 2.3 %collective-permute-done.4.refs_2_ = f32[8,2,8,256]{3,2,1,0:T(8,128)S(1)} collective-permute-done((f32[8,2,8,256]{3,2,1,0:T(8,128)S(1)}, f32[8,2,8,256]{3,2,1,0:T(8,128)S(1)}, u32[]{:S(2)}, u32[]{:S(2)}) %collective-permute-start.4) | collective-permute-done | bytes 131104 | tf_op jit(solution)/shard_map/ppermute | solution.py:562
  21.4 1.7 %collective-permute-done.5.refs_3_ = f32[8,2,8,256]{3,2,1,0:T(8,128)S(1)} collective-permute-done((f32[8,2,8,256]{3,2,1,0:T(8,128)S(1)}, f32[8,2,8,256]{3,2,1,0:T(8,128)S(1)}, u32[]{:S(2)}, u32[]{:S(2)}) %collective-permute-start.5) | collective-permute-done | bytes 131104 | tf_op jit(solution)/shard_map/ppermute | solution.py:562
  23.4 3.3 %collective-permute-start.6 = (f32[6,2,8,256]{3,2,1,0:T(8,128)S(1)}, f32[6,2,8,256]{3,2,1,0:T(8,128)S(1)}, u32[]{:S(2)}, u32[]{:S(2)}) collective-permute-start(f32[6,2,8,256]{3,2,1,0:T(8,128)S(1)} %get-tuple-element.57), channel_id=1, source_target_pairs={{0,16},{2,18},{4,20},{6,22},{8,24},{10,26},{12,28},{14,30},{16,0},... | collective-permute-start | bytes 294920 | tf_op jit(solution)/shard_map/ppermute | solution.py:643
  26.7 4.1 %collective-permute-done.6.refs_2_ = f32[6,2,8,256]{3,2,1,0:T(8,128)S(1)} collective-permute-done((f32[6,2,8,256]{3,2,1,0:T(8,128)S(1)}, f32[6,2,8,256]{3,2,1,0:T(8,128)S(1)}, u32[]{:S(2)}, u32[]{:S(2)}) %collective-permute-start.6) | collective-permute-done | bytes 98336 | tf_op jit(solution)/shard_map/ppermute | solution.py:643
  30.9 1.3 %collective-permute-start.7 = (f32[6,2,8,256]{3,2,1,0:T(8,128)S(1)}, f32[6,2,8,256]{3,2,1,0:T(8,128)S(1)}, u32[]{:S(2)}, u32[]{:S(2)}) collective-permute-start(f32[6,2,8,256]{3,2,1,0:T(8,128)S(1)} %get-tuple-element.59), channel_id=1, source_target_pairs={{0,4},{2,6},{4,0},{6,2},{8,12},{10,14},{12,8},{14,10},{16,20},{18,... | collective-permute-start | bytes 294920 | tf_op jit(solution)/shard_map/ppermute | solution.py:562
  32.2 0.9 %collective-permute-start.8 = (f32[6,2,8,256]{3,2,1,0:T(8,128)S(1)}, f32[6,2,8,256]{3,2,1,0:T(8,128)S(1)}, u32[]{:S(2)}, u32[]{:S(2)}) collective-permute-start(f32[6,2,8,256]{3,2,1,0:T(8,128)S(1)} %get-tuple-element.60), channel_id=1, source_target_pairs={{0,8},{2,10},{4,12},{6,14},{8,0},{10,2},{12,4},{14,6},{16,24},{18,... | collective-permute-start | bytes 294920 | tf_op jit(solution)/shard_map/ppermute | solution.py:562
  33.1 1.3 %collective-permute-start.9 = (f32[6,2,8,256]{3,2,1,0:T(8,128)S(1)}, f32[6,2,8,256]{3,2,1,0:T(8,128)S(1)}, u32[]{:S(2)}, u32[]{:S(2)}) collective-permute-start(f32[6,2,8,256]{3,2,1,0:T(8,128)S(1)} %get-tuple-element.61), channel_id=1, source_target_pairs={{0,12},{2,14},{4,8},{6,10},{8,4},{10,6},{12,0},{14,2},{16,28},{18,... | collective-permute-start | bytes 294920 | tf_op jit(solution)/shard_map/ppermute | solution.py:562
  34.4 2.0 %collective-permute-done.7.refs_1_ = f32[6,2,8,256]{3,2,1,0:T(8,128)S(1)} collective-permute-done((f32[6,2,8,256]{3,2,1,0:T(8,128)S(1)}, f32[6,2,8,256]{3,2,1,0:T(8,128)S(1)}, u32[]{:S(2)}, u32[]{:S(2)}) %collective-permute-start.7) | collective-permute-done | bytes 98336 | tf_op jit(solution)/shard_map/ppermute | solution.py:562
  36.4 0.4 %collective-permute-done.8.refs_2_ = f32[6,2,8,256]{3,2,1,0:T(8,128)S(1)} collective-permute-done((f32[6,2,8,256]{3,2,1,0:T(8,128)S(1)}, f32[6,2,8,256]{3,2,1,0:T(8,128)S(1)}, u32[]{:S(2)}, u32[]{:S(2)}) %collective-permute-start.8) | collective-permute-done | bytes 98336 | tf_op jit(solution)/shard_map/ppermute | solution.py:562
  36.8 1.8 %collective-permute-done.9.refs_3_ = f32[6,2,8,256]{3,2,1,0:T(8,128)S(1)} collective-permute-done((f32[6,2,8,256]{3,2,1,0:T(8,128)S(1)}, f32[6,2,8,256]{3,2,1,0:T(8,128)S(1)}, u32[]{:S(2)}, u32[]{:S(2)}) %collective-permute-start.9) | collective-permute-done | bytes 98336 | tf_op jit(solution)/shard_map/ppermute | solution.py:562
  38.6 0.2 shard_map.127
  39.0 0.8 %fusion = f32[1,3,4,32,256]{4,3,2,1,0:T(8,128)} fusion(f32[3,4,32,256]{3,2,1,0:T(8,128)S(1)} %collective-permute-done.11, f32[3,3,4,32,256]{4,3,2,1,0:T(8,128)S(1)} %copy-done, pred[]{:T(512)S(6)} %eq.3), kind=kLoop, calls=%fused_computation.1 | loop fusion | flops 98304 | bytes 1179649 | tf_op jit(solution)/shard_map/broadcast_in_dim | solution.py:662
  39.8 0.8 %shard_map.128 = (f32[1,3,4,32,256]{4,3,2,1,0:T(8,128)}, f32[1,3,4,32,256]{4,3,2,1,0:T(8,128)}) custom-call(f32[6,8,8,256]{3,2,1,0:T(8,128)S(1)} %get-tuple-element.63.refs_0_), custom_call_target="tpu_custom_call" | custom-call | tf_op jit(solution)/shard_map/pallas_call | solution.py:30
  40.7 0.8 %shard_map.129 = (f32[1,3,4,32,256]{4,3,2,1,0:T(8,128)}, f32[1,3,4,32,256]{4,3,2,1,0:T(8,128)}) custom-call(f32[6,8,8,256]{3,2,1,0:T(8,128)S(1)} %collective-permute-done.10.refs_0_, f32[1,3,4,32,256]{4,3,2,1,0:T(8,128)} %get-tuple-element.64.refs_1_, f32[1,3,4,32,256]{4,3,2,1,0:T(8,128)} %get-tuple-element.65.refs_2_), custom_call_target="tpu_custom_call", output_to_operand_aliasing={{0}: (1, {}), {1}: (2, {})} | custom-call | tf_op jit(solution)/shard_map/pallas_call | solution.py:30
  (12 shorter events, 1.0 us)
Async XLA Ops:
  1.8 8.5 %collective-permute-start = (f32[27,8,256]{2,1,0:T(8,128)S(1)}, f32[27,8,256]{2,1,0:T(8,128)S(1)}, u32[]{:S(2)}, u32[]{:S(2)}) collective-permute-start(f32[27,8,256]{2,1,0:T(8,128)S(1)} %shard_map.121), channel_id=1, source_target_pairs={{0,1},{1,0},{2,3},{3,2},{4,5},{5,4},{6,7},{7,6},{8,9},{9,8},{10,11... | collective-permute-start | bytes 663560 | tf_op jit(solution)/shard_map/ppermute | solution.py:597
  10.2 2.9 %collective-permute-start.2 = (f32[7,6,8,256]{3,2,1,0:T(8,128)S(1)}, f32[7,6,8,256]{3,2,1,0:T(8,128)S(1)}, u32[]{:S(2)}, u32[]{:S(2)}) collective-permute-start(f32[7,6,8,256]{3,2,1,0:T(8,128)S(1)} %get-tuple-element.51), channel_id=1, source_target_pairs={{0,2},{2,0},{4,6},{6,4},{8,10},{10,8},{12,14},{14,12},{16,18},{18,... | collective-permute-start | bytes 1032200 | tf_op jit(solution)/shard_map/ppermute | solution.py:555
  11.6 11.6 %copy-start = (f32[3,3,4,32,256]{4,3,2,1,0:T(8,128)S(1)}, f32[3,3,4,32,256]{4,3,2,1,0:T(8,128)}, u32[]{:S(2)}) copy-start(f32[3,3,4,32,256]{4,3,2,1,0:T(8,128)} %refs_1_.5) | copy-start | bytes 3538948
  11.6 1.5 %collective-permute-start.1 = (f32[7,2,8,256]{3,2,1,0:T(8,128)S(1)}, f32[7,2,8,256]{3,2,1,0:T(8,128)S(1)}, u32[]{:S(2)}, u32[]{:S(2)}) collective-permute-start(f32[7,2,8,256]{3,2,1,0:T(8,128)S(1)} %get-tuple-element.50), channel_id=1, source_target_pairs={{0,2},{2,0},{4,6},{6,4},{8,10},{10,8},{12,14},{14,12},{16,18},{18,... | collective-permute-start | bytes 344072 | tf_op jit(solution)/shard_map/ppermute | solution.py:555
  13.3 5.8 %collective-permute-start.3 = (f32[8,2,8,256]{3,2,1,0:T(8,128)S(1)}, f32[8,2,8,256]{3,2,1,0:T(8,128)S(1)}, u32[]{:S(2)}, u32[]{:S(2)}) collective-permute-start(f32[8,2,8,256]{3,2,1,0:T(8,128)S(1)} %get-tuple-element.53), channel_id=1, source_target_pairs={{0,4},{2,6},{4,0},{6,2},{8,12},{10,14},{12,8},{14,10},{16,20},{18,... | collective-permute-start | bytes 393224 | tf_op jit(solution)/shard_map/ppermute | solution.py:562
  15.1 6.4 %collective-permute-start.4 = (f32[8,2,8,256]{3,2,1,0:T(8,128)S(1)}, f32[8,2,8,256]{3,2,1,0:T(8,128)S(1)}, u32[]{:S(2)}, u32[]{:S(2)}) collective-permute-start(f32[8,2,8,256]{3,2,1,0:T(8,128)S(1)} %get-tuple-element.54), channel_id=1, source_target_pairs={{0,8},{2,10},{4,12},{6,14},{8,0},{10,2},{12,4},{14,6},{16,24},{18,... | collective-permute-start | bytes 393224 | tf_op jit(solution)/shard_map/ppermute | solution.py:562
  16.7 6.5 %collective-permute-start.5 = (f32[8,2,8,256]{3,2,1,0:T(8,128)S(1)}, f32[8,2,8,256]{3,2,1,0:T(8,128)S(1)}, u32[]{:S(2)}, u32[]{:S(2)}) collective-permute-start(f32[8,2,8,256]{3,2,1,0:T(8,128)S(1)} %get-tuple-element.55), channel_id=1, source_target_pairs={{0,12},{2,14},{4,8},{6,10},{8,4},{10,6},{12,0},{14,2},{16,28},{18,... | collective-permute-start | bytes 393224 | tf_op jit(solution)/shard_map/ppermute | solution.py:562
  16.9 22.1 %collective-permute-start.11 = (f32[3,4,32,256]{3,2,1,0:T(8,128)S(1)}, f32[3,4,32,256]{3,2,1,0:T(8,128)S(1)}, u32[]{:S(2)}, u32[]{:S(2)}) collective-permute-start(f32[3,4,32,256]{3,2,1,0:T(8,128)S(1)} %get-tuple-element.68), channel_id=1, source_target_pairs={{0,2},{2,4},{4,6},{6,8},{8,10},{10,12},{12,14},{14,16},{16,18},{18... | collective-permute-start | bytes 1179656 | tf_op jit(solution)/shard_map/ppermute | solution.py:632
  23.4 7.4 %collective-permute-start.6 = (f32[6,2,8,256]{3,2,1,0:T(8,128)S(1)}, f32[6,2,8,256]{3,2,1,0:T(8,128)S(1)}, u32[]{:S(2)}, u32[]{:S(2)}) collective-permute-start(f32[6,2,8,256]{3,2,1,0:T(8,128)S(1)} %get-tuple-element.57), channel_id=1, source_target_pairs={{0,16},{2,18},{4,20},{6,22},{8,24},{10,26},{12,28},{14,30},{16,0},... | collective-permute-start | bytes 294920 | tf_op jit(solution)/shard_map/ppermute | solution.py:643
  30.9 5.5 %collective-permute-start.7 = (f32[6,2,8,256]{3,2,1,0:T(8,128)S(1)}, f32[6,2,8,256]{3,2,1,0:T(8,128)S(1)}, u32[]{:S(2)}, u32[]{:S(2)}) collective-permute-start(f32[6,2,8,256]{3,2,1,0:T(8,128)S(1)} %get-tuple-element.59), channel_id=1, source_target_pairs={{0,4},{2,6},{4,0},{6,2},{8,12},{10,14},{12,8},{14,10},{16,20},{18,... | collective-permute-start | bytes 294920 | tf_op jit(solution)/shard_map/ppermute | solution.py:562
  32.2 4.6 %collective-permute-start.8 = (f32[6,2,8,256]{3,2,1,0:T(8,128)S(1)}, f32[6,2,8,256]{3,2,1,0:T(8,128)S(1)}, u32[]{:S(2)}, u32[]{:S(2)}) collective-permute-start(f32[6,2,8,256]{3,2,1,0:T(8,128)S(1)} %get-tuple-element.60), channel_id=1, source_target_pairs={{0,8},{2,10},{4,12},{6,14},{8,0},{10,2},{12,4},{14,6},{16,24},{18,... | collective-permute-start | bytes 294920 | tf_op jit(solution)/shard_map/ppermute | solution.py:562
  33.1 5.5 %collective-permute-start.9 = (f32[6,2,8,256]{3,2,1,0:T(8,128)S(1)}, f32[6,2,8,256]{3,2,1,0:T(8,128)S(1)}, u32[]{:S(2)}, u32[]{:S(2)}) collective-permute-start(f32[6,2,8,256]{3,2,1,0:T(8,128)S(1)} %get-tuple-element.61), channel_id=1, source_target_pairs={{0,12},{2,14},{4,8},{6,10},{8,4},{10,6},{12,0},{14,2},{16,28},{18,... | collective-permute-start | bytes 294920 | tf_op jit(solution)/shard_map/ppermute | solution.py:562
  38.9 1.8 %collective-permute-start.10 = (f32[6,8,8,256]{3,2,1,0:T(8,128)S(1)}, f32[6,8,8,256]{3,2,1,0:T(8,128)S(1)}, u32[]{:S(2)}, u32[]{:S(2)}) collective-permute-start(f32[6,8,8,256]{3,2,1,0:T(8,128)S(1)} %get-tuple-element.62), channel_id=1, source_target_pairs={{0,2},{2,0},{4,6},{6,4},{8,10},{10,8},{12,14},{14,12},{16,18},{18,... | collective-permute-start | bytes 1179656 | tf_op jit(solution)/shard_map/ppermute | solution.py:555
